TPU v7x, 256 devices: a whole 4x4x8 slice. The times are simulated.
256 devices in a mesh: context: 32 (over z_lo, x, core), tensor: 8 (over y, z_hi).
Axes of the slice: x: 4, y: 4, z: 8 (z_hi: 2, z_lo: 4; z = z_hi * 4 + z_lo), core: 2. Of those that a mesh axis runs over, the one named last changes fastest.
Arguments:
- q_gate: bfloat16 [8192, 4096], P('context', 'tensor'), may hold values from -6 to 6
- k_gate: bfloat16 [8192, 4096], P('context', 'tensor'), may hold values from -6 to 6
- v_input: bfloat16 [8192, 4096], P('context', 'tensor'), may hold values from -6 to 6
- filter_taps: bfloat16 [8192, 4096], P('context', 'tensor'), may hold values from -6 to 6
- skip_bias: float32 [4096], P('tensor'), may hold values from -4 to 4
- out_grad: bfloat16 [8192, 4096], P('context', 'tensor'), may hold values from -6 to 6
Outputs:
- mixed: bfloat16 [8192, 4096], P('context', 'tensor')
- q_grad: bfloat16 [8192, 4096], P('context', 'tensor')
- k_grad: bfloat16 [8192, 4096], P('context', 'tensor')
- v_grad: bfloat16 [8192, 4096], P('context', 'tensor')
- filter_grad: bfloat16 [8192, 4096], P('context', 'tensor')
All inputs are finite; a program needn't handle non-finite values.
Results may differ from a plain program's by a relative error of at most 0.013.
Values may be sent and summed in bfloat16 or wider, within the bound.
No kernel may reach another device: no remote copies, remote signals or barrier semaphores. Data moves between devices by JAX's collectives and lax.ppermute only.
A program may use at most 64 MiB of HBM per device.

v0:
```python
import functools
import math

import jax
import jax.numpy as jnp
import ml_dtypes
import numpy as np
from jax import lax
from jax.experimental import pallas as pl
from jax.experimental.pallas import tpu as pltpu
from jax.sharding import PartitionSpec as P

BF16 = jnp.bfloat16
F32 = jnp.float32


def make_tables(groups, rows, chans):
    length = 2 * groups * rows
    a = np.arange(groups)[None, :]
    b = np.arange(rows)[None, :]
    half = np.arange(groups)[:, None] + 0.5
    theta = 2.0 * math.pi * a * half / (2 * groups)
    eye = np.eye(chans)
    first = np.concatenate([np.kron(np.cos(theta), eye), np.kron(-np.sin(theta), eye)], axis=0)
    k2 = np.arange(rows)[:, None]
    phi = 2.0 * math.pi * ((k2 * b) % rows) / rows
    second = np.block([[np.cos(phi), -np.sin(phi)], [np.sin(phi), np.cos(phi)]])
    psi = 2.0 * math.pi * b * half / length
    low = ml_dtypes.bfloat16
    return (
        first.astype(low),
        np.ascontiguousarray(first.T).astype(low),
        second.astype(low),
        np.ascontiguousarray(second.T).astype(low),
        np.cos(psi).astype(np.float32)[:, None, :],
        (-np.sin(psi)).astype(np.float32)[:, None, :],
    )


def prep_kernel(q_ref, k_ref, v_ref, f_ref, og_ref, out_ref):
    owners, three, rows = out_ref.shape
    chans = three // 3

    def put(slot, block):
        out_ref[:, slot * chans : (slot + 1) * chans, :] = block.T.reshape(owners, chans, rows)

    put(0, k_ref[...] * v_ref[...])
    put(1, f_ref[...])
    put(2, og_ref[...] * q_ref[...])


def dot(a, b):
    return jnp.dot(a, b, preferred_element_type=F32)


def core_kernel(scale, x_ref, first_ref, first_t_ref, second_ref, second_t_ref, twr_ref, twi_ref, y_ref):
    groups, three, rows = x_ref.shape
    chans = three // 3
    lines = groups * chans
    twr, twi = twr_ref[...], twi_ref[...]

    def split3(block):
        return block.reshape(groups, chans, rows)

    def spectrum(slot):
        block = x_ref[:, slot * chans : (slot + 1) * chans, :].reshape(lines, rows)
        part = dot(first_ref[...], block)
        real, imag = split3(part[:lines]), split3(part[lines:])
        turned_real = (real * twr - imag * twi).astype(BF16).reshape(lines, rows)
        turned_imag = (real * twi + imag * twr).astype(BF16).reshape(lines, rows)
        out = dot(jnp.concatenate([turned_real, turned_imag], axis=1), second_ref[...])
        return out[:, :rows], out[:, rows:]

    def signal(real, imag, slot):
        joined = jnp.concatenate([real.astype(BF16), imag.astype(BF16)], axis=1)
        back = dot(joined, second_t_ref[...])
        real, imag = split3(back[:, :rows]), split3(back[:, rows:])
        turned_real = (real * twr + imag * twi).astype(BF16).reshape(lines, rows)
        turned_imag = (imag * twr - real * twi).astype(BF16).reshape(lines, rows)
        out = dot(first_t_ref[...], jnp.concatenate([turned_real, turned_imag], axis=0))
        y_ref[:, slot * chans : (slot + 1) * chans, :] = split3((out * scale).astype(BF16))

    gr, gi = spectrum(0)
    fr, fi = spectrum(1)
    signal(gr * fr - gi * fi, gr * fi + gi * fr, 0)
    dr, di = spectrum(2)
    signal(fr * dr + fi * di, fr * di - fi * dr, 1)
    signal(gr * dr + gi * di, gr * di - gi * dr, 2)


def post_kernel(y_ref, q_ref, k_ref, v_ref, og_ref, bias_ref, mixed_ref, qg_ref, kg_ref, vg_ref, fg_ref):
    owners, three, rows = y_ref.shape
    chans = three // 3

    def take(slot):
        return y_ref[:, slot * chans : (slot + 1) * chans, :].reshape(owners * chans, rows).T

    q, k, v, og = q_ref[...], k_ref[...], v_ref[...], og_ref[...]
    bias = bias_ref[...]
    q32, og32 = q.astype(F32), og.astype(F32)
    pre_gate = take(0).astype(F32) + bias * (k * v).astype(F32)
    mixed_ref[...] = (q32 * pre_gate).astype(BF16)
    qg_ref[...] = (og32 * pre_gate).astype(BF16)
    gated_grad = take(1).astype(F32) + bias * (og * q).astype(F32)
    kg_ref[...] = (gated_grad * v.astype(F32)).astype(BF16)
    vg_ref[...] = (gated_grad * k.astype(F32)).astype(BF16)
    fg_ref[...] = take(2)


def local(q_gate, k_gate, v_input, filter_taps, skip_bias, out_grad):
    groups = lax.axis_size("context")
    rows, width = q_gate.shape
    chans = width // groups
    tables = make_tables(groups, rows, chans)
    seq = groups * rows
    scale = 2.0 / (2 * seq) / math.sqrt(seq)
    steps = 4
    cols = width // steps
    owners = groups // steps
    tile = pl.BlockSpec((rows, cols), lambda i: (0, i))
    message = pl.BlockSpec((owners, 3 * chans, rows), lambda i: (i, 0, 0))
    messages = jax.ShapeDtypeStruct((groups, 3 * chans, rows), BF16)
    whole = jax.ShapeDtypeStruct((rows, width), BF16)
    limit = pltpu.CompilerParams(vmem_limit_bytes=48 * 1024 * 1024)

    sent = pl.pallas_call(
        prep_kernel, grid=(steps,), in_specs=[tile] * 5, out_specs=message, out_shape=messages, compiler_params=limit
    )(q_gate, k_gate, v_input, filter_taps, out_grad)
    items = lax.all_to_all(sent, "context", split_axis=0, concat_axis=0, tiled=True)
    terms = pl.pallas_call(
        functools.partial(core_kernel, scale), out_shape=messages, compiler_params=limit
    )(items, *tables)
    back = lax.all_to_all(terms, "context", split_axis=0, concat_axis=0, tiled=True)
    return pl.pallas_call(
        post_kernel,
        grid=(steps,),
        in_specs=[message] + [tile] * 4 + [pl.BlockSpec((1, cols), lambda i: (0, i))],
        out_specs=[tile] * 5,
        out_shape=[whole] * 5,
        compiler_params=limit,
    )(back, q_gate, k_gate, v_input, out_grad, skip_bias[None, :])


def solution(mesh):
    spec = P("context", "tensor")
    return jax.shard_map(
        local,
        mesh=mesh,
        in_specs=(spec, spec, spec, spec, P("tensor"), spec),
        out_specs=(spec,) * 5,
        check_vma=False,
    )
```

profile of v0, /device:TPU:1, one launch (start us, length us, event | category | flops | bytes accessed | tf_op | source)
XLA Modules:
  0.0 70.2 jit_solution(5167218064176869044)
XLA Ops:
  0.6 0.0 copy-start.2
  0.6 0.9 %copy-done.2 = bf16[256,512]{1,0:T(8,128)(2,1)S(1)} copy-done((bf16[256,512]{1,0:T(8,128)(2,1)S(1)}, bf16[256,512]{1,0:T(8,128)(2,1)}, u32[]{:S(2)}) %copy-start.2) | copy-done | bytes 262168
  1.6 0.9 %copy-done.4 = bf16[256,512]{1,0:T(8,128)(2,1)S(1)} copy-done((bf16[256,512]{1,0:T(8,128)(2,1)S(1)}, bf16[256,512]{1,0:T(8,128)(2,1)}, u32[]{:S(2)}) %copy-start.4) | copy-done | bytes 262168
  2.5 0.9 %copy-done.6 = bf16[256,512]{1,0:T(8,128)(2,1)S(1)} copy-done((bf16[256,512]{1,0:T(8,128)(2,1)S(1)}, bf16[256,512]{1,0:T(8,128)(2,1)}, u32[]{:S(2)}) %copy-start.6) | copy-done | bytes 262168
  3.5 0.9 %copy-done.8 = bf16[256,512]{1,0:T(8,128)(2,1)S(1)} copy-done((bf16[256,512]{1,0:T(8,128)(2,1)S(1)}, bf16[256,512]{1,0:T(8,128)(2,1)}, u32[]{:S(2)}) %copy-start.8) | copy-done | bytes 262168
  4.4 0.9 %copy-done.12 = bf16[256,512]{1,0:T(8,128)(2,1)S(1)} copy-done((bf16[256,512]{1,0:T(8,128)(2,1)S(1)}, bf16[256,512]{1,0:T(8,128)(2,1)}, u32[]{:S(2)}) %copy-start.12) | copy-done | bytes 262168
  5.4 0.8 %shard_map.155 = bf16[32,48,256]{2,1,0:T(8,128)(2,1)S(1)} custom-call(bf16[256,512]{1,0:T(8,128)(2,1)S(1)} %copy-done.2, bf16[256,512]{1,0:T(8,128)(2,1)S(1)} %copy-done.4, bf16[256,512]{1,0:T(8,128)(2,1)S(1)} %copy-done.6, bf16[256,512]{1,0:T(8,128)(2,1)S(1)} %copy-done.12, bf16[256,512]{1,0:T(8,128)(2,1)S(1)} %copy-done.8), custom_call_target="tpu_custom_call" | custom-call | tf_op jit(solution)/shard_map/pallas_call | solution.py:126
  6.2 0.0 copy-start
  6.2 0.0 copy-start.10
  6.2 31.5 %all_to_all.10.x_ref = bf16[32,48,256]{2,1,0:T(8,128)(2,1)S(1)} all-to-all(bf16[32,48,256]{2,1,0:T(8,128)(2,1)S(1)} %shard_map.155), channel_id=1, replica_groups=mesh['context'=32,'tensor'=8] {'context'}, dimensions={0} | all-to-all | bytes 1572864 | tf_op jit(solution)/shard_map/all_to_all | solution.py:129
  37.7 0.0 copy-done.1
  37.7 0.0 copy-done.11
  37.7 0.0 copy-done.13
  37.7 0.0 copy-done.14
  37.7 0.0 copy-done
  37.7 0.0 copy-done.10
  37.7 4.2 %shard_map.156 = bf16[32,48,256]{2,1,0:T(8,128)(2,1)S(1)} custom-call(bf16[32,48,256]{2,1,0:T(8,128)(2,1)S(1)} %all_to_all.10.x_ref, bf16[1024,512]{1,0:T(8,128)(2,1)S(1)} %copy-done.1, bf16[512,1024]{1,0:T(8,128)(2,1)S(1)} %copy-done, bf16[512,512]{1,0:T(8,128)(2,1)S(1)} %copy-done.11, bf16[512,512]{1,0:T(8,128)(2,1)S(1)} %copy-done.10, ...), custom_call_target="tpu_custom_call" | custom-call | tf_op jit(solution)/shard_map/pallas_call | solution.py:130
  42.0 0.0 copy-start.3
  42.0 0.0 copy-start.5
  42.0 0.0 copy-start.7
  42.0 0.0 copy-start.9
  42.0 0.0 copy-start.15
  42.0 26.1 %all_to_all.11.y_ref = bf16[32,48,256]{2,1,0:T(8,128)(2,1)S(1)} all-to-all(bf16[32,48,256]{2,1,0:T(8,128)(2,1)S(1)} %shard_map.156), channel_id=1, replica_groups=mesh['context'=32,'tensor'=8] {'context'}, dimensions={0} | all-to-all | bytes 1572864 | tf_op jit(solution)/shard_map/all_to_all | solution.py:133
  68.2 2.0 %shard_map.157 = (bf16[256,512]{1,0:T(8,128)(2,1)}, bf16[256,512]{1,0:T(8,128)(2,1)}, bf16[256,512]{1,0:T(8,128)(2,1)}, bf16[256,512]{1,0:T(8,128)(2,1)}, bf16[256,512]{1,0:T(8,128)(2,1)}) custom-call(bf16[32,48,256]{2,1,0:T(8,128)(2,1)S(1)} %all_to_all.11.y_ref, bf16[256,512]{1,0:T(8,128)(2,1)S(1)} %copy-done.3, bf16[256,512]{1,0:T(8,128)(2,1)S(1)} %copy-done.5, ...), custom_call_target="tpu_custom_call" | custom-call | tf_op jit(solution)/shard_map/pallas_call | solution.py:134
  (13 shorter events, 0.0 us)
Async XLA Ops:
  0.6 1.0 %copy-start.2 = (bf16[256,512]{1,0:T(8,128)(2,1)S(1)}, bf16[256,512]{1,0:T(8,128)(2,1)}, u32[]{:S(2)}) copy-start(bf16[256,512]{1,0:T(8,128)(2,1)} %q_ref.3) | copy-start | bytes 786436
  1.6 0.9 %copy-start.4 = (bf16[256,512]{1,0:T(8,128)(2,1)S(1)}, bf16[256,512]{1,0:T(8,128)(2,1)}, u32[]{:S(2)}) copy-start(bf16[256,512]{1,0:T(8,128)(2,1)} %k_ref.3) | copy-start | bytes 786436
  2.5 0.9 %copy-start.6 = (bf16[256,512]{1,0:T(8,128)(2,1)S(1)}, bf16[256,512]{1,0:T(8,128)(2,1)}, u32[]{:S(2)}) copy-start(bf16[256,512]{1,0:T(8,128)(2,1)} %v_ref.3) | copy-start | bytes 786436
  3.5 0.9 %copy-start.8 = (bf16[256,512]{1,0:T(8,128)(2,1)S(1)}, bf16[256,512]{1,0:T(8,128)(2,1)}, u32[]{:S(2)}) copy-start(bf16[256,512]{1,0:T(8,128)(2,1)} %og_ref.3) | copy-start | bytes 786436
  4.4 0.9 %copy-start.12 = (bf16[256,512]{1,0:T(8,128)(2,1)S(1)}, bf16[256,512]{1,0:T(8,128)(2,1)}, u32[]{:S(2)}) copy-start(bf16[256,512]{1,0:T(8,128)(2,1)} %f_ref.1) | copy-start | bytes 786436
  5.4 32.3 %copy-start.1 = (bf16[1024,512]{1,0:T(8,128)(2,1)S(1)}, bf16[1024,512]{1,0:T(8,128)(2,1)}, u32[]{:S(2)}) copy-start(bf16[1024,512]{1,0:T(8,128)(2,1)} %constant.12.clone.first_ref) | copy-start | bytes 3145732
  5.4 32.3 %copy-start.11 = (bf16[512,512]{1,0:T(8,128)(2,1)S(1)}, bf16[512,512]{1,0:T(8,128)(2,1)}, u32[]{:S(2)}) copy-start(bf16[512,512]{1,0:T(8,128)(2,1)} %constant.14.clone.second_ref) | copy-start | bytes 1572868
  5.4 32.3 %copy-start.13 = (f32[32,1,256]{2,1,0:T(1,128)S(1)}, f32[32,1,256]{2,1,0:T(1,128)}, u32[]{:S(2)}) copy-start(f32[32,1,256]{2,1,0:T(1,128)} %constant.17.clone.twi_ref) | copy-start | bytes 98308
  5.4 32.3 %copy-start.14 = (f32[32,1,256]{2,1,0:T(1,128)S(1)}, f32[32,1,256]{2,1,0:T(1,128)}, u32[]{:S(2)}) copy-start(f32[32,1,256]{2,1,0:T(1,128)} %constant.16.clone.twr_ref) | copy-start | bytes 98308
  6.2 31.5 %copy-start = (bf16[512,1024]{1,0:T(8,128)(2,1)S(1)}, bf16[512,1024]{1,0:T(8,128)(2,1)}, u32[]{:S(2)}) copy-start(bf16[512,1024]{1,0:T(8,128)(2,1)} %constant.13.clone.first_t_ref) | copy-start | bytes 3145732
  6.2 31.5 %copy-start.10 = (bf16[512,512]{1,0:T(8,128)(2,1)S(1)}, bf16[512,512]{1,0:T(8,128)(2,1)}, u32[]{:S(2)}) copy-start(bf16[512,512]{1,0:T(8,128)(2,1)} %constant.15.clone.second_t_ref) | copy-start | bytes 1572868
  42.0 26.2 %copy-start.3 = (bf16[256,512]{1,0:T(8,128)(2,1)S(1)}, bf16[256,512]{1,0:T(8,128)(2,1)}, u32[]{:S(2)}) copy-start(bf16[256,512]{1,0:T(8,128)(2,1)} %q_ref.3) | copy-start | bytes 786436
  42.0 26.1 %copy-start.5 = (bf16[256,512]{1,0:T(8,128)(2,1)S(1)}, bf16[256,512]{1,0:T(8,128)(2,1)}, u32[]{:S(2)}) copy-start(bf16[256,512]{1,0:T(8,128)(2,1)} %k_ref.3) | copy-start | bytes 786436
  42.0 26.1 %copy-start.7 = (bf16[256,512]{1,0:T(8,128)(2,1)S(1)}, bf16[256,512]{1,0:T(8,128)(2,1)}, u32[]{:S(2)}) copy-start(bf16[256,512]{1,0:T(8,128)(2,1)} %v_ref.3) | copy-start | bytes 786436
  42.0 26.1 %copy-start.9 = (bf16[256,512]{1,0:T(8,128)(2,1)S(1)}, bf16[256,512]{1,0:T(8,128)(2,1)}, u32[]{:S(2)}) copy-start(bf16[256,512]{1,0:T(8,128)(2,1)} %og_ref.3) | copy-start | bytes 786436
  42.0 26.1 %copy-start.15 = (f32[512]{0:T(512)S(1)}, f32[512]{0:T(512)}, u32[]{:S(2)}) copy-start(f32[512]{0:T(512)} %param.16) | copy-start | bytes 6148
where the time goes:
time: 70.5 us; the launch traced here: 70.2 us
  blocking collectives  57.6 us (82%)
  Pallas kernels  7.02 us (10%)
  local copies, waits for them, and re-layouts  4.8 us (7%)
  between operations  0.77 us (1%)
    all_to_all x1, blocking collectives, local(): lax.all_to_all(sent, 'context', split_axis=0, concat_axis=0, tiled=True)  31.5 us
    all_to_all x1, blocking collectives, local(): lax.all_to_all(terms, 'context', split_axis=0, concat_axis=0, tiled=True)  26.1 us
    unnamed x32, local copies, waits for them, and re-layouts  4.8 us
    pallas_call x1, Pallas kernels, local(): pl.pallas_call(functools.partial(core_kernel, scale), out_shape=messages,...  4.25 us
    pallas_call x1, Pallas kernels, local(): pl.pallas_call(post_kernel, grid=(steps,), in_specs=[message] + [tile] *...  2.01 us

commit v1 on v0

v1 whole, which is shorter than its diff:
```python
import functools
import math

import jax
import jax.numpy as jnp
import ml_dtypes
import numpy as np
from jax import lax
from jax.experimental import pallas as pl
from jax.experimental.pallas import tpu as pltpu
from jax.sharding import PartitionSpec as P

BF16 = jnp.bfloat16
F32 = jnp.float32


def device_order(groups):
    quarter = groups // 4
    ids = list(range(groups))
    return ids[quarter : 2 * quarter] + ids[:quarter] + ids[2 * quarter :]


def make_tables(order, rows):
    groups = len(order)
    length = 2 * groups * rows
    a = np.array(order)[None, :]
    b = np.arange(rows)[None, :]
    half = np.arange(groups)[:, None] + 0.5
    theta = 2.0 * math.pi * a * half / (2 * groups)
    first = np.concatenate([np.cos(theta), -np.sin(theta)], axis=0)
    psi = 2.0 * math.pi * b * half / length
    low = np.arange(rows // 2)[:, None]
    m = np.arange(rows // 2)[None, :]
    second = []
    for parity in (0, 1):
        phi = 2.0 * math.pi * ((low * (2 * m + parity)) % rows) / rows
        second.append(np.block([[np.cos(phi), -np.sin(phi)], [np.sin(phi), np.cos(phi)]]))
    second = np.stack(second)
    narrow = ml_dtypes.bfloat16
    return (
        first.astype(narrow),
        np.ascontiguousarray(first.T).astype(narrow),
        second.astype(narrow),
        np.ascontiguousarray(second.transpose(0, 2, 1)).astype(narrow),
        np.cos(psi).astype(np.float32),
        (-np.sin(psi)).astype(np.float32),
    )


def prep_kernel(f_hbm, k_hbm, v_hbm, q_hbm, og_hbm, out_ref, held, sems):
    owners, three, rows = out_ref.shape
    chans = three // 3
    copies = [
        pltpu.make_async_copy(src, held.at[i], sems.at[i]) for i, src in enumerate((f_hbm, k_hbm, v_hbm, q_hbm, og_hbm))
    ]
    for copy in copies:
        copy.start()

    def put(slot, block):
        out_ref[:, slot * chans : (slot + 1) * chans, :] = block.T.reshape(owners, chans, rows)

    copies[0].wait()
    put(1, held[0])
    copies[1].wait()
    copies[2].wait()
    put(0, held[1] * held[2])
    copies[3].wait()
    copies[4].wait()
    put(2, held[3] * held[4])


def dot(a, b):
    return jnp.dot(a, b, preferred_element_type=F32)


def core_kernel(scale, x_ref, first_ref, first_t_ref, second_ref, second_t_ref, twr_ref, twi_ref, y_ref, t_ref, v_ref):
    groups, three, rows = x_ref.shape
    chans = three // 3
    h = rows // 2
    twr, twi = twr_ref[...], twi_ref[...]
    for s in range(3):
        items = jnp.swapaxes(x_ref[:, s * chans : (s + 1) * chans, :], 0, 1)
        for c in range(chans):
            part = dot(first_ref[...], items[c])
            real, imag = part[:groups], part[groups:]
            tr, ti = real * twr - imag * twi, real * twi + imag * twr
            lines = slice(c * groups, (c + 1) * groups)
            t_ref[s, 0, lines, :h] = (tr[:, :h] + tr[:, h:]).astype(BF16)
            t_ref[s, 0, lines, h:] = (ti[:, :h] + ti[:, h:]).astype(BF16)
            t_ref[s, 1, lines, :h] = (tr[:, :h] - tr[:, h:]).astype(BF16)
            t_ref[s, 1, lines, h:] = (ti[:, :h] - ti[:, h:]).astype(BF16)
    halves = []
    for parity in (0, 1):
        g, f, d = (dot(t_ref[s, parity], second_ref[parity]) for s in range(3))
        gr, gi, fr, fi, dr, di = g[:, :h], g[:, h:], f[:, :h], f[:, h:], d[:, :h], d[:, h:]
        products = (
            (gr * fr - gi * fi, gr * fi + gi * fr),
            (fr * dr + fi * di, fr * di - fi * dr),
            (gr * dr + gi * di, gr * di - gi * dr),
        )
        halves.append(
            [
                dot(jnp.concatenate([real.astype(BF16), imag.astype(BF16)], axis=1), second_t_ref[parity])
                for real, imag in products
            ]
        )
    for s in range(3):
        even, odd = (half[s].reshape(chans, groups, rows) for half in halves)
        for part, lanes in ((even + odd, slice(0, h)), (even - odd, slice(h, rows))):
            real, imag = part[:, :, :h], part[:, :, h:]
            v_ref[s, :, :groups, lanes] = (real * twr[:, lanes] + imag * twi[:, lanes]).astype(BF16)
            v_ref[s, :, groups:, lanes] = (imag * twr[:, lanes] - real * twi[:, lanes]).astype(BF16)
    for s in range(3):
        out = jnp.stack([dot(first_t_ref[...], v_ref[s, c]) * scale for c in range(chans)], axis=0)
        y_ref[:, s * chans : (s + 1) * chans, :] = jnp.swapaxes(out.astype(BF16), 0, 1)


def post_kernel(y_ref, q_ref, k_ref, v_ref, og_ref, bias_ref, mixed_hbm, qg_hbm, kg_hbm, vg_hbm, fg_hbm, held, sems):
    owners, three, rows = y_ref.shape
    chans = three // 3
    parts = held.shape[1]
    step = rows // parts
    bias = bias_ref[...]
    outs = (fg_hbm, mixed_hbm, qg_hbm, kg_hbm, vg_hbm)
    copies = []

    def put(i, p, block):
        held[i, p] = block.astype(BF16)
        copy = pltpu.make_async_copy(held.at[i, p], outs[i].at[pl.ds(p * step, step)], sems.at[i, p])
        copy.start()
        copies.append(copy)

    for p in range(parts):
        span = slice(p * step, (p + 1) * step)

        def take(slot):
            return y_ref[:, slot * chans : (slot + 1) * chans, span].reshape(owners * chans, step).T

        put(0, p, take(2))
        q, k, v, og = q_ref[span], k_ref[span], v_ref[span], og_ref[span]
        pre_gate = take(0).astype(F32) + bias * (k * v).astype(F32)
        put(1, p, q.astype(F32) * pre_gate)
        put(2, p, og.astype(F32) * pre_gate)
        gated_grad = take(1).astype(F32) + bias * (og * q).astype(F32)
        put(3, p, gated_grad * v.astype(F32))
        put(4, p, gated_grad * k.astype(F32))
    for copy in copies:
        copy.wait()


def local(q_gate, k_gate, v_input, filter_taps, skip_bias, out_grad):
    groups = lax.axis_size("context")
    rows, width = q_gate.shape
    chans = width // groups
    order = device_order(groups)
    seq = groups * rows
    scale = 2.0 / (2 * seq) / math.sqrt(seq)
    messages = jax.ShapeDtypeStruct((groups, 3 * chans, rows), BF16)
    whole = jax.ShapeDtypeStruct((rows, width), BF16)
    limit = pltpu.CompilerParams(vmem_limit_bytes=48 * 1024 * 1024)
    far = pl.BlockSpec(memory_space=pltpu.HBM)
    near = pl.BlockSpec(memory_space=pltpu.VMEM)

    def swap(block):
        return lax.all_to_all(
            block, "context", split_axis=0, concat_axis=0, tiled=True, axis_index_groups=[order]
        )

    sent = pl.pallas_call(
        prep_kernel,
        in_specs=[far] * 5,
        out_specs=near,
        out_shape=messages,
        scratch_shapes=[pltpu.VMEM((5, rows, width), BF16), pltpu.SemaphoreType.DMA((5,))],
        name="gate_and_pack",
    )(filter_taps, k_gate, v_input, q_gate, out_grad)
    terms = pl.pallas_call(
        functools.partial(core_kernel, scale),
        out_shape=messages,
        scratch_shapes=[
            pltpu.VMEM((3, 2, chans * groups, rows), BF16),
            pltpu.VMEM((3, chans, 2 * groups, rows), BF16),
        ],
        compiler_params=limit,
        name="transforms",
    )(swap(sent), *make_tables(order, rows))
    parts = 2
    return pl.pallas_call(
        post_kernel,
        in_specs=[near] * 6,
        out_specs=[far] * 5,
        out_shape=[whole] * 5,
        scratch_shapes=[
            pltpu.VMEM((5, parts, rows // parts, width), BF16),
            pltpu.SemaphoreType.DMA((5, parts)),
        ],
        compiler_params=limit,
        name="unpack_and_gate",
    )(swap(terms), q_gate, k_gate, v_input, out_grad, skip_bias[None, :])


def solution(mesh):
    spec = P("context", "tensor")
    return jax.shard_map(
        local,
        mesh=mesh,
        in_specs=(spec, spec, spec, spec, P("tensor"), spec),
        out_specs=(spec,) * 5,
        check_vma=False,
    )
```

time: 70.5 us -> 63.7 us (0.904)
  local copies, waits for them, and re-layouts: 4.8 us -> 0.07 us
  blocking collectives: 57.6 us -> 56.5 us
  Pallas kernels: 7.02 us -> 6.13 us
    unnamed x32 -> x22, local copies, waits for them, and re-layouts: 4.8 us -> 0.07 us
    pallas_call x1, Pallas kernels: 4.25 us -> 2.58 us  [local(): pl.pallas_call(functools.partial(core_kernel, scale), out_shape=messages,...]
    all_to_all x2, blocking collectives: 57.6 us -> 56.5 us  [swap(): lax.all_to_all(block, 'context', split_axis=0, concat_axis=0, tiled=True,...]
    pallas_call x2, Pallas kernels: 2.77 us -> 3.55 us  [the longest x1 2.31 us: local(): pl.pallas_call(prep_kernel, in_specs=[far] * 5, out_specs=near, out_shape...]
where the time goes in v1:
time: 63.7 us; the launch traced here: 63.4 us
  blocking collectives  56.5 us (89%)
  Pallas kernels  6.13 us (10%)
  between operations  0.78 us (1%)
    all_to_all x2, blocking collectives, swap(): lax.all_to_all(block, 'context', split_axis=0, concat_axis=0, tiled=True,...  56.5 us
    pallas_call x1, Pallas kernels, local(): pl.pallas_call(functools.partial(core_kernel, scale), out_shape=messages,...  2.58 us
    pallas_call x1, Pallas kernels, local(): pl.pallas_call(prep_kernel, in_specs=[far] * 5, out_specs=near, out_shape...  2.31 us

profile of v1, /device:TPU:1, one launch (start us, length us, event | category | flops | bytes accessed | tf_op | source)
XLA Modules:
  0.0 63.4 jit_solution(10017663468763404054)
XLA Ops:
  0.6 2.3 %gate_and_pack.1 = bf16[32,48,256]{2,1,0:T(8,128)(2,1)} custom-call(bf16[256,512]{1,0:T(8,128)(2,1)} %f_hbm.1, bf16[256,512]{1,0:T(8,128)(2,1)} %k_ref.1, bf16[256,512]{1,0:T(8,128)(2,1)} %v_ref.1, bf16[256,512]{1,0:T(8,128)(2,1)} %q_ref.1, bf16[256,512]{1,0:T(8,128)(2,1)} %og_ref.1), custom_call_target="tpu_custom_call" | custom-call | tf_op jit(solution)/shard_map/gate_and_pack/pallas_call | solution.py:169
  2.9 0.0 copy-start.4
  3.0 0.0 copy-start.5
  3.0 0.0 copy-start.6
  3.0 0.0 copy-start.7
  3.0 0.0 copy-start.8
  3.0 0.0 copy-start.9
  3.0 31.6 %all_to_all.10.x_ref = bf16[32,48,256]{2,1,0:T(8,128)(2,1)S(1)} all-to-all(bf16[32,48,256]{2,1,0:T(8,128)(2,1)} %gate_and_pack.1), channel_id=1, replica_groups={{64,72,80,88,96,104,112,120,0,8,16,24,32,40,48,56,128,136,144,152,160,1..., dimensions={0} | all-to-all | bytes 1572864 | tf_op jit(solution)/shard_map/all_to_all | solution.py:165
  34.6 0.0 copy-done.4
  34.6 0.0 copy-done.5
  34.6 0.0 copy-done.6
  34.7 0.0 copy-done.7
  34.7 0.0 copy-done.8
  34.7 0.0 copy-done.9
  34.7 2.6 %transforms.1 = bf16[32,48,256]{2,1,0:T(8,128)(2,1)S(1)} custom-call(bf16[32,48,256]{2,1,0:T(8,128)(2,1)S(1)} %all_to_all.10.x_ref, bf16[64,32]{1,0:T(8,128)(2,1)S(1)} %copy-done.8, bf16[32,64]{1,0:T(8,128)(2,1)S(1)} %copy-done.9, bf16[2,256,256]{2,1,0:T(8,128)(2,1)S(1)} %copy-done.5, bf16[2,256,256]{2,1,0:T(8,128)(2,1)S(1)} %copy-done.4, ...), custom_call_target="tpu_custom_call" | custom-call | tf_op jit(solution)/shard_map/transforms/pallas_call | solution.py:177
  37.3 0.0 copy-start
  37.3 0.0 copy-start.1
  37.3 0.0 copy-start.2
  37.3 0.0 copy-start.3
  37.3 0.0 copy-start.10
  37.3 24.8 %all_to_all.11.y_ref = bf16[32,48,256]{2,1,0:T(8,128)(2,1)S(1)} all-to-all(bf16[32,48,256]{2,1,0:T(8,128)(2,1)S(1)} %transforms.1), channel_id=1, replica_groups={{64,72,80,88,96,104,112,120,0,8,16,24,32,40,48,56,128,136,144,152,160,1..., dimensions={0} | all-to-all | bytes 1572864 | tf_op jit(solution)/shard_map/all_to_all | solution.py:165
  62.2 0.0 copy-done
  62.2 0.0 copy-done.2
  62.2 1.2 %unpack_and_gate.1 = (bf16[256,512]{1,0:T(8,128)(2,1)}, bf16[256,512]{1,0:T(8,128)(2,1)}, bf16[256,512]{1,0:T(8,128)(2,1)}, bf16[256,512]{1,0:T(8,128)(2,1)}, bf16[256,512]{1,0:T(8,128)(2,1)}) custom-call(bf16[32,48,256]{2,1,0:T(8,128)(2,1)S(1)} %all_to_all.11.y_ref, bf16[256,512]{1,0:T(8,128)(2,1)S(1)} %copy-done.2, bf16[256,512]{1,0:T(8,128)(2,1)S(1)} %copy-done, ...), custom_call_target="tpu_custom_call" | custom-call | tf_op jit(solution)/shard_map/unpack_and_gate/pallas_call | solution.py:188
  (3 shorter events, 0.0 us)
Async XLA Ops:
  2.9 31.7 %copy-start.4 = (bf16[2,256,256]{2,1,0:T(8,128)(2,1)S(1)}, bf16[2,256,256]{2,1,0:T(8,128)(2,1)}, u32[]{:S(2)}) copy-start(bf16[2,256,256]{2,1,0:T(8,128)(2,1)} %constant.15.clone.second_t_ref) | copy-start | bytes 786436
  3.0 31.7 %copy-start.5 = (bf16[2,256,256]{2,1,0:T(8,128)(2,1)S(1)}, bf16[2,256,256]{2,1,0:T(8,128)(2,1)}, u32[]{:S(2)}) copy-start(bf16[2,256,256]{2,1,0:T(8,128)(2,1)} %constant.14.clone.second_ref) | copy-start | bytes 786436
  3.0 31.7 %copy-start.6 = (f32[32,256]{1,0:T(8,128)S(1)}, f32[32,256]{1,0:T(8,128)}, u32[]{:S(2)}) copy-start(f32[32,256]{1,0:T(8,128)} %constant.17.clone.twi_ref) | copy-start | bytes 98308
  3.0 31.7 %copy-start.7 = (f32[32,256]{1,0:T(8,128)S(1)}, f32[32,256]{1,0:T(8,128)}, u32[]{:S(2)}) copy-start(f32[32,256]{1,0:T(8,128)} %constant.16.clone.twr_ref) | copy-start | bytes 98308
  3.0 31.7 %copy-start.8 = (bf16[64,32]{1,0:T(8,128)(2,1)S(1)}, bf16[64,32]{1,0:T(8,128)(2,1)}, u32[]{:S(2)}) copy-start(bf16[64,32]{1,0:T(8,128)(2,1)} %constant.12.clone.first_ref) | copy-start | bytes 12292
  3.0 31.7 %copy-start.9 = (bf16[32,64]{1,0:T(8,128)(2,1)S(1)}, bf16[32,64]{1,0:T(8,128)(2,1)}, u32[]{:S(2)}) copy-start(bf16[32,64]{1,0:T(8,128)(2,1)} %constant.13.clone.first_t_ref) | copy-start | bytes 12292
  37.3 24.9 %copy-start = (bf16[256,512]{1,0:T(8,128)(2,1)S(1)}, bf16[256,512]{1,0:T(8,128)(2,1)}, u32[]{:S(2)}) copy-start(bf16[256,512]{1,0:T(8,128)(2,1)} %k_ref.1) | copy-start | bytes 786436
  37.3 24.9 %copy-start.1 = (bf16[256,512]{1,0:T(8,128)(2,1)S(1)}, bf16[256,512]{1,0:T(8,128)(2,1)}, u32[]{:S(2)}) copy-start(bf16[256,512]{1,0:T(8,128)(2,1)} %v_ref.1) | copy-start | bytes 786436
  37.3 24.9 %copy-start.2 = (bf16[256,512]{1,0:T(8,128)(2,1)S(1)}, bf16[256,512]{1,0:T(8,128)(2,1)}, u32[]{:S(2)}) copy-start(bf16[256,512]{1,0:T(8,128)(2,1)} %q_ref.1) | copy-start | bytes 786436
  37.3 24.9 %copy-start.3 = (bf16[256,512]{1,0:T(8,128)(2,1)S(1)}, bf16[256,512]{1,0:T(8,128)(2,1)}, u32[]{:S(2)}) copy-start(bf16[256,512]{1,0:T(8,128)(2,1)} %og_ref.1) | copy-start | bytes 786436
  37.3 24.9 %copy-start.10 = (f32[512]{0:T(512)S(1)}, f32[512]{0:T(512)}, u32[]{:S(2)}) copy-start(f32[512]{0:T(512)} %param.16) | copy-start | bytes 6148

commit v2 on v1

--- a/solution.py
+++ b/solution.py
@@ -170,10 +170,11 @@
         prep_kernel,
         in_specs=[far] * 5,
         out_specs=near,
-        out_shape=messages,
+        out_shape=pltpu.VMEM(messages.shape, BF16),
         scratch_shapes=[pltpu.VMEM((5, rows, width), BF16), pltpu.SemaphoreType.DMA((5,))],
+        compiler_params=limit,
         name="gate_and_pack",
-    )(filter_taps, k_gate, v_input, q_gate, out_grad)
+    )(*(pltpu.with_memory_space_constraint(x, pltpu.HBM) for x in (filter_taps, k_gate, v_input, q_gate, out_grad)))
     terms = pl.pallas_call(
         functools.partial(core_kernel, scale),
         out_shape=messages,

time: 63.7 us -> 62.7 us (0.984)
  Pallas kernels: 6.13 us -> 5.37 us
    pallas_call x1, Pallas kernels: 2.31 us -> 1.44 us  [local(): pl.pallas_call(prep_kernel, in_specs=[far] * 5, out_specs=near, out_shape...]
where the time goes in v2:
time: 62.7 us; the launch traced here: 62.5 us
  blocking collectives  56.2 us (90%)
  Pallas kernels  5.37 us (9%)
  between operations  0.78 us (1%)
    all_to_all x2, blocking collectives, swap(): lax.all_to_all(block, 'context', split_axis=0, concat_axis=0, tiled=True,...  56.2 us
    pallas_call x1, Pallas kernels, local(): pl.pallas_call(functools.partial(core_kernel, scale), out_shape=messages,...  2.66 us
    pallas_call x1, Pallas kernels, local(): pl.pallas_call(prep_kernel, in_specs=[far] * 5, out_specs=near, out_shape...  1.44 us
    pallas_call x1, Pallas kernels, local(): pl.pallas_call(post_kernel, in_specs=[near] * 6, out_specs=[far] * 5, out...  1.27 us

profile of v2, /device:TPU:1, one launch (start us, length us, event | category | flops | bytes accessed | tf_op | source)
XLA Modules:
  0.0 62.5 jit_solution(11229217446496608702)
XLA Ops:
  0.6 1.4 %gate_and_pack.1 = bf16[32,48,256]{2,1,0:T(8,128)(2,1)S(1)} custom-call(bf16[256,512]{1,0:T(8,128)(2,1)} %f_hbm.1, bf16[256,512]{1,0:T(8,128)(2,1)} %k_ref.1, bf16[256,512]{1,0:T(8,128)(2,1)} %v_ref.1, bf16[256,512]{1,0:T(8,128)(2,1)} %q_ref.1, bf16[256,512]{1,0:T(8,128)(2,1)} %og_ref.1), custom_call_target="tpu_custom_call" | custom-call | tf_op jit(solution)/shard_map/gate_and_pack/pallas_call | solution.py:169
  2.1 0.0 copy-start.4
  2.1 0.0 copy-start.5
  2.1 0.0 copy-start.6
  2.1 0.0 copy-start.7
  2.1 0.0 copy-start.8
  2.1 0.0 copy-start.9
  2.1 31.4 %all_to_all.10.x_ref = bf16[32,48,256]{2,1,0:T(8,128)(2,1)S(1)} all-to-all(bf16[32,48,256]{2,1,0:T(8,128)(2,1)S(1)} %gate_and_pack.1), channel_id=1, replica_groups={{64,72,80,88,96,104,112,120,0,8,16,24,32,40,48,56,128,136,144,152,160,1..., dimensions={0} | all-to-all | bytes 1572864 | tf_op jit(solution)/shard_map/all_to_all | solution.py:165
  33.6 0.0 copy-done.4
  33.6 0.0 copy-done.5
  33.6 0.0 copy-done.6
  33.6 0.0 copy-done.7
  33.6 0.0 copy-done.8
  33.6 0.0 copy-done.9
  33.6 2.7 %transforms.1 = bf16[32,48,256]{2,1,0:T(8,128)(2,1)S(1)} custom-call(bf16[32,48,256]{2,1,0:T(8,128)(2,1)S(1)} %all_to_all.10.x_ref, bf16[64,32]{1,0:T(8,128)(2,1)S(1)} %copy-done.8, bf16[32,64]{1,0:T(8,128)(2,1)S(1)} %copy-done.9, bf16[2,256,256]{2,1,0:T(8,128)(2,1)S(1)} %copy-done.5, bf16[2,256,256]{2,1,0:T(8,128)(2,1)S(1)} %copy-done.4, ...), custom_call_target="tpu_custom_call" | custom-call | tf_op jit(solution)/shard_map/transforms/pallas_call | solution.py:178
  36.3 0.0 copy-start
  36.3 0.0 copy-start.1
  36.3 0.0 copy-start.2
  36.3 0.0 copy-start.3
  36.3 0.0 copy-start.10
  36.3 24.8 %all_to_all.11.y_ref = bf16[32,48,256]{2,1,0:T(8,128)(2,1)S(1)} all-to-all(bf16[32,48,256]{2,1,0:T(8,128)(2,1)S(1)} %transforms.1), channel_id=1, replica_groups={{64,72,80,88,96,104,112,120,0,8,16,24,32,40,48,56,128,136,144,152,160,1..., dimensions={0} | all-to-all | bytes 1572864 | tf_op jit(solution)/shard_map/all_to_all | solution.py:165
  61.2 0.0 copy-done
  61.2 0.0 copy-done.1
  61.2 1.3 %unpack_and_gate.1 = (bf16[256,512]{1,0:T(8,128)(2,1)}, bf16[256,512]{1,0:T(8,128)(2,1)}, bf16[256,512]{1,0:T(8,128)(2,1)}, bf16[256,512]{1,0:T(8,128)(2,1)}, bf16[256,512]{1,0:T(8,128)(2,1)}) custom-call(bf16[32,48,256]{2,1,0:T(8,128)(2,1)S(1)} %all_to_all.11.y_ref, bf16[256,512]{1,0:T(8,128)(2,1)S(1)} %copy-done.2, bf16[256,512]{1,0:T(8,128)(2,1)S(1)} %copy-done, ...), custom_call_target="tpu_custom_call" | custom-call | tf_op jit(solution)/shard_map/unpack_and_gate/pallas_call | solution.py:189
  (3 shorter events, 0.0 us)
Async XLA Ops:
  2.1 31.5 %copy-start.4 = (bf16[2,256,256]{2,1,0:T(8,128)(2,1)S(1)}, bf16[2,256,256]{2,1,0:T(8,128)(2,1)}, u32[]{:S(2)}) copy-start(bf16[2,256,256]{2,1,0:T(8,128)(2,1)} %constant.15.clone.second_t_ref) | copy-start | bytes 786436
  2.1 31.5 %copy-start.5 = (bf16[2,256,256]{2,1,0:T(8,128)(2,1)S(1)}, bf16[2,256,256]{2,1,0:T(8,128)(2,1)}, u32[]{:S(2)}) copy-start(bf16[2,256,256]{2,1,0:T(8,128)(2,1)} %constant.14.clone.second_ref) | copy-start | bytes 786436
  2.1 31.5 %copy-start.6 = (f32[32,256]{1,0:T(8,128)S(1)}, f32[32,256]{1,0:T(8,128)}, u32[]{:S(2)}) copy-start(f32[32,256]{1,0:T(8,128)} %constant.17.clone.twi_ref) | copy-start | bytes 98308
  2.1 31.5 %copy-start.7 = (f32[32,256]{1,0:T(8,128)S(1)}, f32[32,256]{1,0:T(8,128)}, u32[]{:S(2)}) copy-start(f32[32,256]{1,0:T(8,128)} %constant.16.clone.twr_ref) | copy-start | bytes 98308
  2.1 31.5 %copy-start.8 = (bf16[64,32]{1,0:T(8,128)(2,1)S(1)}, bf16[64,32]{1,0:T(8,128)(2,1)}, u32[]{:S(2)}) copy-start(bf16[64,32]{1,0:T(8,128)(2,1)} %constant.12.clone.first_ref) | copy-start | bytes 12292
  2.1 31.5 %copy-start.9 = (bf16[32,64]{1,0:T(8,128)(2,1)S(1)}, bf16[32,64]{1,0:T(8,128)(2,1)}, u32[]{:S(2)}) copy-start(bf16[32,64]{1,0:T(8,128)(2,1)} %constant.13.clone.first_t_ref) | copy-start | bytes 12292
  36.3 24.9 %copy-start = (bf16[256,512]{1,0:T(8,128)(2,1)S(1)}, bf16[256,512]{1,0:T(8,128)(2,1)}, u32[]{:S(2)}) copy-start(bf16[256,512]{1,0:T(8,128)(2,1)} %k_ref.1) | copy-start | bytes 786436
  36.3 24.9 %copy-start.1 = (bf16[256,512]{1,0:T(8,128)(2,1)S(1)}, bf16[256,512]{1,0:T(8,128)(2,1)}, u32[]{:S(2)}) copy-start(bf16[256,512]{1,0:T(8,128)(2,1)} %v_ref.1) | copy-start | bytes 786436
  36.3 24.9 %copy-start.2 = (bf16[256,512]{1,0:T(8,128)(2,1)S(1)}, bf16[256,512]{1,0:T(8,128)(2,1)}, u32[]{:S(2)}) copy-start(bf16[256,512]{1,0:T(8,128)(2,1)} %q_ref.1) | copy-start | bytes 786436
  36.3 24.9 %copy-start.3 = (bf16[256,512]{1,0:T(8,128)(2,1)S(1)}, bf16[256,512]{1,0:T(8,128)(2,1)}, u32[]{:S(2)}) copy-start(bf16[256,512]{1,0:T(8,128)(2,1)} %og_ref.1) | copy-start | bytes 786436
  36.3 24.9 %copy-start.10 = (f32[512]{0:T(512)S(1)}, f32[512]{0:T(512)}, u32[]{:S(2)}) copy-start(f32[512]{0:T(512)} %param.16) | copy-start | bytes 6148

commit v3 on v2

v3 whole, which is shorter than its diff:
```python
import functools
import math

import jax
import jax.numpy as jnp
import ml_dtypes
import numpy as np
from jax import lax
from jax.experimental import pallas as pl
from jax.experimental.pallas import tpu as pltpu
from jax.sharding import PartitionSpec as P

BF16 = jnp.bfloat16
F32 = jnp.float32
WEIGHT = 8 * 10**9


QUARTERS = 4


def place(here):
    along = 4
    return here // (2 * along), here // 2 % along, here % 2


def block_of(here, dz, dx, dc):
    z, x, c = place(here)
    z = z ^ dz
    return ((z ^ (1 - z // 2)) * 4 + (x + dx) % 4) * 2 + (c ^ dc)


def device_order(groups):
    return [block_of(here, 0, 0, 0) for here in range(groups)]


def send(block, dz, dx, dc):
    groups = lax.axis_size("context")
    order = device_order(groups)
    moves = [(here, order[block_of(here, dz, dx, dc)]) for here in range(groups)]
    return lax.ppermute(block, "context", moves)


def make_tables(order, rows):
    groups = len(order)
    length = 2 * groups * rows
    a = np.array(order)[None, :]
    b = np.arange(rows)[None, :]
    half = np.arange(groups)[:, None] + 0.5
    theta = 2.0 * math.pi * a * half / (2 * groups)
    first = np.concatenate([np.cos(theta), -np.sin(theta)], axis=0)
    psi = 2.0 * math.pi * b * half / length
    low = np.arange(rows // 2)[:, None]
    m = np.arange(rows // 2)[None, :]
    second = []
    for parity in (0, 1):
        phi = 2.0 * math.pi * ((low * (2 * m + parity)) % rows) / rows
        second.append(np.block([[np.cos(phi), -np.sin(phi)], [np.sin(phi), np.cos(phi)]]))
    second = np.stack(second)
    narrow = ml_dtypes.bfloat16
    return (
        first.astype(narrow),
        np.ascontiguousarray(first.T).astype(narrow),
        second.astype(narrow),
        np.ascontiguousarray(second.transpose(0, 2, 1)).astype(narrow),
        np.cos(psi).astype(np.float32),
        (-np.sin(psi)).astype(np.float32),
    )


def prep_kernel(f_hbm, k_hbm, v_hbm, q_hbm, og_hbm, out_ref, held, sems):
    owners, three, rows = out_ref.shape
    chans = three // 3
    copies = [
        pltpu.make_async_copy(src, held.at[i], sems.at[i]) for i, src in enumerate((f_hbm, k_hbm, v_hbm, q_hbm, og_hbm))
    ]
    for copy in copies:
        copy.start()

    def put(slot, block):
        out_ref[:, slot * chans : (slot + 1) * chans, :] = block.T.reshape(owners, chans, rows)

    copies[0].wait()
    put(1, held[0])
    copies[1].wait()
    copies[2].wait()
    put(0, held[1] * held[2])
    copies[3].wait()
    copies[4].wait()
    put(2, held[3] * held[4])


def halve(me, blocks, own_ref, other_ref):
    for dz in range(4):
        for dx in range(4):
            own_ref[dz, dx] = blocks[block_of(me, dz, dx, 0)]
            other_ref[dz, dx] = blocks[block_of(me, dz, dx, 1)]


def across_kernel(own_ref, other_ref, after_ref, out_ref):
    for sc, ref in enumerate((own_ref, other_ref)):
        for near in range(2):
            for dx in range(4):
                out_ref[sc, near, dx] = ref[2 + near, dx]


STEPS = [(near, dx) for near in range(2) for dx in range(4)]


def near_kernel(own_ref, other_ref, across_ref, *outs):
    for (near, dx), out in zip(STEPS, outs):
        for sc, ref in enumerate((own_ref, other_ref)):
            out[0, sc] = ref[near, dx]
            out[1, sc] = across_ref[sc, near, dx]


def gather(me, arrived, x_ref):
    for (near, dx), ref in zip(STEPS, arrived):
        for far in range(2):
            for sc in range(2):
                x_ref[block_of(me, near ^ (2 * far), -dx, sc)] = ref[far, sc]


def dot(a, b):
    return jnp.dot(a, b, preferred_element_type=F32)


def spectrum(items, first_ref, second_ref, twr, twi, t_ref):
    chans, groups, rows = items.shape
    h = rows // 2
    for c in range(chans):
        part = dot(first_ref[...], items[c])
        real, imag = part[:groups], part[groups:]
        tr, ti = real * twr - imag * twi, real * twi + imag * twr
        lines = slice(c * groups, (c + 1) * groups)
        t_ref[0, lines, :h] = (tr[:, :h] + tr[:, h:]).astype(BF16)
        t_ref[0, lines, h:] = (ti[:, :h] + ti[:, h:]).astype(BF16)
        t_ref[1, lines, :h] = (tr[:, :h] - tr[:, h:]).astype(BF16)
        t_ref[1, lines, h:] = (ti[:, :h] - ti[:, h:]).astype(BF16)
    return [dot(t_ref[parity], second_ref[parity]) for parity in (0, 1)]


def products(left, right, h, conjugate):
    lr, li, rr, ri = left[:, :h], left[:, h:], right[:, :h], right[:, h:]
    if conjugate:
        real, imag = lr * rr + li * ri, lr * ri - li * rr
    else:
        real, imag = lr * rr - li * ri, lr * ri + li * rr
    return jnp.concatenate([real.astype(BF16), imag.astype(BF16)], axis=1)


def signal(scale, even, odd, first_t_ref, twr, twi, v_ref):
    chans, twice, rows = v_ref.shape
    groups = twice // 2
    h = rows // 2
    even, odd = even.reshape(chans, groups, rows), odd.reshape(chans, groups, rows)
    for part, lanes in ((even + odd, slice(0, h)), (even - odd, slice(h, rows))):
        real, imag = part[:, :, :h], part[:, :, h:]
        v_ref[:, :groups, lanes] = (real * twr[:, lanes] + imag * twi[:, lanes]).astype(BF16)
        v_ref[:, groups:, lanes] = (imag * twr[:, lanes] - real * twi[:, lanes]).astype(BF16)
    out = jnp.stack([dot(first_t_ref[...], v_ref[c]) * scale for c in range(chans)], axis=0)
    return jnp.swapaxes(out.astype(BF16), 0, 1)


def forward_kernel(
    scale,
    x_ref,
    first_ref,
    first_t_ref,
    second_ref,
    second_t_ref,
    twr_ref,
    twi_ref,
    own_ref,
    other_ref,
    spec_ref,
    t_ref,
    v_ref,
    y_ref,
):
    groups, three, rows = x_ref.shape
    chans = three // 3
    h = rows // 2
    twr, twi = twr_ref[...], twi_ref[...]
    for s in range(2):
        items = jnp.swapaxes(x_ref[:, s * chans : (s + 1) * chans, :], 0, 1)
        for parity, bins in enumerate(spectrum(items, first_ref, second_ref, twr, twi, t_ref.at[s])):
            spec_ref[s, parity] = bins
    even, odd = (
        dot(products(spec_ref[0, parity], spec_ref[1, parity], h, False), second_t_ref[parity]) for parity in (0, 1)
    )
    y_ref[...] = signal(scale, even, odd, first_t_ref, twr, twi, v_ref)
    halve(lax.axis_index("context"), y_ref, own_ref, other_ref)


def backward_kernel(
    scale,
    x_ref,
    spec_ref,
    first_ref,
    first_t_ref,
    second_ref,
    second_t_ref,
    twr_ref,
    twi_ref,
    y_hbm,
    t_ref,
    v_ref,
    y_ref,
    sems,
):
    groups, three, rows = x_ref.shape
    chans = three // 3
    h = rows // 2
    twr, twi = twr_ref[...], twi_ref[...]
    items = jnp.swapaxes(x_ref[:, 2 * chans :, :], 0, 1)
    delta = spectrum(items, first_ref, second_ref, twr, twi, t_ref)
    copies = []
    for s in range(2):
        even, odd = (
            dot(products(spec_ref[1 - s, parity], delta[parity], h, True), second_t_ref[parity]) for parity in (0, 1)
        )
        y_ref[s] = signal(scale, even, odd, first_t_ref, twr, twi, v_ref.at[s])
        copy = pltpu.make_async_copy(y_ref.at[s], y_hbm.at[:, pl.ds(s * chans, chans), :], sems.at[s])
        copy.start()
        copies.append(copy)
    for copy in copies:
        copy.wait()


class Writer:
    def __init__(self, outs, held, sems):
        self.outs, self.held, self.sems, self.copies = outs, held, sems, []

    def put(self, i, p, block):
        step = self.held.shape[2]
        self.held[i, p] = block.astype(BF16)
        copy = pltpu.make_async_copy(self.held.at[i, p], self.outs[i].at[pl.ds(p * step, step)], self.sems.at[i, p])
        copy.start()
        self.copies.append(copy)

    def wait(self):
        for copy in self.copies:
            copy.wait()


def forward_gate_kernel(*refs):
    arrived = refs[:8]
    q_ref, k_ref, v_ref, og_ref, bias_ref, mixed_hbm, qg_hbm, x_ref, held, sems = refs[8:]
    gather(lax.axis_index("context"), arrived, x_ref)
    owners, chans, rows = x_ref.shape
    writer = Writer((mixed_hbm, qg_hbm), held, sems)
    parts, step = held.shape[1:3]
    for p in range(parts):
        span = slice(p * step, (p + 1) * step)
        term = x_ref[:, :, span].reshape(owners * chans, step).T
        pre_gate = term.astype(F32) + bias_ref[...] * (k_ref[span] * v_ref[span]).astype(F32)
        writer.put(0, p, q_ref[span].astype(F32) * pre_gate)
        writer.put(1, p, og_ref[span].astype(F32) * pre_gate)
    writer.wait()


def backward_gate_kernel(y_ref, q_ref, k_ref, v_ref, og_ref, bias_ref, kg_hbm, vg_hbm, fg_hbm, held, sems):
    owners, pair, rows = y_ref.shape
    chans = pair // 2
    writer = Writer((kg_hbm, vg_hbm, fg_hbm), held, sems)
    parts, step = held.shape[1:3]
    for p in range(parts):
        span = slice(p * step, (p + 1) * step)

        def take(slot):
            return y_ref[:, slot * chans : (slot + 1) * chans, span].reshape(owners * chans, step).T

        writer.put(2, p, take(1))
        gated_grad = take(0).astype(F32) + bias_ref[...] * (og_ref[span] * q_ref[span]).astype(F32)
        writer.put(0, p, gated_grad * v_ref[span].astype(F32))
        writer.put(1, p, gated_grad * k_ref[span].astype(F32))
    writer.wait()


def local(q_gate, k_gate, v_input, filter_taps, skip_bias, out_grad):
    groups = lax.axis_size("context")
    rows, width = q_gate.shape
    chans = width // groups
    order = device_order(groups)
    seq = groups * rows
    scale = 2.0 / (2 * seq) / math.sqrt(seq)
    messages = jax.ShapeDtypeStruct((groups, 3 * chans, rows), BF16)
    whole = jax.ShapeDtypeStruct((rows, width), BF16)
    limit = pltpu.CompilerParams(vmem_limit_bytes=48 * 1024 * 1024)
    far = pl.BlockSpec(memory_space=pltpu.HBM)
    near = pl.BlockSpec(memory_space=pltpu.VMEM)

    def swap(block):
        return lax.all_to_all(
            block, "context", split_axis=0, concat_axis=0, tiled=True, axis_index_groups=[order]
        )

    block = (chans, rows)
    bins = (chans * groups, rows)

    def call(kernel, name, out_shape, scratch_shapes=(), weight=0, **more):
        if weight:
            more["cost_estimate"] = pl.CostEstimate(flops=weight, bytes_accessed=weight, transcendentals=0)
        return pl.pallas_call(
            kernel, out_shape=out_shape, scratch_shapes=list(scratch_shapes), compiler_params=limit, name=name, **more
        )

    def shape(*dims):
        return jax.ShapeDtypeStruct(dims, BF16)

    def travel(own, other, after):
        other = send(other, 0, 0, 1)
        across = call(
            across_kernel,
            "across",
            shape(2, 2, 4, *block),
            weight=WEIGHT,
            in_specs=[near] * 2 + [pl.BlockSpec(memory_space=pl.ANY)],
            out_specs=near,
        )(own, other, after)
        across = send(across, 2, 0, 0)
        kept, *leaving = call(near_kernel, "near", [shape(2, 2, *block)] * 8, weight=WEIGHT)(own, other, across)
        return [kept] + [send(part, dz, dx, 0) for part, (dz, dx) in zip(leaving, STEPS[1:])]

    first, first_t, second, second_t, twr, twi = make_tables(order, rows)
    sent = call(
        prep_kernel,
        "gate_and_pack",
        pltpu.VMEM(messages.shape, BF16),
        [pltpu.VMEM((5, rows, width), BF16), pltpu.SemaphoreType.DMA((5,))],
        in_specs=[far] * 5,
        out_specs=near,
    )(*(pltpu.with_memory_space_constraint(x, pltpu.HBM) for x in (filter_taps, k_gate, v_input, q_gate, out_grad)))
    items = swap(sent)
    own, other, spec = call(
        functools.partial(forward_kernel, scale),
        "forward",
        [shape(4, 4, *block)] * 2 + [jax.ShapeDtypeStruct((2, 2, *bins), F32)],
        [pltpu.VMEM((2, 2, *bins), BF16), pltpu.VMEM((chans, 2 * groups, rows), BF16), pltpu.VMEM((groups, *block), BF16)],
    )(items, first, first_t, second, second_t, twr, twi)
    terms = call(
        functools.partial(backward_kernel, scale),
        "backward",
        shape(groups, 2 * chans, rows),
        [
            pltpu.VMEM((2, *bins), BF16),
            pltpu.VMEM((2, chans, 2 * groups, rows), BF16),
            pltpu.VMEM((2, groups, *block), BF16),
            pltpu.SemaphoreType.DMA((2,)),
        ],
        in_specs=[near] * 8,
        out_specs=far,
    )(items, spec, first, first_t, second, second_t, twr, twi)
    arrived = travel(own, other, terms)
    gates = (q_gate, k_gate, v_input, out_grad, skip_bias[None, :])
    parts = 2

    def held(outs):
        return [pltpu.VMEM((outs, parts, rows // parts, width), BF16), pltpu.SemaphoreType.DMA((outs, parts))]

    mixed, q_grad = call(
        forward_gate_kernel,
        "gate_forward",
        [whole] * 2,
        [pltpu.VMEM((groups, *block), BF16)] + held(2),
        weight=WEIGHT,
        in_specs=[near] * 13,
        out_specs=[far] * 2,
    )(*arrived, *gates)
    k_grad, v_grad, filter_grad = call(
        backward_gate_kernel, "gate_backward", [whole] * 3, held(3), in_specs=[near] * 6, out_specs=[far] * 3
    )(swap(terms), *gates)
    return mixed, q_grad, k_grad, v_grad, filter_grad


def solution(mesh):
    spec = P("context", "tensor")
    return jax.shard_map(
        local,
        mesh=mesh,
        in_specs=(spec, spec, spec, spec, P("tensor"), spec),
        out_specs=(spec,) * 5,
        check_vma=False,
    )
```

time: 62.7 us -> 60.5 us (0.965)
  blocking collectives: 56.2 us -> 31.3 us
  starting transfers between devices: 0 us -> 14.2 us
  waiting for transfers between devices: 0 us -> 6.29 us
  Pallas kernels: 5.37 us -> 7.21 us
    all_to_all x2 -> x1, blocking collectives: 56.2 us -> 31.3 us  [swap(): lax.all_to_all(block, 'context', split_axis=0, concat_axis=0, tiled=True,...]
    ppermute x0 -> x9, starting transfers between devices: none -> 8.51 us  [send(): return lax.ppermute(block, 'context', moves)]
    ppermute x0 -> x9, waiting for transfers between devices: none -> 6.16 us  [send(): return lax.ppermute(block, 'context', moves)]
    all_to_all x0 -> x1, starting transfers between devices: none -> 5.74 us  [swap(): lax.all_to_all(block, 'context', split_axis=0, concat_axis=0, tiled=True,...]
    pallas_call x3 -> x7, Pallas kernels: 5.37 us -> 7.21 us  [the longest x1 2.24 us: local(): call(functools.partial(backward_kernel, scale), 'backward', shape(groups,...]
  transfers between devices with their start and end apart: 0 -> 10, of which waited for: 0 -> 6; matrix products, arithmetic and copies ran while one was open for 0% -> 0% of each run, Pallas kernels for 0% -> 5%
where the time goes in v3:
time: 60.5 us; the launch traced here: 60 us
  blocking collectives  31.3 us (52%)
  starting transfers between devices  14.2 us (23%)
  Pallas kernels  7.21 us (12%)
  waiting for transfers between devices  6.29 us (10%)
  between operations  0.85 us (1%)
    all_to_all x1, blocking collectives, swap(): lax.all_to_all(block, 'context', split_axis=0, concat_axis=0, tiled=True,...  31.3 us
    ppermute x9, starting transfers between devices, send(): return lax.ppermute(block, 'context', moves)  8.51 us
    ppermute x9, waiting for transfers between devices, send(): return lax.ppermute(block, 'context', moves)  6.16 us
    all_to_all x1, starting transfers between devices, swap(): lax.all_to_all(block, 'context', split_axis=0, concat_axis=0, tiled=True,...  5.74 us
    pallas_call x1, Pallas kernels, local(): call(functools.partial(backward_kernel, scale), 'backward', shape(groups,...  2.24 us
    pallas_call x1, Pallas kernels, local(): call(prep_kernel, 'gate_and_pack', pltpu.VMEM(messages.shape, BF16), [plt...  1.48 us
    pallas_call x1, Pallas kernels, local(): call(functools.partial(forward_kernel, scale), 'forward', [shape(4, 4, *b...  1.41 us
  transfers between devices with their start and end apart: 10, of which 6 were waited for; matrix products, arithmetic and copies ran while one was open for 0% of the time, Pallas kernels for 5%

profile of v3, /device:TPU:1, one launch (start us, length us, event | category | flops | bytes accessed | tf_op | source)
XLA Modules:
  0.0 60.0 jit_solution(6317138970319685791)
XLA Ops:
  0.6 0.0 copy-start.8
  0.6 0.0 copy-start.9
  0.7 0.0 copy-start.4
  0.7 1.5 %gate_and_pack.1 = bf16[32,48,256]{2,1,0:T(8,128)(2,1)S(1)} custom-call(bf16[256,512]{1,0:T(8,128)(2,1)} %f_hbm.1, bf16[256,512]{1,0:T(8,128)(2,1)} %k_ref.1, bf16[256,512]{1,0:T(8,128)(2,1)} %v_ref.1, bf16[256,512]{1,0:T(8,128)(2,1)} %q_ref.1, bf16[256,512]{1,0:T(8,128)(2,1)} %og_ref.1), custom_call_target="tpu_custom_call" | custom-call | tf_op jit(solution)/shard_map/gate_and_pack/pallas_call | solution.py:326
  2.2 31.3 %all_to_all.10.x_ref = bf16[32,48,256]{2,1,0:T(8,128)(2,1)S(1)} all-to-all(bf16[32,48,256]{2,1,0:T(8,128)(2,1)S(1)} %gate_and_pack.1), channel_id=1, replica_groups={{64,72,80,88,96,104,112,120,0,8,16,24,32,40,48,56,128,136,144,152,160,1..., dimensions={0} | all-to-all | bytes 1572864 | tf_op jit(solution)/shard_map/all_to_all | solution.py:294
  33.5 1.4 %forward.1 = (bf16[4,4,16,256]{3,2,1,0:T(8,128)(2,1)S(1)}, bf16[4,4,16,256]{3,2,1,0:T(8,128)(2,1)S(1)}, f32[2,2,512,256]{3,2,1,0:T(8,128)S(1)}) custom-call(bf16[32,48,256]{2,1,0:T(8,128)(2,1)S(1)} %all_to_all.10.x_ref, bf16[64,32]{1,0:T(8,128)(2,1)S(1)} %copy-done.8, bf16[32,64]{1,0:T(8,128)(2,1)S(1)} %copy-done.9, bf16[2,256,256]{2,1,0:T(8,128)(2,1)S(1)} %copy-done.4, ...), custom_call_target="tpu_custom_call" | custom-call | tf_op jit(solution)/shard_map/forward/pallas_call | solution.py:335
  34.9 0.1 collective-permute-start
  35.0 2.2 %backward.1.after_ref = bf16[32,32,256]{2,1,0:T(8,128)(2,1)} custom-call(bf16[32,48,256]{2,1,0:T(8,128)(2,1)S(1)} %all_to_all.10.x_ref, f32[2,2,512,256]{3,2,1,0:T(8,128)S(1)} %get-tuple-element.23.spec_ref, bf16[64,32]{1,0:T(8,128)(2,1)S(1)} %copy-done.8, bf16[32,64]{1,0:T(8,128)(2,1)S(1)} %copy-done.9, bf16[2,256,256]{2,1,0:T(8,128)(2,1)S(1)} %copy-done.4, ...), custom_call_target="tpu_custom_call" | custom-call | tf_op jit(solution)/shard_map/backward/pallas_call | solution.py:341
  37.3 0.1 collective-permute-start.1
  37.4 5.7 %all-to-all-start.1 = ((bf16[32,32,256]{2,1,0:T(8,128)(2,1)}), bf16[32,32,256]{2,1,0:T(8,128)(2,1)S(1)}, u32[]{:S(2)}, u32[]{:S(2)}) async-start(bf16[32,32,256]{2,1,0:T(8,128)(2,1)} %backward.1.after_ref), calls=%async_computation.1 | async-start | bytes 1048576 | tf_op jit(solution)/shard_map/all_to_all | solution.py:294
  43.2 2.5 %collective-permute-done.1.across_ref = bf16[2,2,4,16,256]{4,3,2,1,0:T(8,128)(2,1)S(1)} collective-permute-done((bf16[2,2,4,16,256]{4,3,2,1,0:T(8,128)(2,1)S(1)}, bf16[2,2,4,16,256]{4,3,2,1,0:T(8,128)(2,1)S(1)}, u32[]{:S(2)}, u32[]{:S(2)}) %collective-permute-start.1) | collective-permute-done | bytes 131104 | tf_op jit(solution)/shard_map/ppermute | solution.py:40
  45.7 0.9 %collective-permute-start.2 = (bf16[2,2,16,256]{3,2,1,0:T(8,128)(2,1)S(1)}, bf16[2,2,16,256]{3,2,1,0:T(8,128)(2,1)S(1)}, u32[]{:S(2)}, u32[]{:S(2)}) collective-permute-start(bf16[2,2,16,256]{3,2,1,0:T(8,128)(2,1)S(1)} %get-tuple-element.25), channel_id=1, source_target_pairs={{0,16},{8,24},{16,32},{24,40},{32,48},{40,56},{48,0},{56,8},{64,80... | collective-permute-start | bytes 98312 | tf_op jit(solution)/shard_map/ppermute | solution.py:40
  46.6 1.6 %collective-permute-start.3 = (bf16[2,2,16,256]{3,2,1,0:T(8,128)(2,1)S(1)}, bf16[2,2,16,256]{3,2,1,0:T(8,128)(2,1)S(1)}, u32[]{:S(2)}, u32[]{:S(2)}) collective-permute-start(bf16[2,2,16,256]{3,2,1,0:T(8,128)(2,1)S(1)} %get-tuple-element.26), channel_id=1, source_target_pairs={{0,32},{8,40},{16,48},{24,56},{32,0},{40,8},{48,16},{56,24},{64,96... | collective-permute-start | bytes 98312 | tf_op jit(solution)/shard_map/ppermute | solution.py:40
  48.2 1.0 %collective-permute-start.4 = (bf16[2,2,16,256]{3,2,1,0:T(8,128)(2,1)S(1)}, bf16[2,2,16,256]{3,2,1,0:T(8,128)(2,1)S(1)}, u32[]{:S(2)}, u32[]{:S(2)}) collective-permute-start(bf16[2,2,16,256]{3,2,1,0:T(8,128)(2,1)S(1)} %get-tuple-element.27), channel_id=1, source_target_pairs={{0,48},{8,56},{16,0},{24,8},{32,16},{40,24},{48,32},{56,40},{64,11... | collective-permute-start | bytes 98312 | tf_op jit(solution)/shard_map/ppermute | solution.py:40
  49.2 1.7 %collective-permute-start.6 = (bf16[2,2,16,256]{3,2,1,0:T(8,128)(2,1)S(1)}, bf16[2,2,16,256]{3,2,1,0:T(8,128)(2,1)S(1)}, u32[]{:S(2)}, u32[]{:S(2)}) collective-permute-start(bf16[2,2,16,256]{3,2,1,0:T(8,128)(2,1)S(1)} %get-tuple-element.29), channel_id=1, source_target_pairs={{0,80},{8,88},{16,96},{24,104},{32,112},{40,120},{48,64},{56,72},{... | collective-permute-start | bytes 98312 | tf_op jit(solution)/shard_map/ppermute | solution.py:40
  50.9 0.7 %collective-permute-done.2.refs_1_ = bf16[2,2,16,256]{3,2,1,0:T(8,128)(2,1)S(1)} collective-permute-done((bf16[2,2,16,256]{3,2,1,0:T(8,128)(2,1)S(1)}, bf16[2,2,16,256]{3,2,1,0:T(8,128)(2,1)S(1)}, u32[]{:S(2)}, u32[]{:S(2)}) %collective-permute-start.2) | collective-permute-done | bytes 32800 | tf_op jit(solution)/shard_map/ppermute | solution.py:40
  51.6 0.4 collective-permute-start.7
  52.0 0.2 collective-permute-done.3.refs_2_
  52.2 2.7 %collective-permute-start.8 = (bf16[2,2,16,256]{3,2,1,0:T(8,128)(2,1)S(1)}, bf16[2,2,16,256]{3,2,1,0:T(8,128)(2,1)S(1)}, u32[]{:S(2)}, u32[]{:S(2)}) collective-permute-start(bf16[2,2,16,256]{3,2,1,0:T(8,128)(2,1)S(1)} %get-tuple-element.31), channel_id=1, source_target_pairs={{0,112},{8,120},{16,64},{24,72},{32,80},{40,88},{48,96},{56,104},{... | collective-permute-start | bytes 98312 | tf_op jit(solution)/shard_map/ppermute | solution.py:40
  55.0 2.2 %collective-permute-done.7.refs_6_ = bf16[2,2,16,256]{3,2,1,0:T(8,128)(2,1)S(1)} collective-permute-done((bf16[2,2,16,256]{3,2,1,0:T(8,128)(2,1)S(1)}, bf16[2,2,16,256]{3,2,1,0:T(8,128)(2,1)S(1)}, u32[]{:S(2)}, u32[]{:S(2)}) %collective-permute-start.7) | collective-permute-done | bytes 32800 | tf_op jit(solution)/shard_map/ppermute | solution.py:40
  57.2 0.5 collective-permute-done.8.refs_7_
  57.8 1.0 %gate_forward.1 = (bf16[256,512]{1,0:T(8,128)(2,1)}, bf16[256,512]{1,0:T(8,128)(2,1)}) custom-call(bf16[2,2,16,256]{3,2,1,0:T(8,128)(2,1)S(1)} %get-tuple-element.24.refs_0_, bf16[2,2,16,256]{3,2,1,0:T(8,128)(2,1)S(1)} %collective-permute-done.2.refs_1_, bf16[2,2,16,256]{3,2,1,0:T(8,128)(2,1)S(1)} %collective-permute-done.3.refs_2_, ...), custom_call_target="tpu_custom_call" | custom-call | flops 8000000000 | bytes 8000000000 | tf_op jit(solution)/shard_map/gate_forward/pallas_call | solution.py:361
  58.8 0.1 all-to-all-done.1.y_ref
  58.9 1.0 %gate_backward.1 = (bf16[256,512]{1,0:T(8,128)(2,1)}, bf16[256,512]{1,0:T(8,128)(2,1)}, bf16[256,512]{1,0:T(8,128)(2,1)}) custom-call(bf16[32,32,256]{2,1,0:T(8,128)(2,1)S(1)} %all-to-all-done.1.y_ref, bf16[256,512]{1,0:T(8,128)(2,1)S(1)} %copy-done.2, bf16[256,512]{1,0:T(8,128)(2,1)S(1)} %copy-done, bf16[256,512]{1,0:T(8,128)(2,1)S(1)} %copy-done.1, ...), custom_call_target="tpu_custom_call" | custom-call | tf_op jit(solution)/shard_map/gate_backward/pallas_call | solution.py:370
  (26 shorter events, 0.1 us)
Async XLA Ops:
  0.6 32.8 %copy-start.8 = (bf16[64,32]{1,0:T(8,128)(2,1)S(1)}, bf16[64,32]{1,0:T(8,128)(2,1)}, u32[]{:S(2)}) copy-start(bf16[64,32]{1,0:T(8,128)(2,1)} %constant.12.clone.first_ref) | copy-start | bytes 12292
  0.6 32.8 %copy-start.9 = (bf16[32,64]{1,0:T(8,128)(2,1)S(1)}, bf16[32,64]{1,0:T(8,128)(2,1)}, u32[]{:S(2)}) copy-start(bf16[32,64]{1,0:T(8,128)(2,1)} %constant.13.clone.first_t_ref) | copy-start | bytes 12292
  0.7 32.8 %copy-start.4 = (bf16[2,256,256]{2,1,0:T(8,128)(2,1)S(1)}, bf16[2,256,256]{2,1,0:T(8,128)(2,1)}, u32[]{:S(2)}) copy-start(bf16[2,256,256]{2,1,0:T(8,128)(2,1)} %constant.14.clone.second_ref) | copy-start | bytes 786436
  0.7 32.8 %copy-start.5 = (bf16[2,256,256]{2,1,0:T(8,128)(2,1)S(1)}, bf16[2,256,256]{2,1,0:T(8,128)(2,1)}, u32[]{:S(2)}) copy-start(bf16[2,256,256]{2,1,0:T(8,128)(2,1)} %constant.15.clone.second_t_ref) | copy-start | bytes 786436
  0.7 32.8 %copy-start.6 = (f32[32,256]{1,0:T(8,128)S(1)}, f32[32,256]{1,0:T(8,128)}, u32[]{:S(2)}) copy-start(f32[32,256]{1,0:T(8,128)} %constant.16.clone.twr_ref) | copy-start | bytes 98308
  0.7 32.8 %copy-start.7 = (f32[32,256]{1,0:T(8,128)S(1)}, f32[32,256]{1,0:T(8,128)}, u32[]{:S(2)}) copy-start(f32[32,256]{1,0:T(8,128)} %constant.17.clone.twi_ref) | copy-start | bytes 98308
  34.9 2.3 %collective-permute-start = (bf16[4,4,16,256]{3,2,1,0:T(8,128)(2,1)S(1)}, bf16[4,4,16,256]{3,2,1,0:T(8,128)(2,1)S(1)}, u32[]{:S(2)}, u32[]{:S(2)}) collective-permute-start(bf16[4,4,16,256]{3,2,1,0:T(8,128)(2,1)S(1)} %get-tuple-element.22), channel_id=1, source_target_pairs={{0,8},{8,0},{16,24},{24,16},{32,40},{40,32},{48,56},{56,48},{64,72... | collective-permute-start | bytes 393224 | tf_op jit(solution)/shard_map/ppermute | solution.py:40
  37.3 8.4 %collective-permute-start.1 = (bf16[2,2,4,16,256]{4,3,2,1,0:T(8,128)(2,1)S(1)}, bf16[2,2,4,16,256]{4,3,2,1,0:T(8,128)(2,1)S(1)}, u32[]{:S(2)}, u32[]{:S(2)}) collective-permute-start(bf16[2,2,4,16,256]{4,3,2,1,0:T(8,128)(2,1)S(1)} %across.1), channel_id=1, source_target_pairs={{0,128},{8,136},{16,144},{24,152},{32,160},{40,168},{48,176},{56,1... | collective-permute-start | bytes 393224 | tf_op jit(solution)/shard_map/ppermute | solution.py:40
  37.4 21.5 %all-to-all-start.1 = ((bf16[32,32,256]{2,1,0:T(8,128)(2,1)}), bf16[32,32,256]{2,1,0:T(8,128)(2,1)S(1)}, u32[]{:S(2)}, u32[]{:S(2)}) async-start(bf16[32,32,256]{2,1,0:T(8,128)(2,1)} %backward.1.after_ref), calls=%async_computation.1 | async-start | bytes 1048576 | tf_op jit(solution)/shard_map/all_to_all | solution.py:294
  43.2 14.6 %copy-start = (bf16[256,512]{1,0:T(8,128)(2,1)S(1)}, bf16[256,512]{1,0:T(8,128)(2,1)}, u32[]{:S(2)}) copy-start(bf16[256,512]{1,0:T(8,128)(2,1)} %k_ref.1) | copy-start | bytes 786436
  43.2 14.6 %copy-start.1 = (bf16[256,512]{1,0:T(8,128)(2,1)S(1)}, bf16[256,512]{1,0:T(8,128)(2,1)}, u32[]{:S(2)}) copy-start(bf16[256,512]{1,0:T(8,128)(2,1)} %v_ref.1) | copy-start | bytes 786436
  43.2 14.6 %copy-start.2 = (bf16[256,512]{1,0:T(8,128)(2,1)S(1)}, bf16[256,512]{1,0:T(8,128)(2,1)}, u32[]{:S(2)}) copy-start(bf16[256,512]{1,0:T(8,128)(2,1)} %q_ref.1) | copy-start | bytes 786436
  43.2 14.6 %copy-start.3 = (bf16[256,512]{1,0:T(8,128)(2,1)S(1)}, bf16[256,512]{1,0:T(8,128)(2,1)}, u32[]{:S(2)}) copy-start(bf16[256,512]{1,0:T(8,128)(2,1)} %og_ref.1) | copy-start | bytes 786436
  43.2 14.6 %copy-start.10 = (f32[512]{0:T(512)S(1)}, f32[512]{0:T(512)}, u32[]{:S(2)}) copy-start(f32[512]{0:T(512)} %param.16) | copy-start | bytes 6148
  45.7 5.9 %collective-permute-start.2 = (bf16[2,2,16,256]{3,2,1,0:T(8,128)(2,1)S(1)}, bf16[2,2,16,256]{3,2,1,0:T(8,128)(2,1)S(1)}, u32[]{:S(2)}, u32[]{:S(2)}) collective-permute-start(bf16[2,2,16,256]{3,2,1,0:T(8,128)(2,1)S(1)} %get-tuple-element.25), channel_id=1, source_target_pairs={{0,16},{8,24},{16,32},{24,40},{32,48},{40,56},{48,0},{56,8},{64,80... | collective-permute-start | bytes 98312 | tf_op jit(solution)/shard_map/ppermute | solution.py:40
  46.6 5.7 %collective-permute-start.3 = (bf16[2,2,16,256]{3,2,1,0:T(8,128)(2,1)S(1)}, bf16[2,2,16,256]{3,2,1,0:T(8,128)(2,1)S(1)}, u32[]{:S(2)}, u32[]{:S(2)}) collective-permute-start(bf16[2,2,16,256]{3,2,1,0:T(8,128)(2,1)S(1)} %get-tuple-element.26), channel_id=1, source_target_pairs={{0,32},{8,40},{16,48},{24,56},{32,0},{40,8},{48,16},{56,24},{64,96... | collective-permute-start | bytes 98312 | tf_op jit(solution)/shard_map/ppermute | solution.py:40
  48.2 6.7 %collective-permute-start.4 = (bf16[2,2,16,256]{3,2,1,0:T(8,128)(2,1)S(1)}, bf16[2,2,16,256]{3,2,1,0:T(8,128)(2,1)S(1)}, u32[]{:S(2)}, u32[]{:S(2)}) collective-permute-start(bf16[2,2,16,256]{3,2,1,0:T(8,128)(2,1)S(1)} %get-tuple-element.27), channel_id=1, source_target_pairs={{0,48},{8,56},{16,0},{24,8},{32,16},{40,24},{48,32},{56,40},{64,11... | collective-permute-start | bytes 98312 | tf_op jit(solution)/shard_map/ppermute | solution.py:40
  49.2 5.8 %collective-permute-start.5 = (bf16[2,2,16,256]{3,2,1,0:T(8,128)(2,1)S(1)}, bf16[2,2,16,256]{3,2,1,0:T(8,128)(2,1)S(1)}, u32[]{:S(2)}, u32[]{:S(2)}) collective-permute-start(bf16[2,2,16,256]{3,2,1,0:T(8,128)(2,1)S(1)} %get-tuple-element.28), channel_id=1, source_target_pairs={{0,64},{8,72},{16,80},{24,88},{32,96},{40,104},{48,112},{56,120},{... | collective-permute-start | bytes 98312 | tf_op jit(solution)/shard_map/ppermute | solution.py:40
  49.2 5.8 %collective-permute-start.6 = (bf16[2,2,16,256]{3,2,1,0:T(8,128)(2,1)S(1)}, bf16[2,2,16,256]{3,2,1,0:T(8,128)(2,1)S(1)}, u32[]{:S(2)}, u32[]{:S(2)}) collective-permute-start(bf16[2,2,16,256]{3,2,1,0:T(8,128)(2,1)S(1)} %get-tuple-element.29), channel_id=1, source_target_pairs={{0,80},{8,88},{16,96},{24,104},{32,112},{40,120},{48,64},{56,72},{... | collective-permute-start | bytes 98312 | tf_op jit(solution)/shard_map/ppermute | solution.py:40
  51.6 5.6 %collective-permute-start.7 = (bf16[2,2,16,256]{3,2,1,0:T(8,128)(2,1)S(1)}, bf16[2,2,16,256]{3,2,1,0:T(8,128)(2,1)S(1)}, u32[]{:S(2)}, u32[]{:S(2)}) collective-permute-start(bf16[2,2,16,256]{3,2,1,0:T(8,128)(2,1)S(1)} %get-tuple-element.30), channel_id=1, source_target_pairs={{0,96},{8,104},{16,112},{24,120},{32,64},{40,72},{48,80},{56,88},{... | collective-permute-start | bytes 98312 | tf_op jit(solution)/shard_map/ppermute | solution.py:40
  52.2 5.5 %collective-permute-start.8 = (bf16[2,2,16,256]{3,2,1,0:T(8,128)(2,1)S(1)}, bf16[2,2,16,256]{3,2,1,0:T(8,128)(2,1)S(1)}, u32[]{:S(2)}, u32[]{:S(2)}) collective-permute-start(bf16[2,2,16,256]{3,2,1,0:T(8,128)(2,1)S(1)} %get-tuple-element.31), channel_id=1, source_target_pairs={{0,112},{8,120},{16,64},{24,72},{32,80},{40,88},{48,96},{56,104},{... | collective-permute-start | bytes 98312 | tf_op jit(solution)/shard_map/ppermute | solution.py:40

commit v4 on v3

v4 whole, which is shorter than its diff:
```python
import functools
import math

import jax
import jax.numpy as jnp
import ml_dtypes
import numpy as np
from jax import lax
from jax.experimental import pallas as pl
from jax.experimental.pallas import tpu as pltpu
from jax.sharding import PartitionSpec as P

BF16 = jnp.bfloat16
ZORDER = (1, 2, 3)
F32 = jnp.float32
WEIGHT1 = 5 * 10**9
WEIGHT = 8 * 10**9


QUARTERS = 4


def place(here):
    along = 4
    return here // (2 * along), here // 2 % along, here % 2


def block_of(here, dz, dx, dc):
    z, x, c = place(here)
    z = z ^ dz
    return ((z ^ (1 - z // 2)) * 4 + (x + dx) % 4) * 2 + (c ^ dc)


def device_order(groups):
    return [block_of(here, 0, 0, 0) for here in range(groups)]


def send(block, dz, dx, dc):
    groups = lax.axis_size("context")
    order = device_order(groups)
    moves = [(here, order[block_of(here, dz, dx, dc)]) for here in range(groups)]
    return lax.ppermute(block, "context", moves)


def make_tables(order, rows):
    groups = len(order)
    length = 2 * groups * rows
    a = np.array(order)[None, :]
    b = np.arange(rows)[None, :]
    half = np.arange(groups)[:, None] + 0.5
    theta = 2.0 * math.pi * a * half / (2 * groups)
    first = np.concatenate([np.cos(theta), -np.sin(theta)], axis=0)
    psi = 2.0 * math.pi * b * half / length
    low = np.arange(rows // 2)[:, None]
    m = np.arange(rows // 2)[None, :]
    second = []
    for parity in (0, 1):
        phi = 2.0 * math.pi * ((low * (2 * m + parity)) % rows) / rows
        second.append(np.block([[np.cos(phi), -np.sin(phi)], [np.sin(phi), np.cos(phi)]]))
    second = np.stack(second)
    narrow = ml_dtypes.bfloat16
    return (
        first.astype(narrow),
        np.ascontiguousarray(first.T).astype(narrow),
        second.astype(narrow),
        np.ascontiguousarray(second.transpose(0, 2, 1)).astype(narrow),
        np.cos(psi).astype(np.float32),
        (-np.sin(psi)).astype(np.float32),
    )


def halve(me, blocks, own_ref, other_ref):
    for dz in range(4):
        for dx in range(4):
            own_ref[dz, dx] = blocks[block_of(me, dz, dx, 0)]
            other_ref[dz, dx] = blocks[block_of(me, dz, dx, 1)]


def turn(block, chans):
    rows, width = block.shape
    return block.T.reshape(width // chans, chans, rows)


def pack_early_kernel(f_hbm, k_hbm, v_hbm, own_ref, other_ref, rest_ref, held, turned, sems):
    owners, chans, h = rest_ref.shape
    rows = 2 * h
    copies = [pltpu.make_async_copy(src, held.at[i], sems.at[i]) for i, src in enumerate((f_hbm, k_hbm, v_hbm))]
    for copy in copies:
        copy.start()
    me = lax.axis_index("context")
    copies[0].wait()
    turned[:, :, :rows] = turn(held[0], chans)
    copies[1].wait()
    copies[2].wait()
    gated = turn(held[1] * held[2], chans)
    turned[:, :, rows:] = gated[:, :, :h]
    rest_ref[...] = gated[:, :, h:]
    halve(me, turned, own_ref, other_ref)


def pack_late_kernel(q_hbm, og_hbm, rest_ref, out_hbm, held, out_ref, sems):
    owners, chans, rows = out_ref.shape
    copies = [pltpu.make_async_copy(src, held.at[i], sems.at[i]) for i, src in enumerate((q_hbm, og_hbm))]
    leaving = [
        pltpu.make_async_copy(rest_ref, out_hbm.at[:, :, pl.ds(rows, rows // 2)], sems.at[2]),
        pltpu.make_async_copy(out_ref, out_hbm.at[:, :, pl.ds(0, rows)], sems.at[3]),
    ]
    for copy in copies:
        copy.start()
    leaving[0].start()
    for copy in copies:
        copy.wait()
    out_ref[...] = turn(held[0] * held[1], chans)
    leaving[1].start()
    for copy in leaving:
        copy.wait()


def along_z_kernel(own_ref, other_ref, after_ref, *outs):
    for dz, out in enumerate(outs, start=1):
        for sc, ref in enumerate((own_ref, other_ref)):
            for dx in range(4):
                out[sc, dx] = ref[dz, dx]


def along_x_kernel(own_ref, other_ref, *refs):
    arrived, outs = refs[:3], refs[3:]
    for dx, out in enumerate(outs):
        for sc, ref in enumerate((own_ref, other_ref)):
            out[0, sc] = ref[0, dx]
            for dz, ref in enumerate(arrived, start=1):
                out[dz, sc] = ref[sc, dx]


def gather(me, arrived, x_ref):
    for dx, ref in enumerate(arrived):
        for dz in range(4):
            for sc in range(2):
                x_ref[block_of(me, dz, -dx, sc)] = ref[dz, sc]


def dot(a, b):
    return jnp.dot(a, b, preferred_element_type=F32)


def spectrum(items, first_ref, second_ref, twr, twi, t_ref):
    chans, groups, rows = items.shape
    h = rows // 2
    for c in range(chans):
        part = dot(first_ref[...], items[c])
        real, imag = part[:groups], part[groups:]
        tr, ti = real * twr - imag * twi, real * twi + imag * twr
        lines = slice(c * groups, (c + 1) * groups)
        t_ref[0, lines, :h] = (tr[:, :h] + tr[:, h:]).astype(BF16)
        t_ref[0, lines, h:] = (ti[:, :h] + ti[:, h:]).astype(BF16)
        t_ref[1, lines, :h] = (tr[:, :h] - tr[:, h:]).astype(BF16)
        t_ref[1, lines, h:] = (ti[:, :h] - ti[:, h:]).astype(BF16)
    return [dot(t_ref[parity], second_ref[parity]) for parity in (0, 1)]


def filter_kernel(*refs):
    arrived = refs[:4]
    first_ref, second_ref, twr_ref, twi_ref, spec_ref, rest_ref, x_ref, t_ref = refs[4:]
    gather(lax.axis_index("context"), arrived, x_ref)
    rows = twr_ref.shape[1]
    items = jnp.swapaxes(x_ref[:, :, :rows], 0, 1)
    for parity, bins in enumerate(spectrum(items, first_ref, second_ref, twr_ref[...], twi_ref[...], t_ref)):
        spec_ref[parity] = bins
    rest_ref[...] = x_ref[:, :, rows:]


def products(left, right, h, conjugate):
    lr, li, rr, ri = left[:, :h], left[:, h:], right[:, :h], right[:, h:]
    if conjugate:
        real, imag = lr * rr + li * ri, lr * ri - li * rr
    else:
        real, imag = lr * rr - li * ri, lr * ri + li * rr
    return jnp.concatenate([real.astype(BF16), imag.astype(BF16)], axis=1)


def signal(scale, even, odd, first_t_ref, twr, twi, v_ref):
    chans, twice, rows = v_ref.shape
    groups = twice // 2
    h = rows // 2
    even, odd = even.reshape(chans, groups, rows), odd.reshape(chans, groups, rows)
    for part, lanes in ((even + odd, slice(0, h)), (even - odd, slice(h, rows))):
        real, imag = part[:, :, :h], part[:, :, h:]
        v_ref[:, :groups, lanes] = (real * twr[:, lanes] + imag * twi[:, lanes]).astype(BF16)
        v_ref[:, groups:, lanes] = (imag * twr[:, lanes] - real * twi[:, lanes]).astype(BF16)
    out = jnp.stack([dot(first_t_ref[...], v_ref[c]) * scale for c in range(chans)], axis=0)
    return jnp.swapaxes(out.astype(BF16), 0, 1)


def forward_kernel(
    scale,
    x_ref,
    taps_ref,
    part_ref,
    first_ref,
    first_t_ref,
    second_ref,
    second_t_ref,
    twr_ref,
    twi_ref,
    own_ref,
    other_ref,
    rest_ref,
    spec_ref,
    t_ref,
    v_ref,
    y_ref,
):
    rows = twr_ref.shape[1]
    h = rows // 2
    twr, twi = twr_ref[...], twi_ref[...]
    gated = jnp.concatenate([part_ref[...], x_ref[:, :, rows:]], axis=2)
    spectra = [
        spectrum(jnp.swapaxes(block, 0, 1), first_ref, second_ref, twr, twi, t_ref.at[s])
        for s, block in enumerate((gated, x_ref[:, :, :rows]))
    ]
    gated, delta = spectra
    taps = taps_ref
    for parity in (0, 1):
        spec_ref[0, parity] = gated[parity]
        spec_ref[1, parity] = delta[parity]
    even, odd = (dot(products(gated[parity], taps[parity], h, False), second_t_ref[parity]) for parity in (0, 1))
    y_ref[:, :, :rows] = signal(scale, even, odd, first_t_ref, twr, twi, v_ref.at[0])
    even, odd = (dot(products(taps[parity], delta[parity], h, True), second_t_ref[parity]) for parity in (0, 1))
    back = signal(scale, even, odd, first_t_ref, twr, twi, v_ref.at[1])
    y_ref[:, :, rows:] = back[:, :, :h]
    rest_ref[...] = back[:, :, h:]
    halve(lax.axis_index("context"), y_ref, own_ref, other_ref)


def backward_kernel(
    scale, spec_ref, rest_ref, first_t_ref, second_t_ref, twr_ref, twi_ref, y_hbm, v_ref, y_ref, sems
):
    groups, chans, rows = y_ref.shape
    h = rows // 2
    twr, twi = twr_ref[...], twi_ref[...]
    copies = [
        pltpu.make_async_copy(rest_ref, y_hbm.at[:, :, pl.ds(rows, h)], sems.at[0]),
        pltpu.make_async_copy(y_ref, y_hbm.at[:, :, pl.ds(0, rows)], sems.at[1]),
    ]
    copies[0].start()
    even, odd = (dot(products(spec_ref[0, parity], spec_ref[1, parity], h, True), second_t_ref[parity]) for parity in (0, 1))
    y_ref[...] = signal(scale, even, odd, first_t_ref, twr, twi, v_ref)
    copies[1].start()
    for copy in copies:
        copy.wait()


class Writer:
    def __init__(self, outs, held, sems):
        self.outs, self.held, self.sems, self.copies = outs, held, sems, []

    def put(self, i, p, block):
        step = self.held.shape[2]
        self.held[i, p] = block.astype(BF16)
        copy = pltpu.make_async_copy(self.held.at[i, p], self.outs[i].at[pl.ds(p * step, step)], self.sems.at[i, p])
        copy.start()
        self.copies.append(copy)

    def wait(self):
        for copy in self.copies:
            copy.wait()


def gate_kernel(*refs):
    arrived = refs[:4]
    y_ref, q_ref, k_ref, v_ref, og_ref, bias_ref, mixed_hbm, qg_hbm, kg_hbm, vg_hbm, fg_hbm, x_ref, held, sems = refs[4:]
    owners, chans, _ = x_ref.shape
    writer = Writer((mixed_hbm, qg_hbm, kg_hbm, vg_hbm, fg_hbm), held, sems)
    parts, step = held.shape[1:3]
    bias = bias_ref[...]

    def take(ref, p):
        return ref[:, :, p * step : (p + 1) * step].reshape(owners * chans, step).T

    for p in range(parts):
        writer.put(4, p, take(y_ref, p))
    gather(lax.axis_index("context"), arrived, x_ref)
    for p in range(parts):
        span = slice(p * step, (p + 1) * step)
        q, k, v, og = q_ref[span], k_ref[span], v_ref[span], og_ref[span]
        pre_gate = take(x_ref, p).astype(F32) + bias * (k * v).astype(F32)
        writer.put(0, p, q.astype(F32) * pre_gate)
        writer.put(1, p, og.astype(F32) * pre_gate)
        back = take((x_ref, y_ref)[p], parts)
        gated_grad = back.astype(F32) + bias * (og * q).astype(F32)
        writer.put(2, p, gated_grad * v.astype(F32))
        writer.put(3, p, gated_grad * k.astype(F32))
    writer.wait()


def local(q_gate, k_gate, v_input, filter_taps, skip_bias, out_grad):
    groups = lax.axis_size("context")
    rows, width = q_gate.shape
    chans = width // groups
    order = device_order(groups)
    seq = groups * rows
    scale = 2.0 / (2 * seq) / math.sqrt(seq)
    messages = jax.ShapeDtypeStruct((groups, 3 * chans, rows), BF16)
    whole = jax.ShapeDtypeStruct((rows, width), BF16)
    limit = pltpu.CompilerParams(vmem_limit_bytes=48 * 1024 * 1024)
    far = pl.BlockSpec(memory_space=pltpu.HBM)
    near = pl.BlockSpec(memory_space=pltpu.VMEM)

    def swap(block):
        return lax.all_to_all(
            block, "context", split_axis=0, concat_axis=0, tiled=True, axis_index_groups=[order]
        )

    block = (chans, rows + rows // 2)
    bins = (chans * groups, rows)

    def call(kernel, name, out_shape, scratch_shapes=(), weight=0, **more):
        if weight:
            more["cost_estimate"] = pl.CostEstimate(flops=weight, bytes_accessed=weight, transcendentals=0)
        return pl.pallas_call(
            kernel, out_shape=out_shape, scratch_shapes=list(scratch_shapes), compiler_params=limit, name=name, **more
        )

    def shape(*dims):
        return jax.ShapeDtypeStruct(dims, BF16)

    def travel(own, other, after, weight):
        other = send(other, 0, 0, 1)
        leaving = call(
            along_z_kernel,
            "along_z",
            [shape(2, 4, *own.shape[2:])] * 3,
            weight=weight,
            in_specs=[near] * 2 + [pl.BlockSpec(memory_space=pl.ANY)],
            out_specs=[near] * 3,
        )(own, other, after)
        arrived = [None] * 3
        for dz in ZORDER:
            arrived[dz - 1] = send(leaving[dz - 1], dz, 0, 0)
        kept, *leaving = call(along_x_kernel, "along_x", [shape(4, 2, *own.shape[2:])] * 4, weight=weight)(
            own, other, *arrived
        )
        return [kept] + [send(part, 0, dx, 0) for dx, part in enumerate(leaving, start=1)]

    first, first_t, second, second_t, twr, twi = make_tables(order, rows)
    def keep(*arrays):
        return [pltpu.with_memory_space_constraint(x, pltpu.HBM) for x in arrays]

    one, half = (chans, rows), (chans, rows // 2)
    own, other, rest = call(
        pack_early_kernel,
        "pack_early",
        [pltpu.VMEM((4, 4, *block), BF16)] * 2 + [pltpu.VMEM((groups, *half), BF16)],
        [pltpu.VMEM((3, rows, width), BF16), pltpu.VMEM((groups, *block), BF16), pltpu.SemaphoreType.DMA((3,))],
        in_specs=[far] * 3,
        out_specs=[near] * 3,
    )(*keep(filter_taps, k_gate, v_input))
    sent = call(
        pack_late_kernel,
        "pack_late",
        shape(groups, *block),
        [pltpu.VMEM((2, rows, width), BF16), pltpu.VMEM((groups, *one), BF16), pltpu.SemaphoreType.DMA((4,))],
        in_specs=[far] * 2 + [near],
        out_specs=far,
    )(*keep(q_gate, out_grad), rest)
    taps, part = call(
        filter_kernel,
        "filter_spectrum",
        [jax.ShapeDtypeStruct((2, *bins), F32), shape(groups, *half)],
        [pltpu.VMEM((groups, *block), BF16), pltpu.VMEM((2, *bins), BF16)],
        weight=WEIGHT1,
    )(*travel(own, other, sent, WEIGHT1), first, second, twr, twi)
    items = swap(sent)
    own, other, rest, spec = call(
        functools.partial(forward_kernel, scale),
        "forward",
        [shape(4, 4, *block)] * 2
        + [shape(groups, *half), jax.ShapeDtypeStruct((2, 2, *bins), F32)],
        [
            pltpu.VMEM((2, 2, *bins), BF16),
            pltpu.VMEM((2, chans, 2 * groups, rows), BF16),
            pltpu.VMEM((groups, *block), BF16),
        ],
    )(items, taps, part, first, first_t, second, second_t, twr, twi)
    terms = call(
        functools.partial(backward_kernel, scale),
        "backward",
        shape(groups, *block),
        [
            pltpu.VMEM((chans, 2 * groups, rows), BF16),
            pltpu.VMEM((groups, *one), BF16),
            pltpu.SemaphoreType.DMA((2,)),
        ],
        in_specs=[near] * 6,
        out_specs=far,
    )(spec, rest, first_t, second_t, twr, twi)
    arrived = travel(own, other, terms, WEIGHT)
    parts = 2
    return call(
        gate_kernel,
        "gate",
        [whole] * 5,
        [
            pltpu.VMEM((groups, *block), BF16),
            pltpu.VMEM((5, parts, rows // parts, width), BF16),
            pltpu.SemaphoreType.DMA((5, parts)),
        ],
        in_specs=[near] * 10,
        out_specs=[far] * 5,
    )(*arrived, swap(terms), q_gate, k_gate, v_input, out_grad, skip_bias[None, :])


def solution(mesh):
    spec = P("context", "tensor")
    return jax.shard_map(
        local,
        mesh=mesh,
        in_specs=(spec, spec, spec, spec, P("tensor"), spec),
        out_specs=(spec,) * 5,
        check_vma=False,
    )
```

time: 60.5 us -> 60.1 us (level)
  blocking collectives: 31.3 us -> 0 us
  starting transfers between devices: 14.2 us -> 34.9 us
  waiting for transfers between devices: 6.29 us -> 15.3 us
  Pallas kernels: 7.21 us -> 8.58 us
    all_to_all x1 -> x0, blocking collectives: 31.3 us -> none  [swap(): lax.all_to_all(block, 'context', split_axis=0, concat_axis=0, tiled=True,...]
    ppermute x9 -> x14, starting transfers between devices: 8.51 us -> 20.9 us  [send(): return lax.ppermute(block, 'context', moves)]
    all_to_all x1 -> x2, starting transfers between devices: 5.74 us -> 14 us  [swap(): lax.all_to_all(block, 'context', split_axis=0, concat_axis=0, tiled=True,...]
    ppermute x9 -> x14, waiting for transfers between devices: 6.16 us -> 13.6 us  [send(): return lax.ppermute(block, 'context', moves)]
    pallas_call x5 -> x8, Pallas kernels: 3.57 us -> 5.24 us  [the longest x1 1.94 us: local(): call(pack_late_kernel, 'pack_late', shape(groups, *block), [pltpu.VMEM((2...]
    all_to_all x1 -> x2, waiting for transfers between devices: 0.13 us -> 1.72 us  [swap(): lax.all_to_all(block, 'context', split_axis=0, concat_axis=0, tiled=True,...]
    pallas_call x1, Pallas kernels: 2.24 us -> 1.32 us  [local(): call(functools.partial(backward_kernel, scale), 'backward', shape(groups,...]
    pallas_call x1, Pallas kernels: 1.41 us -> 2.02 us  [local(): call(functools.partial(forward_kernel, scale), 'forward', [shape(4, 4, *b...]
  transfers between devices with their start and end apart: 10 -> 16, of which waited for: 6 -> 6; matrix products, arithmetic and copies ran while one was open for 0% -> 0% of each run, Pallas kernels for 5% -> 7%
where the time goes in v4:
time: 60.1 us; the launch traced here: 59.8 us
  starting transfers between devices  34.9 us (58%)
  waiting for transfers between devices  15.3 us (25%)
  Pallas kernels  8.58 us (14%)
  between operations  0.91 us (2%)
    ppermute x14, starting transfers between devices, send(): return lax.ppermute(block, 'context', moves)  20.9 us
    all_to_all x2, starting transfers between devices, swap(): lax.all_to_all(block, 'context', split_axis=0, concat_axis=0, tiled=True,...  14 us
    ppermute x14, waiting for transfers between devices, send(): return lax.ppermute(block, 'context', moves)  13.6 us
    pallas_call x1, Pallas kernels, local(): call(functools.partial(forward_kernel, scale), 'forward', [shape(4, 4, *b...  2.02 us
    pallas_call x1, Pallas kernels, local(): call(pack_late_kernel, 'pack_late', shape(groups, *block), [pltpu.VMEM((2...  1.94 us
    all_to_all x2, waiting for transfers between devices, swap(): lax.all_to_all(block, 'context', split_axis=0, concat_axis=0, tiled=True,...  1.72 us
    pallas_call x1, Pallas kernels, local(): call(functools.partial(backward_kernel, scale), 'backward', shape(groups,...  1.32 us
    pallas_call x1, Pallas kernels, local(): call(gate_kernel, 'gate', [whole] * 5, [pltpu.VMEM((groups, *block), BF16...  1.28 us
  transfers between devices with their start and end apart: 16, of which 6 were waited for; matrix products, arithmetic and copies ran while one was open for 0% of the time, Pallas kernels for 7%

profile of v4, /device:TPU:1, one launch (start us, length us, event | category | flops | bytes accessed | tf_op | source)
XLA Modules:
  0.0 59.8 jit_solution(788840617577527304)
XLA Ops:
  0.6 1.3 %pack_early.1 = (bf16[4,4,16,384]{3,2,1,0:T(8,128)(2,1)S(1)}, bf16[4,4,16,384]{3,2,1,0:T(8,128)(2,1)S(1)}, bf16[32,16,128]{2,1,0:T(8,128)(2,1)S(1)}) custom-call(bf16[256,512]{1,0:T(8,128)(2,1)} %f_hbm.1, bf16[256,512]{1,0:T(8,128)(2,1)} %refs_6_.2, bf16[256,512]{1,0:T(8,128)(2,1)} %refs_7_.2), custom_call_target="tpu_custom_call" | custom-call | tf_op jit(solution)/shard_map/pack_early/pallas_call | solution.py:350
  1.9 3.3 %collective-permute-start = (bf16[4,4,16,384]{3,2,1,0:T(8,128)(2,1)S(1)}, bf16[4,4,16,384]{3,2,1,0:T(8,128)(2,1)S(1)}, u32[]{:S(2)}, u32[]{:S(2)}) collective-permute-start(bf16[4,4,16,384]{3,2,1,0:T(8,128)(2,1)S(1)} %get-tuple-element.30), channel_id=1, source_target_pairs={{0,8},{8,0},{16,24},{24,16},{32,40},{40,32},{48,56},{56,48},{64,72... | collective-permute-start | bytes 589832 | tf_op jit(solution)/shard_map/ppermute | solution.py:42
  5.2 1.9 %pack_late.1.after_ref = bf16[32,16,384]{2,1,0:T(8,128)(2,1)} custom-call(bf16[256,512]{1,0:T(8,128)(2,1)} %refs_5_.2, bf16[256,512]{1,0:T(8,128)(2,1)} %refs_8_.1, bf16[32,16,128]{2,1,0:T(8,128)(2,1)S(1)} %get-tuple-element.28.rest_ref), custom_call_target="tpu_custom_call" | custom-call | tf_op jit(solution)/shard_map/pack_late/pallas_call | solution.py:358
  7.3 2.9 %collective-permute-start.2 = (bf16[2,4,16,384]{3,2,1,0:T(8,128)(2,1)S(1)}, bf16[2,4,16,384]{3,2,1,0:T(8,128)(2,1)S(1)}, u32[]{:S(2)}, u32[]{:S(2)}) collective-permute-start(bf16[2,4,16,384]{3,2,1,0:T(8,128)(2,1)S(1)} %get-tuple-element.32), channel_id=1, source_target_pairs={{0,128},{8,136},{16,144},{24,152},{32,160},{40,168},{48,176},{56,1... | collective-permute-start | bytes 294920 | tf_op jit(solution)/shard_map/ppermute | solution.py:42
  10.9 7.8 %all-to-all-start = ((bf16[32,16,384]{2,1,0:T(8,128)(2,1)}), bf16[32,16,384]{2,1,0:T(8,128)(2,1)S(1)}, u32[]{:S(2)}, u32[]{:S(2)}) async-start(bf16[32,16,384]{2,1,0:T(8,128)(2,1)} %pack_late.1.after_ref), calls=%async_computation | async-start | bytes 786432 | tf_op jit(solution)/shard_map/all_to_all | solution.py:310
  18.9 1.3 %collective-permute-start.4 = (bf16[4,2,16,384]{3,2,1,0:T(8,128)(2,1)S(1)}, bf16[4,2,16,384]{3,2,1,0:T(8,128)(2,1)S(1)}, u32[]{:S(2)}, u32[]{:S(2)}) collective-permute-start(bf16[4,2,16,384]{3,2,1,0:T(8,128)(2,1)S(1)} %get-tuple-element.35), channel_id=1, source_target_pairs={{0,16},{8,24},{16,32},{24,40},{32,48},{40,56},{48,0},{56,8},{64,80... | collective-permute-start | bytes 294920 | tf_op jit(solution)/shard_map/ppermute | solution.py:42
  20.1 2.4 %collective-permute-start.5 = (bf16[4,2,16,384]{3,2,1,0:T(8,128)(2,1)S(1)}, bf16[4,2,16,384]{3,2,1,0:T(8,128)(2,1)S(1)}, u32[]{:S(2)}, u32[]{:S(2)}) collective-permute-start(bf16[4,2,16,384]{3,2,1,0:T(8,128)(2,1)S(1)} %get-tuple-element.36), channel_id=1, source_target_pairs={{0,32},{8,40},{16,48},{24,56},{32,0},{40,8},{48,16},{56,24},{64,96... | collective-permute-start | bytes 294920 | tf_op jit(solution)/shard_map/ppermute | solution.py:42
  22.5 1.2 %collective-permute-start.6 = (bf16[4,2,16,384]{3,2,1,0:T(8,128)(2,1)S(1)}, bf16[4,2,16,384]{3,2,1,0:T(8,128)(2,1)S(1)}, u32[]{:S(2)}, u32[]{:S(2)}) collective-permute-start(bf16[4,2,16,384]{3,2,1,0:T(8,128)(2,1)S(1)} %get-tuple-element.37), channel_id=1, source_target_pairs={{0,48},{8,56},{16,0},{24,8},{32,16},{40,24},{48,32},{56,40},{64,11... | collective-permute-start | bytes 294920 | tf_op jit(solution)/shard_map/ppermute | solution.py:42
  23.7 3.7 %collective-permute-done.4.refs_1_ = bf16[4,2,16,384]{3,2,1,0:T(8,128)(2,1)S(1)} collective-permute-done((bf16[4,2,16,384]{3,2,1,0:T(8,128)(2,1)S(1)}, bf16[4,2,16,384]{3,2,1,0:T(8,128)(2,1)S(1)}, u32[]{:S(2)}, u32[]{:S(2)}) %collective-permute-start.4) | collective-permute-done | bytes 98336 | tf_op jit(solution)/shard_map/ppermute | solution.py:42
  27.4 3.1 %collective-permute-done.5.refs_2_ = bf16[4,2,16,384]{3,2,1,0:T(8,128)(2,1)S(1)} collective-permute-done((bf16[4,2,16,384]{3,2,1,0:T(8,128)(2,1)S(1)}, bf16[4,2,16,384]{3,2,1,0:T(8,128)(2,1)S(1)}, u32[]{:S(2)}, u32[]{:S(2)}) %collective-permute-start.5) | collective-permute-done | bytes 98336 | tf_op jit(solution)/shard_map/ppermute | solution.py:42
  31.7 2.0 %forward.1 = (bf16[4,4,16,384]{3,2,1,0:T(8,128)(2,1)S(1)}, bf16[4,4,16,384]{3,2,1,0:T(8,128)(2,1)S(1)}, bf16[32,16,128]{2,1,0:T(8,128)(2,1)S(1)}, f32[2,2,512,256]{3,2,1,0:T(8,128)S(1)}) custom-call(bf16[32,16,384]{2,1,0:T(8,128)(2,1)S(1)} %all-to-all-done.x_ref, f32[2,512,256]{2,1,0:T(8,128)S(1)} %get-tuple-element.38.taps_ref, ...), custom_call_target="tpu_custom_call" | custom-call | tf_op jit(solution)/shard_map/forward/pallas_call | solution.py:374
  33.7 0.7 %collective-permute-start.7 = (bf16[4,4,16,384]{3,2,1,0:T(8,128)(2,1)S(1)}, bf16[4,4,16,384]{3,2,1,0:T(8,128)(2,1)S(1)}, u32[]{:S(2)}, u32[]{:S(2)}) collective-permute-start(bf16[4,4,16,384]{3,2,1,0:T(8,128)(2,1)S(1)} %get-tuple-element.41), channel_id=1, source_target_pairs={{0,8},{8,0},{16,24},{24,16},{32,40},{40,32},{48,56},{56,48},{64,72... | collective-permute-start | bytes 589832 | tf_op jit(solution)/shard_map/ppermute | solution.py:42
  34.4 1.3 %backward.1.after_ref = bf16[32,16,384]{2,1,0:T(8,128)(2,1)} custom-call(f32[2,2,512,256]{3,2,1,0:T(8,128)S(1)} %get-tuple-element.42.spec_ref, bf16[32,16,128]{2,1,0:T(8,128)(2,1)S(1)} %get-tuple-element.43.rest_ref, bf16[32,64]{1,0:T(8,128)(2,1)S(1)} %copy-done.8, bf16[2,256,256]{2,1,0:T(8,128)(2,1)S(1)} %copy-done, f32[32,256]{1,0:T(8,128)S(1)} %copy-done.7, ...), custom_call_target="tpu_custom_call" | custom-call | tf_op jit(solution)/shard_map/backward/pallas_call | solution.py:385
  35.7 1.1 %collective-permute-start.8 = (bf16[2,4,16,384]{3,2,1,0:T(8,128)(2,1)S(1)}, bf16[2,4,16,384]{3,2,1,0:T(8,128)(2,1)S(1)}, u32[]{:S(2)}, u32[]{:S(2)}) collective-permute-start(bf16[2,4,16,384]{3,2,1,0:T(8,128)(2,1)S(1)} %get-tuple-element.44), channel_id=1, source_target_pairs={{0,64},{8,72},{16,80},{24,88},{32,96},{40,104},{48,112},{56,120},{... | collective-permute-start | bytes 294920 | tf_op jit(solution)/shard_map/ppermute | solution.py:42
  36.8 1.8 %collective-permute-start.9 = (bf16[2,4,16,384]{3,2,1,0:T(8,128)(2,1)S(1)}, bf16[2,4,16,384]{3,2,1,0:T(8,128)(2,1)S(1)}, u32[]{:S(2)}, u32[]{:S(2)}) collective-permute-start(bf16[2,4,16,384]{3,2,1,0:T(8,128)(2,1)S(1)} %get-tuple-element.45), channel_id=1, source_target_pairs={{0,128},{8,136},{16,144},{24,152},{32,160},{40,168},{48,176},{56,1... | collective-permute-start | bytes 294920 | tf_op jit(solution)/shard_map/ppermute | solution.py:42
  38.6 0.8 %collective-permute-start.10 = (bf16[2,4,16,384]{3,2,1,0:T(8,128)(2,1)S(1)}, bf16[2,4,16,384]{3,2,1,0:T(8,128)(2,1)S(1)}, u32[]{:S(2)}, u32[]{:S(2)}) collective-permute-start(bf16[2,4,16,384]{3,2,1,0:T(8,128)(2,1)S(1)} %get-tuple-element.46), channel_id=1, source_target_pairs={{0,192},{8,200},{16,208},{24,216},{32,224},{40,232},{48,240},{56,2... | collective-permute-start | bytes 294920 | tf_op jit(solution)/shard_map/ppermute | solution.py:42
  39.4 6.1 %all-to-all-start.1 = ((bf16[32,16,384]{2,1,0:T(8,128)(2,1)}), bf16[32,16,384]{2,1,0:T(8,128)(2,1)S(1)}, u32[]{:S(2)}, u32[]{:S(2)}) async-start(bf16[32,16,384]{2,1,0:T(8,128)(2,1)} %backward.1.after_ref), calls=%async_computation.1 | async-start | bytes 786432 | tf_op jit(solution)/shard_map/all_to_all | solution.py:310
  45.7 1.3 %collective-permute-start.11 = (bf16[4,2,16,384]{3,2,1,0:T(8,128)(2,1)S(1)}, bf16[4,2,16,384]{3,2,1,0:T(8,128)(2,1)S(1)}, u32[]{:S(2)}, u32[]{:S(2)}) collective-permute-start(bf16[4,2,16,384]{3,2,1,0:T(8,128)(2,1)S(1)} %get-tuple-element.48), channel_id=1, source_target_pairs={{0,16},{8,24},{16,32},{24,40},{32,48},{40,56},{48,0},{56,8},{64,80... | collective-permute-start | bytes 294920 | tf_op jit(solution)/shard_map/ppermute | solution.py:42
  46.9 2.4 %collective-permute-start.12 = (bf16[4,2,16,384]{3,2,1,0:T(8,128)(2,1)S(1)}, bf16[4,2,16,384]{3,2,1,0:T(8,128)(2,1)S(1)}, u32[]{:S(2)}, u32[]{:S(2)}) collective-permute-start(bf16[4,2,16,384]{3,2,1,0:T(8,128)(2,1)S(1)} %get-tuple-element.49), channel_id=1, source_target_pairs={{0,32},{8,40},{16,48},{24,56},{32,0},{40,8},{48,16},{56,24},{64,96... | collective-permute-start | bytes 294920 | tf_op jit(solution)/shard_map/ppermute | solution.py:42
  49.3 1.2 %collective-permute-start.13 = (bf16[4,2,16,384]{3,2,1,0:T(8,128)(2,1)S(1)}, bf16[4,2,16,384]{3,2,1,0:T(8,128)(2,1)S(1)}, u32[]{:S(2)}, u32[]{:S(2)}) collective-permute-start(bf16[4,2,16,384]{3,2,1,0:T(8,128)(2,1)S(1)} %get-tuple-element.50), channel_id=1, source_target_pairs={{0,48},{8,56},{16,0},{24,8},{32,16},{40,24},{48,32},{56,40},{64,11... | collective-permute-start | bytes 294920 | tf_op jit(solution)/shard_map/ppermute | solution.py:42
  50.5 3.4 %collective-permute-done.11.refs_1_ = bf16[4,2,16,384]{3,2,1,0:T(8,128)(2,1)S(1)} collective-permute-done((bf16[4,2,16,384]{3,2,1,0:T(8,128)(2,1)S(1)}, bf16[4,2,16,384]{3,2,1,0:T(8,128)(2,1)S(1)}, u32[]{:S(2)}, u32[]{:S(2)}) %collective-permute-start.11) | collective-permute-done | bytes 98336 | tf_op jit(solution)/shard_map/ppermute | solution.py:42
  53.9 3.3 %collective-permute-done.12.refs_2_ = bf16[4,2,16,384]{3,2,1,0:T(8,128)(2,1)S(1)} collective-permute-done((bf16[4,2,16,384]{3,2,1,0:T(8,128)(2,1)S(1)}, bf16[4,2,16,384]{3,2,1,0:T(8,128)(2,1)S(1)}, u32[]{:S(2)}, u32[]{:S(2)}) %collective-permute-start.12) | collective-permute-done | bytes 98336 | tf_op jit(solution)/shard_map/ppermute | solution.py:42
  57.2 1.2 %all-to-all-done.1.refs_4_ = bf16[32,16,384]{2,1,0:T(8,128)(2,1)S(1)} async-done(((bf16[32,16,384]{2,1,0:T(8,128)(2,1)}), bf16[32,16,384]{2,1,0:T(8,128)(2,1)S(1)}, u32[]{:S(2)}, u32[]{:S(2)}) %all-to-all-start.1) | async-done | bytes 393248 | tf_op jit(solution)/shard_map/all_to_all | solution.py:310
  58.5 1.3 %gate.1 = (bf16[256,512]{1,0:T(8,128)(2,1)}, bf16[256,512]{1,0:T(8,128)(2,1)}, bf16[256,512]{1,0:T(8,128)(2,1)}, bf16[256,512]{1,0:T(8,128)(2,1)}, bf16[256,512]{1,0:T(8,128)(2,1)}) custom-call(bf16[4,2,16,384]{3,2,1,0:T(8,128)(2,1)S(1)} %get-tuple-element.47.refs_0_, bf16[4,2,16,384]{3,2,1,0:T(8,128)(2,1)S(1)} %collective-permute-done.11.refs_1_, ...), custom_call_target="tpu_custom_call" | custom-call | tf_op jit(solution)/shard_map/gate/pallas_call | solution.py:399
  (40 shorter events, 2.1 us)
Async XLA Ops:
  1.9 5.3 %collective-permute-start = (bf16[4,4,16,384]{3,2,1,0:T(8,128)(2,1)S(1)}, bf16[4,4,16,384]{3,2,1,0:T(8,128)(2,1)S(1)}, u32[]{:S(2)}, u32[]{:S(2)}) collective-permute-start(bf16[4,4,16,384]{3,2,1,0:T(8,128)(2,1)S(1)} %get-tuple-element.30), channel_id=1, source_target_pairs={{0,8},{8,0},{16,24},{24,16},{32,40},{40,32},{48,56},{56,48},{64,72... | collective-permute-start | bytes 589832 | tf_op jit(solution)/shard_map/ppermute | solution.py:42
  7.2 11.5 %collective-permute-start.1 = (bf16[2,4,16,384]{3,2,1,0:T(8,128)(2,1)S(1)}, bf16[2,4,16,384]{3,2,1,0:T(8,128)(2,1)S(1)}, u32[]{:S(2)}, u32[]{:S(2)}) collective-permute-start(bf16[2,4,16,384]{3,2,1,0:T(8,128)(2,1)S(1)} %get-tuple-element.31), channel_id=1, source_target_pairs={{0,64},{8,72},{16,80},{24,88},{32,96},{40,104},{48,112},{56,120},{... | collective-permute-start | bytes 294920 | tf_op jit(solution)/shard_map/ppermute | solution.py:42
  7.3 11.4 %collective-permute-start.2 = (bf16[2,4,16,384]{3,2,1,0:T(8,128)(2,1)S(1)}, bf16[2,4,16,384]{3,2,1,0:T(8,128)(2,1)S(1)}, u32[]{:S(2)}, u32[]{:S(2)}) collective-permute-start(bf16[2,4,16,384]{3,2,1,0:T(8,128)(2,1)S(1)} %get-tuple-element.32), channel_id=1, source_target_pairs={{0,128},{8,136},{16,144},{24,152},{32,160},{40,168},{48,176},{56,1... | collective-permute-start | bytes 294920 | tf_op jit(solution)/shard_map/ppermute | solution.py:42
  10.2 8.6 %collective-permute-start.3 = (bf16[2,4,16,384]{3,2,1,0:T(8,128)(2,1)S(1)}, bf16[2,4,16,384]{3,2,1,0:T(8,128)(2,1)S(1)}, u32[]{:S(2)}, u32[]{:S(2)}) collective-permute-start(bf16[2,4,16,384]{3,2,1,0:T(8,128)(2,1)S(1)} %get-tuple-element.33), channel_id=1, source_target_pairs={{0,192},{8,200},{16,208},{24,216},{32,224},{40,232},{48,240},{56,2... | collective-permute-start | bytes 294920 | tf_op jit(solution)/shard_map/ppermute | solution.py:42
  10.9 20.8 %all-to-all-start = ((bf16[32,16,384]{2,1,0:T(8,128)(2,1)}), bf16[32,16,384]{2,1,0:T(8,128)(2,1)S(1)}, u32[]{:S(2)}, u32[]{:S(2)}) async-start(bf16[32,16,384]{2,1,0:T(8,128)(2,1)} %pack_late.1.after_ref), calls=%async_computation | async-start | bytes 786432 | tf_op jit(solution)/shard_map/all_to_all | solution.py:310
  18.7 11.8 %copy-start.5 = (bf16[2,256,256]{2,1,0:T(8,128)(2,1)S(1)}, bf16[2,256,256]{2,1,0:T(8,128)(2,1)}, u32[]{:S(2)}) copy-start(bf16[2,256,256]{2,1,0:T(8,128)(2,1)} %constant.13.clone.refs_5_.second_ref) | copy-start | bytes 786436
  18.7 11.8 %copy-start.6 = (f32[32,256]{1,0:T(8,128)S(1)}, f32[32,256]{1,0:T(8,128)}, u32[]{:S(2)}) copy-start(f32[32,256]{1,0:T(8,128)} %constant.15.clone.refs_7_.twi_ref) | copy-start | bytes 98308
  18.8 11.8 %copy-start.7 = (f32[32,256]{1,0:T(8,128)S(1)}, f32[32,256]{1,0:T(8,128)}, u32[]{:S(2)}) copy-start(f32[32,256]{1,0:T(8,128)} %constant.14.clone.refs_6_.twr_ref) | copy-start | bytes 98308
  18.9 8.6 %collective-permute-start.4 = (bf16[4,2,16,384]{3,2,1,0:T(8,128)(2,1)S(1)}, bf16[4,2,16,384]{3,2,1,0:T(8,128)(2,1)S(1)}, u32[]{:S(2)}, u32[]{:S(2)}) collective-permute-start(bf16[4,2,16,384]{3,2,1,0:T(8,128)(2,1)S(1)} %get-tuple-element.35), channel_id=1, source_target_pairs={{0,16},{8,24},{16,32},{24,40},{32,48},{40,56},{48,0},{56,8},{64,80... | collective-permute-start | bytes 294920 | tf_op jit(solution)/shard_map/ppermute | solution.py:42
  20.1 10.4 %collective-permute-start.5 = (bf16[4,2,16,384]{3,2,1,0:T(8,128)(2,1)S(1)}, bf16[4,2,16,384]{3,2,1,0:T(8,128)(2,1)S(1)}, u32[]{:S(2)}, u32[]{:S(2)}) collective-permute-start(bf16[4,2,16,384]{3,2,1,0:T(8,128)(2,1)S(1)} %get-tuple-element.36), channel_id=1, source_target_pairs={{0,32},{8,40},{16,48},{24,56},{32,0},{40,8},{48,16},{56,24},{64,96... | collective-permute-start | bytes 294920 | tf_op jit(solution)/shard_map/ppermute | solution.py:42
  22.5 8.0 %collective-permute-start.6 = (bf16[4,2,16,384]{3,2,1,0:T(8,128)(2,1)S(1)}, bf16[4,2,16,384]{3,2,1,0:T(8,128)(2,1)S(1)}, u32[]{:S(2)}, u32[]{:S(2)}) collective-permute-start(bf16[4,2,16,384]{3,2,1,0:T(8,128)(2,1)S(1)} %get-tuple-element.37), channel_id=1, source_target_pairs={{0,48},{8,56},{16,0},{24,8},{32,16},{40,24},{48,32},{56,40},{64,11... | collective-permute-start | bytes 294920 | tf_op jit(solution)/shard_map/ppermute | solution.py:42
  33.7 2.0 %collective-permute-start.7 = (bf16[4,4,16,384]{3,2,1,0:T(8,128)(2,1)S(1)}, bf16[4,4,16,384]{3,2,1,0:T(8,128)(2,1)S(1)}, u32[]{:S(2)}, u32[]{:S(2)}) collective-permute-start(bf16[4,4,16,384]{3,2,1,0:T(8,128)(2,1)S(1)} %get-tuple-element.41), channel_id=1, source_target_pairs={{0,8},{8,0},{16,24},{24,16},{32,40},{40,32},{48,56},{56,48},{64,72... | collective-permute-start | bytes 589832 | tf_op jit(solution)/shard_map/ppermute | solution.py:42
  35.7 9.8 %collective-permute-start.8 = (bf16[2,4,16,384]{3,2,1,0:T(8,128)(2,1)S(1)}, bf16[2,4,16,384]{3,2,1,0:T(8,128)(2,1)S(1)}, u32[]{:S(2)}, u32[]{:S(2)}) collective-permute-start(bf16[2,4,16,384]{3,2,1,0:T(8,128)(2,1)S(1)} %get-tuple-element.44), channel_id=1, source_target_pairs={{0,64},{8,72},{16,80},{24,88},{32,96},{40,104},{48,112},{56,120},{... | collective-permute-start | bytes 294920 | tf_op jit(solution)/shard_map/ppermute | solution.py:42
  36.8 8.8 %collective-permute-start.9 = (bf16[2,4,16,384]{3,2,1,0:T(8,128)(2,1)S(1)}, bf16[2,4,16,384]{3,2,1,0:T(8,128)(2,1)S(1)}, u32[]{:S(2)}, u32[]{:S(2)}) collective-permute-start(bf16[2,4,16,384]{3,2,1,0:T(8,128)(2,1)S(1)} %get-tuple-element.45), channel_id=1, source_target_pairs={{0,128},{8,136},{16,144},{24,152},{32,160},{40,168},{48,176},{56,1... | collective-permute-start | bytes 294920 | tf_op jit(solution)/shard_map/ppermute | solution.py:42
  38.6 7.0 %collective-permute-start.10 = (bf16[2,4,16,384]{3,2,1,0:T(8,128)(2,1)S(1)}, bf16[2,4,16,384]{3,2,1,0:T(8,128)(2,1)S(1)}, u32[]{:S(2)}, u32[]{:S(2)}) collective-permute-start(bf16[2,4,16,384]{3,2,1,0:T(8,128)(2,1)S(1)} %get-tuple-element.46), channel_id=1, source_target_pairs={{0,192},{8,200},{16,208},{24,216},{32,224},{40,232},{48,240},{56,2... | collective-permute-start | bytes 294920 | tf_op jit(solution)/shard_map/ppermute | solution.py:42
  39.4 19.1 %all-to-all-start.1 = ((bf16[32,16,384]{2,1,0:T(8,128)(2,1)}), bf16[32,16,384]{2,1,0:T(8,128)(2,1)S(1)}, u32[]{:S(2)}, u32[]{:S(2)}) async-start(bf16[32,16,384]{2,1,0:T(8,128)(2,1)} %backward.1.after_ref), calls=%async_computation.1 | async-start | bytes 786432 | tf_op jit(solution)/shard_map/all_to_all | solution.py:310
  45.5 12.9 %copy-start.1 = (bf16[256,512]{1,0:T(8,128)(2,1)S(1)}, bf16[256,512]{1,0:T(8,128)(2,1)}, u32[]{:S(2)}) copy-start(bf16[256,512]{1,0:T(8,128)(2,1)} %refs_6_.2) | copy-start | bytes 786436
  45.5 12.9 %copy-start.2 = (bf16[256,512]{1,0:T(8,128)(2,1)S(1)}, bf16[256,512]{1,0:T(8,128)(2,1)}, u32[]{:S(2)}) copy-start(bf16[256,512]{1,0:T(8,128)(2,1)} %refs_7_.2) | copy-start | bytes 786436
  45.5 12.9 %copy-start.3 = (bf16[256,512]{1,0:T(8,128)(2,1)S(1)}, bf16[256,512]{1,0:T(8,128)(2,1)}, u32[]{:S(2)}) copy-start(bf16[256,512]{1,0:T(8,128)(2,1)} %refs_5_.2) | copy-start | bytes 786436
  45.6 12.9 %copy-start.4 = (bf16[256,512]{1,0:T(8,128)(2,1)S(1)}, bf16[256,512]{1,0:T(8,128)(2,1)}, u32[]{:S(2)}) copy-start(bf16[256,512]{1,0:T(8,128)(2,1)} %refs_8_.1) | copy-start | bytes 786436
  45.6 12.9 %copy-start.10 = (f32[512]{0:T(512)S(1)}, f32[512]{0:T(512)}, u32[]{:S(2)}) copy-start(f32[512]{0:T(512)} %param.16) | copy-start | bytes 6148
  45.7 8.3 %collective-permute-start.11 = (bf16[4,2,16,384]{3,2,1,0:T(8,128)(2,1)S(1)}, bf16[4,2,16,384]{3,2,1,0:T(8,128)(2,1)S(1)}, u32[]{:S(2)}, u32[]{:S(2)}) collective-permute-start(bf16[4,2,16,384]{3,2,1,0:T(8,128)(2,1)S(1)} %get-tuple-element.48), channel_id=1, source_target_pairs={{0,16},{8,24},{16,32},{24,40},{32,48},{40,56},{48,0},{56,8},{64,80... | collective-permute-start | bytes 294920 | tf_op jit(solution)/shard_map/ppermute | solution.py:42
  46.9 10.3 %collective-permute-start.12 = (bf16[4,2,16,384]{3,2,1,0:T(8,128)(2,1)S(1)}, bf16[4,2,16,384]{3,2,1,0:T(8,128)(2,1)S(1)}, u32[]{:S(2)}, u32[]{:S(2)}) collective-permute-start(bf16[4,2,16,384]{3,2,1,0:T(8,128)(2,1)S(1)} %get-tuple-element.49), channel_id=1, source_target_pairs={{0,32},{8,40},{16,48},{24,56},{32,0},{40,8},{48,16},{56,24},{64,96... | collective-permute-start | bytes 294920 | tf_op jit(solution)/shard_map/ppermute | solution.py:42
  49.3 7.9 %collective-permute-start.13 = (bf16[4,2,16,384]{3,2,1,0:T(8,128)(2,1)S(1)}, bf16[4,2,16,384]{3,2,1,0:T(8,128)(2,1)S(1)}, u32[]{:S(2)}, u32[]{:S(2)}) collective-permute-start(bf16[4,2,16,384]{3,2,1,0:T(8,128)(2,1)S(1)} %get-tuple-element.50), channel_id=1, source_target_pairs={{0,48},{8,56},{16,0},{24,8},{32,16},{40,24},{48,32},{56,40},{64,11... | collective-permute-start | bytes 294920 | tf_op jit(solution)/shard_map/ppermute | solution.py:42
  (3 other events, 14.0 us)

commit v5 on v4

--- a/solution.py
+++ b/solution.py
@@ -28,11 +28,11 @@
 def block_of(here, dz, dx, dc):
     z, x, c = place(here)
     z = z ^ dz
-    return ((z ^ (1 - z // 2)) * 4 + (x + dx) % 4) * 2 + (c ^ dc)
+    return (((x + dx) % 4) * 2 + (c ^ dc)) * 4 + (z ^ (1 - z // 2))
 
 
 def device_order(groups):
-    return [block_of(here, 0, 0, 0) for here in range(groups)]
+    return sorted(range(groups), key=lambda here: block_of(here, 0, 0, 0))
 
 
 def send(block, dz, dx, dc):

time: 60.1 us -> 59.2 us (0.985)
  waiting for transfers between devices: 15.3 us -> 14.2 us
    all_to_all x2, waiting for transfers between devices: 1.72 us -> 0.01 us  [swap(): lax.all_to_all(block, 'context', split_axis=0, concat_axis=0, tiled=True,...]
    ppermute x14, waiting for transfers between devices: 13.6 us -> 14.2 us  [send(): return lax.ppermute(block, 'context', moves)]
  transfers between devices with their start and end apart: 16 -> 16, of which waited for: 6 -> 5; matrix products, arithmetic and copies ran while one was open for 0% -> 0% of each run, Pallas kernels for 7% -> 7%
where the time goes in v5:
time: 59.2 us; the launch traced here: 58.9 us
  starting transfers between devices  34.8 us (59%)
  waiting for transfers between devices  14.2 us (24%)
  Pallas kernels  8.57 us (14%)
  between operations  0.93 us (2%)
    ppermute x14, starting transfers between devices, send(): return lax.ppermute(block, 'context', moves)  20.9 us
    ppermute x14, waiting for transfers between devices, send(): return lax.ppermute(block, 'context', moves)  14.2 us
    all_to_all x2, starting transfers between devices, swap(): lax.all_to_all(block, 'context', split_axis=0, concat_axis=0, tiled=True,...  13.9 us
    pallas_call x1, Pallas kernels, local(): call(functools.partial(forward_kernel, scale), 'forward', [shape(4, 4, *b...  2.02 us
    pallas_call x1, Pallas kernels, local(): call(pack_late_kernel, 'pack_late', shape(groups, *block), [pltpu.VMEM((2...  1.94 us
    pallas_call x1, Pallas kernels, local(): call(functools.partial(backward_kernel, scale), 'backward', shape(groups,...  1.32 us
    pallas_call x1, Pallas kernels, local(): call(gate_kernel, 'gate', [whole] * 5, [pltpu.VMEM((groups, *block), BF16...  1.28 us
    pallas_call x1, Pallas kernels, local(): call(pack_early_kernel, 'pack_early', [pltpu.VMEM((4, 4, *block), BF16)]...  1.28 us
  transfers between devices with their start and end apart: 16, of which 5 were waited for; matrix products, arithmetic and copies ran while one was open for 0% of the time, Pallas kernels for 7%

profile of v5, /device:TPU:1, one launch (start us, length us, event | category | flops | bytes accessed | tf_op | source)
XLA Modules:
  0.0 58.9 jit_solution(3706219416127969175)
XLA Ops:
  0.6 1.3 %pack_early.1 = (bf16[4,4,16,384]{3,2,1,0:T(8,128)(2,1)S(1)}, bf16[4,4,16,384]{3,2,1,0:T(8,128)(2,1)S(1)}, bf16[32,16,128]{2,1,0:T(8,128)(2,1)S(1)}) custom-call(bf16[256,512]{1,0:T(8,128)(2,1)} %f_hbm.1, bf16[256,512]{1,0:T(8,128)(2,1)} %refs_6_.2, bf16[256,512]{1,0:T(8,128)(2,1)} %refs_7_.2), custom_call_target="tpu_custom_call" | custom-call | tf_op jit(solution)/shard_map/pack_early/pallas_call | solution.py:350
  1.9 3.3 %collective-permute-start = (bf16[4,4,16,384]{3,2,1,0:T(8,128)(2,1)S(1)}, bf16[4,4,16,384]{3,2,1,0:T(8,128)(2,1)S(1)}, u32[]{:S(2)}, u32[]{:S(2)}) collective-permute-start(bf16[4,4,16,384]{3,2,1,0:T(8,128)(2,1)S(1)} %get-tuple-element.30), channel_id=1, source_target_pairs={{0,8},{8,0},{16,24},{24,16},{32,40},{40,32},{48,56},{56,48},{64,72... | collective-permute-start | bytes 589832 | tf_op jit(solution)/shard_map/ppermute | solution.py:42
  5.2 1.9 %pack_late.1.after_ref = bf16[32,16,384]{2,1,0:T(8,128)(2,1)} custom-call(bf16[256,512]{1,0:T(8,128)(2,1)} %refs_5_.2, bf16[256,512]{1,0:T(8,128)(2,1)} %refs_8_.1, bf16[32,16,128]{2,1,0:T(8,128)(2,1)S(1)} %get-tuple-element.28.rest_ref), custom_call_target="tpu_custom_call" | custom-call | tf_op jit(solution)/shard_map/pack_late/pallas_call | solution.py:358
  7.3 2.9 %collective-permute-start.2 = (bf16[2,4,16,384]{3,2,1,0:T(8,128)(2,1)S(1)}, bf16[2,4,16,384]{3,2,1,0:T(8,128)(2,1)S(1)}, u32[]{:S(2)}, u32[]{:S(2)}) collective-permute-start(bf16[2,4,16,384]{3,2,1,0:T(8,128)(2,1)S(1)} %get-tuple-element.32), channel_id=1, source_target_pairs={{0,128},{8,136},{16,144},{24,152},{32,160},{40,168},{48,176},{56,1... | collective-permute-start | bytes 294920 | tf_op jit(solution)/shard_map/ppermute | solution.py:42
  10.2 0.7 %collective-permute-start.3 = (bf16[2,4,16,384]{3,2,1,0:T(8,128)(2,1)S(1)}, bf16[2,4,16,384]{3,2,1,0:T(8,128)(2,1)S(1)}, u32[]{:S(2)}, u32[]{:S(2)}) collective-permute-start(bf16[2,4,16,384]{3,2,1,0:T(8,128)(2,1)S(1)} %get-tuple-element.33), channel_id=1, source_target_pairs={{0,192},{8,200},{16,208},{24,216},{32,224},{40,232},{48,240},{56,2... | collective-permute-start | bytes 294920 | tf_op jit(solution)/shard_map/ppermute | solution.py:42
  10.9 7.8 %all-to-all-start = ((bf16[32,16,384]{2,1,0:T(8,128)(2,1)}), bf16[32,16,384]{2,1,0:T(8,128)(2,1)S(1)}, u32[]{:S(2)}, u32[]{:S(2)}) async-start(bf16[32,16,384]{2,1,0:T(8,128)(2,1)} %pack_late.1.after_ref), calls=%async_computation | async-start | bytes 786432 | tf_op jit(solution)/shard_map/all_to_all | solution.py:310
  18.9 1.3 %collective-permute-start.4 = (bf16[4,2,16,384]{3,2,1,0:T(8,128)(2,1)S(1)}, bf16[4,2,16,384]{3,2,1,0:T(8,128)(2,1)S(1)}, u32[]{:S(2)}, u32[]{:S(2)}) collective-permute-start(bf16[4,2,16,384]{3,2,1,0:T(8,128)(2,1)S(1)} %get-tuple-element.35), channel_id=1, source_target_pairs={{0,16},{8,24},{16,32},{24,40},{32,48},{40,56},{48,0},{56,8},{64,80... | collective-permute-start | bytes 294920 | tf_op jit(solution)/shard_map/ppermute | solution.py:42
  20.1 2.4 %collective-permute-start.5 = (bf16[4,2,16,384]{3,2,1,0:T(8,128)(2,1)S(1)}, bf16[4,2,16,384]{3,2,1,0:T(8,128)(2,1)S(1)}, u32[]{:S(2)}, u32[]{:S(2)}) collective-permute-start(bf16[4,2,16,384]{3,2,1,0:T(8,128)(2,1)S(1)} %get-tuple-element.36), channel_id=1, source_target_pairs={{0,32},{8,40},{16,48},{24,56},{32,0},{40,8},{48,16},{56,24},{64,96... | collective-permute-start | bytes 294920 | tf_op jit(solution)/shard_map/ppermute | solution.py:42
  22.6 1.1 %collective-permute-start.6 = (bf16[4,2,16,384]{3,2,1,0:T(8,128)(2,1)S(1)}, bf16[4,2,16,384]{3,2,1,0:T(8,128)(2,1)S(1)}, u32[]{:S(2)}, u32[]{:S(2)}) collective-permute-start(bf16[4,2,16,384]{3,2,1,0:T(8,128)(2,1)S(1)} %get-tuple-element.37), channel_id=1, source_target_pairs={{0,48},{8,56},{16,0},{24,8},{32,16},{40,24},{48,32},{56,40},{64,11... | collective-permute-start | bytes 294920 | tf_op jit(solution)/shard_map/ppermute | solution.py:42
  23.7 3.9 %collective-permute-done.4.refs_1_ = bf16[4,2,16,384]{3,2,1,0:T(8,128)(2,1)S(1)} collective-permute-done((bf16[4,2,16,384]{3,2,1,0:T(8,128)(2,1)S(1)}, bf16[4,2,16,384]{3,2,1,0:T(8,128)(2,1)S(1)}, u32[]{:S(2)}, u32[]{:S(2)}) %collective-permute-start.4) | collective-permute-done | bytes 98336 | tf_op jit(solution)/shard_map/ppermute | solution.py:42
  27.6 3.0 %collective-permute-done.5.refs_2_ = bf16[4,2,16,384]{3,2,1,0:T(8,128)(2,1)S(1)} collective-permute-done((bf16[4,2,16,384]{3,2,1,0:T(8,128)(2,1)S(1)}, bf16[4,2,16,384]{3,2,1,0:T(8,128)(2,1)S(1)}, u32[]{:S(2)}, u32[]{:S(2)}) %collective-permute-start.5) | collective-permute-done | bytes 98336 | tf_op jit(solution)/shard_map/ppermute | solution.py:42
  30.7 0.6 %filter_spectrum.1 = (f32[2,512,256]{2,1,0:T(8,128)S(1)}, bf16[32,16,128]{2,1,0:T(8,128)(2,1)S(1)}) custom-call(bf16[4,2,16,384]{3,2,1,0:T(8,128)(2,1)S(1)} %get-tuple-element.34.refs_0_, bf16[4,2,16,384]{3,2,1,0:T(8,128)(2,1)S(1)} %collective-permute-done.4.refs_1_, bf16[4,2,16,384]{3,2,1,0:T(8,128)(2,1)S(1)} %collective-permute-done.5.refs_2_, ...), custom_call_target="tpu_custom_call" | custom-call | flops 5000000000 | bytes 5000000000 | tf_op jit(solution)/shard_map/filter_spectrum/pallas_call | solution.py:366
  31.6 2.0 %forward.1 = (bf16[4,4,16,384]{3,2,1,0:T(8,128)(2,1)S(1)}, bf16[4,4,16,384]{3,2,1,0:T(8,128)(2,1)S(1)}, bf16[32,16,128]{2,1,0:T(8,128)(2,1)S(1)}, f32[2,2,512,256]{3,2,1,0:T(8,128)S(1)}) custom-call(bf16[32,16,384]{2,1,0:T(8,128)(2,1)S(1)} %all-to-all-done.x_ref, f32[2,512,256]{2,1,0:T(8,128)S(1)} %get-tuple-element.38.taps_ref, ...), custom_call_target="tpu_custom_call" | custom-call | tf_op jit(solution)/shard_map/forward/pallas_call | solution.py:374
  33.7 0.9 %collective-permute-start.7 = (bf16[4,4,16,384]{3,2,1,0:T(8,128)(2,1)S(1)}, bf16[4,4,16,384]{3,2,1,0:T(8,128)(2,1)S(1)}, u32[]{:S(2)}, u32[]{:S(2)}) collective-permute-start(bf16[4,4,16,384]{3,2,1,0:T(8,128)(2,1)S(1)} %get-tuple-element.41), channel_id=1, source_target_pairs={{0,8},{8,0},{16,24},{24,16},{32,40},{40,32},{48,56},{56,48},{64,72... | collective-permute-start | bytes 589832 | tf_op jit(solution)/shard_map/ppermute | solution.py:42
  34.6 1.3 %backward.1.after_ref = bf16[32,16,384]{2,1,0:T(8,128)(2,1)} custom-call(f32[2,2,512,256]{3,2,1,0:T(8,128)S(1)} %get-tuple-element.42.spec_ref, bf16[32,16,128]{2,1,0:T(8,128)(2,1)S(1)} %get-tuple-element.43.rest_ref, bf16[32,64]{1,0:T(8,128)(2,1)S(1)} %copy-done.8, bf16[2,256,256]{2,1,0:T(8,128)(2,1)S(1)} %copy-done, f32[32,256]{1,0:T(8,128)S(1)} %copy-done.7, ...), custom_call_target="tpu_custom_call" | custom-call | tf_op jit(solution)/shard_map/backward/pallas_call | solution.py:385
  36.5 2.0 %collective-permute-start.9 = (bf16[2,4,16,384]{3,2,1,0:T(8,128)(2,1)S(1)}, bf16[2,4,16,384]{3,2,1,0:T(8,128)(2,1)S(1)}, u32[]{:S(2)}, u32[]{:S(2)}) collective-permute-start(bf16[2,4,16,384]{3,2,1,0:T(8,128)(2,1)S(1)} %get-tuple-element.45), channel_id=1, source_target_pairs={{0,128},{8,136},{16,144},{24,152},{32,160},{40,168},{48,176},{56,1... | collective-permute-start | bytes 294920 | tf_op jit(solution)/shard_map/ppermute | solution.py:42
  38.5 1.1 %collective-permute-start.10 = (bf16[2,4,16,384]{3,2,1,0:T(8,128)(2,1)S(1)}, bf16[2,4,16,384]{3,2,1,0:T(8,128)(2,1)S(1)}, u32[]{:S(2)}, u32[]{:S(2)}) collective-permute-start(bf16[2,4,16,384]{3,2,1,0:T(8,128)(2,1)S(1)} %get-tuple-element.46), channel_id=1, source_target_pairs={{0,192},{8,200},{16,208},{24,216},{32,224},{40,232},{48,240},{56,2... | collective-permute-start | bytes 294920 | tf_op jit(solution)/shard_map/ppermute | solution.py:42
  39.6 6.0 %all-to-all-start.1 = ((bf16[32,16,384]{2,1,0:T(8,128)(2,1)}), bf16[32,16,384]{2,1,0:T(8,128)(2,1)S(1)}, u32[]{:S(2)}, u32[]{:S(2)}) async-start(bf16[32,16,384]{2,1,0:T(8,128)(2,1)} %backward.1.after_ref), calls=%async_computation.1 | async-start | bytes 786432 | tf_op jit(solution)/shard_map/all_to_all | solution.py:310
  46.0 1.0 %collective-permute-start.11 = (bf16[4,2,16,384]{3,2,1,0:T(8,128)(2,1)S(1)}, bf16[4,2,16,384]{3,2,1,0:T(8,128)(2,1)S(1)}, u32[]{:S(2)}, u32[]{:S(2)}) collective-permute-start(bf16[4,2,16,384]{3,2,1,0:T(8,128)(2,1)S(1)} %get-tuple-element.48), channel_id=1, source_target_pairs={{0,16},{8,24},{16,32},{24,40},{32,48},{40,56},{48,0},{56,8},{64,80... | collective-permute-start | bytes 294920 | tf_op jit(solution)/shard_map/ppermute | solution.py:42
  47.0 2.4 %collective-permute-start.12 = (bf16[4,2,16,384]{3,2,1,0:T(8,128)(2,1)S(1)}, bf16[4,2,16,384]{3,2,1,0:T(8,128)(2,1)S(1)}, u32[]{:S(2)}, u32[]{:S(2)}) collective-permute-start(bf16[4,2,16,384]{3,2,1,0:T(8,128)(2,1)S(1)} %get-tuple-element.49), channel_id=1, source_target_pairs={{0,32},{8,40},{16,48},{24,56},{32,0},{40,8},{48,16},{56,24},{64,96... | collective-permute-start | bytes 294920 | tf_op jit(solution)/shard_map/ppermute | solution.py:42
  49.5 1.1 %collective-permute-start.13 = (bf16[4,2,16,384]{3,2,1,0:T(8,128)(2,1)S(1)}, bf16[4,2,16,384]{3,2,1,0:T(8,128)(2,1)S(1)}, u32[]{:S(2)}, u32[]{:S(2)}) collective-permute-start(bf16[4,2,16,384]{3,2,1,0:T(8,128)(2,1)S(1)} %get-tuple-element.50), channel_id=1, source_target_pairs={{0,48},{8,56},{16,0},{24,8},{32,16},{40,24},{48,32},{56,40},{64,11... | collective-permute-start | bytes 294920 | tf_op jit(solution)/shard_map/ppermute | solution.py:42
  50.6 3.7 %collective-permute-done.11.refs_1_ = bf16[4,2,16,384]{3,2,1,0:T(8,128)(2,1)S(1)} collective-permute-done((bf16[4,2,16,384]{3,2,1,0:T(8,128)(2,1)S(1)}, bf16[4,2,16,384]{3,2,1,0:T(8,128)(2,1)S(1)}, u32[]{:S(2)}, u32[]{:S(2)}) %collective-permute-start.11) | collective-permute-done | bytes 98336 | tf_op jit(solution)/shard_map/ppermute | solution.py:42
  54.3 3.3 %collective-permute-done.12.refs_2_ = bf16[4,2,16,384]{3,2,1,0:T(8,128)(2,1)S(1)} collective-permute-done((bf16[4,2,16,384]{3,2,1,0:T(8,128)(2,1)S(1)}, bf16[4,2,16,384]{3,2,1,0:T(8,128)(2,1)S(1)}, u32[]{:S(2)}, u32[]{:S(2)}) %collective-permute-start.12) | collective-permute-done | bytes 98336 | tf_op jit(solution)/shard_map/ppermute | solution.py:42
  57.6 1.3 %gate.1 = (bf16[256,512]{1,0:T(8,128)(2,1)}, bf16[256,512]{1,0:T(8,128)(2,1)}, bf16[256,512]{1,0:T(8,128)(2,1)}, bf16[256,512]{1,0:T(8,128)(2,1)}, bf16[256,512]{1,0:T(8,128)(2,1)}) custom-call(bf16[4,2,16,384]{3,2,1,0:T(8,128)(2,1)S(1)} %get-tuple-element.47.refs_0_, bf16[4,2,16,384]{3,2,1,0:T(8,128)(2,1)S(1)} %collective-permute-done.11.refs_1_, ...), custom_call_target="tpu_custom_call" | custom-call | tf_op jit(solution)/shard_map/gate/pallas_call | solution.py:399
  (40 shorter events, 1.5 us)
Async XLA Ops:
  1.9 5.3 %collective-permute-start = (bf16[4,4,16,384]{3,2,1,0:T(8,128)(2,1)S(1)}, bf16[4,4,16,384]{3,2,1,0:T(8,128)(2,1)S(1)}, u32[]{:S(2)}, u32[]{:S(2)}) collective-permute-start(bf16[4,4,16,384]{3,2,1,0:T(8,128)(2,1)S(1)} %get-tuple-element.30), channel_id=1, source_target_pairs={{0,8},{8,0},{16,24},{24,16},{32,40},{40,32},{48,56},{56,48},{64,72... | collective-permute-start | bytes 589832 | tf_op jit(solution)/shard_map/ppermute | solution.py:42
  7.2 11.5 %collective-permute-start.1 = (bf16[2,4,16,384]{3,2,1,0:T(8,128)(2,1)S(1)}, bf16[2,4,16,384]{3,2,1,0:T(8,128)(2,1)S(1)}, u32[]{:S(2)}, u32[]{:S(2)}) collective-permute-start(bf16[2,4,16,384]{3,2,1,0:T(8,128)(2,1)S(1)} %get-tuple-element.31), channel_id=1, source_target_pairs={{0,64},{8,72},{16,80},{24,88},{32,96},{40,104},{48,112},{56,120},{... | collective-permute-start | bytes 294920 | tf_op jit(solution)/shard_map/ppermute | solution.py:42
  7.3 11.4 %collective-permute-start.2 = (bf16[2,4,16,384]{3,2,1,0:T(8,128)(2,1)S(1)}, bf16[2,4,16,384]{3,2,1,0:T(8,128)(2,1)S(1)}, u32[]{:S(2)}, u32[]{:S(2)}) collective-permute-start(bf16[2,4,16,384]{3,2,1,0:T(8,128)(2,1)S(1)} %get-tuple-element.32), channel_id=1, source_target_pairs={{0,128},{8,136},{16,144},{24,152},{32,160},{40,168},{48,176},{56,1... | collective-permute-start | bytes 294920 | tf_op jit(solution)/shard_map/ppermute | solution.py:42
  10.2 8.6 %collective-permute-start.3 = (bf16[2,4,16,384]{3,2,1,0:T(8,128)(2,1)S(1)}, bf16[2,4,16,384]{3,2,1,0:T(8,128)(2,1)S(1)}, u32[]{:S(2)}, u32[]{:S(2)}) collective-permute-start(bf16[2,4,16,384]{3,2,1,0:T(8,128)(2,1)S(1)} %get-tuple-element.33), channel_id=1, source_target_pairs={{0,192},{8,200},{16,208},{24,216},{32,224},{40,232},{48,240},{56,2... | collective-permute-start | bytes 294920 | tf_op jit(solution)/shard_map/ppermute | solution.py:42
  10.9 20.4 %all-to-all-start = ((bf16[32,16,384]{2,1,0:T(8,128)(2,1)}), bf16[32,16,384]{2,1,0:T(8,128)(2,1)S(1)}, u32[]{:S(2)}, u32[]{:S(2)}) async-start(bf16[32,16,384]{2,1,0:T(8,128)(2,1)} %pack_late.1.after_ref), calls=%async_computation | async-start | bytes 786432 | tf_op jit(solution)/shard_map/all_to_all | solution.py:310
  18.7 11.9 %copy-start.5 = (bf16[2,256,256]{2,1,0:T(8,128)(2,1)S(1)}, bf16[2,256,256]{2,1,0:T(8,128)(2,1)}, u32[]{:S(2)}) copy-start(bf16[2,256,256]{2,1,0:T(8,128)(2,1)} %constant.13.clone.refs_5_.second_ref) | copy-start | bytes 786436
  18.7 11.9 %copy-start.6 = (f32[32,256]{1,0:T(8,128)S(1)}, f32[32,256]{1,0:T(8,128)}, u32[]{:S(2)}) copy-start(f32[32,256]{1,0:T(8,128)} %constant.15.clone.refs_7_.twi_ref) | copy-start | bytes 98308
  18.7 11.9 %copy-start.7 = (f32[32,256]{1,0:T(8,128)S(1)}, f32[32,256]{1,0:T(8,128)}, u32[]{:S(2)}) copy-start(f32[32,256]{1,0:T(8,128)} %constant.14.clone.refs_6_.twr_ref) | copy-start | bytes 98308
  18.9 8.8 %collective-permute-start.4 = (bf16[4,2,16,384]{3,2,1,0:T(8,128)(2,1)S(1)}, bf16[4,2,16,384]{3,2,1,0:T(8,128)(2,1)S(1)}, u32[]{:S(2)}, u32[]{:S(2)}) collective-permute-start(bf16[4,2,16,384]{3,2,1,0:T(8,128)(2,1)S(1)} %get-tuple-element.35), channel_id=1, source_target_pairs={{0,16},{8,24},{16,32},{24,40},{32,48},{40,56},{48,0},{56,8},{64,80... | collective-permute-start | bytes 294920 | tf_op jit(solution)/shard_map/ppermute | solution.py:42
  20.1 10.5 %collective-permute-start.5 = (bf16[4,2,16,384]{3,2,1,0:T(8,128)(2,1)S(1)}, bf16[4,2,16,384]{3,2,1,0:T(8,128)(2,1)S(1)}, u32[]{:S(2)}, u32[]{:S(2)}) collective-permute-start(bf16[4,2,16,384]{3,2,1,0:T(8,128)(2,1)S(1)} %get-tuple-element.36), channel_id=1, source_target_pairs={{0,32},{8,40},{16,48},{24,56},{32,0},{40,8},{48,16},{56,24},{64,96... | collective-permute-start | bytes 294920 | tf_op jit(solution)/shard_map/ppermute | solution.py:42
  22.6 8.1 %collective-permute-start.6 = (bf16[4,2,16,384]{3,2,1,0:T(8,128)(2,1)S(1)}, bf16[4,2,16,384]{3,2,1,0:T(8,128)(2,1)S(1)}, u32[]{:S(2)}, u32[]{:S(2)}) collective-permute-start(bf16[4,2,16,384]{3,2,1,0:T(8,128)(2,1)S(1)} %get-tuple-element.37), channel_id=1, source_target_pairs={{0,48},{8,56},{16,0},{24,8},{32,16},{40,24},{48,32},{56,40},{64,11... | collective-permute-start | bytes 294920 | tf_op jit(solution)/shard_map/ppermute | solution.py:42
  33.7 2.2 %collective-permute-start.7 = (bf16[4,4,16,384]{3,2,1,0:T(8,128)(2,1)S(1)}, bf16[4,4,16,384]{3,2,1,0:T(8,128)(2,1)S(1)}, u32[]{:S(2)}, u32[]{:S(2)}) collective-permute-start(bf16[4,4,16,384]{3,2,1,0:T(8,128)(2,1)S(1)} %get-tuple-element.41), channel_id=1, source_target_pairs={{0,8},{8,0},{16,24},{24,16},{32,40},{40,32},{48,56},{56,48},{64,72... | collective-permute-start | bytes 589832 | tf_op jit(solution)/shard_map/ppermute | solution.py:42
  35.9 9.7 %collective-permute-start.8 = (bf16[2,4,16,384]{3,2,1,0:T(8,128)(2,1)S(1)}, bf16[2,4,16,384]{3,2,1,0:T(8,128)(2,1)S(1)}, u32[]{:S(2)}, u32[]{:S(2)}) collective-permute-start(bf16[2,4,16,384]{3,2,1,0:T(8,128)(2,1)S(1)} %get-tuple-element.44), channel_id=1, source_target_pairs={{0,64},{8,72},{16,80},{24,88},{32,96},{40,104},{48,112},{56,120},{... | collective-permute-start | bytes 294920 | tf_op jit(solution)/shard_map/ppermute | solution.py:42
  36.5 9.2 %collective-permute-start.9 = (bf16[2,4,16,384]{3,2,1,0:T(8,128)(2,1)S(1)}, bf16[2,4,16,384]{3,2,1,0:T(8,128)(2,1)S(1)}, u32[]{:S(2)}, u32[]{:S(2)}) collective-permute-start(bf16[2,4,16,384]{3,2,1,0:T(8,128)(2,1)S(1)} %get-tuple-element.45), channel_id=1, source_target_pairs={{0,128},{8,136},{16,144},{24,152},{32,160},{40,168},{48,176},{56,1... | collective-permute-start | bytes 294920 | tf_op jit(solution)/shard_map/ppermute | solution.py:42
  38.5 7.4 %collective-permute-start.10 = (bf16[2,4,16,384]{3,2,1,0:T(8,128)(2,1)S(1)}, bf16[2,4,16,384]{3,2,1,0:T(8,128)(2,1)S(1)}, u32[]{:S(2)}, u32[]{:S(2)}) collective-permute-start(bf16[2,4,16,384]{3,2,1,0:T(8,128)(2,1)S(1)} %get-tuple-element.46), channel_id=1, source_target_pairs={{0,192},{8,200},{16,208},{24,216},{32,224},{40,232},{48,240},{56,2... | collective-permute-start | bytes 294920 | tf_op jit(solution)/shard_map/ppermute | solution.py:42
  39.6 18.0 %all-to-all-start.1 = ((bf16[32,16,384]{2,1,0:T(8,128)(2,1)}), bf16[32,16,384]{2,1,0:T(8,128)(2,1)S(1)}, u32[]{:S(2)}, u32[]{:S(2)}) async-start(bf16[32,16,384]{2,1,0:T(8,128)(2,1)} %backward.1.after_ref), calls=%async_computation.1 | async-start | bytes 786432 | tf_op jit(solution)/shard_map/all_to_all | solution.py:310
  45.6 11.9 %copy-start.1 = (bf16[256,512]{1,0:T(8,128)(2,1)S(1)}, bf16[256,512]{1,0:T(8,128)(2,1)}, u32[]{:S(2)}) copy-start(bf16[256,512]{1,0:T(8,128)(2,1)} %refs_6_.2) | copy-start | bytes 786436
  45.6 11.9 %copy-start.2 = (bf16[256,512]{1,0:T(8,128)(2,1)S(1)}, bf16[256,512]{1,0:T(8,128)(2,1)}, u32[]{:S(2)}) copy-start(bf16[256,512]{1,0:T(8,128)(2,1)} %refs_7_.2) | copy-start | bytes 786436
  45.6 11.9 %copy-start.3 = (bf16[256,512]{1,0:T(8,128)(2,1)S(1)}, bf16[256,512]{1,0:T(8,128)(2,1)}, u32[]{:S(2)}) copy-start(bf16[256,512]{1,0:T(8,128)(2,1)} %refs_5_.2) | copy-start | bytes 786436
  45.6 11.9 %copy-start.4 = (bf16[256,512]{1,0:T(8,128)(2,1)S(1)}, bf16[256,512]{1,0:T(8,128)(2,1)}, u32[]{:S(2)}) copy-start(bf16[256,512]{1,0:T(8,128)(2,1)} %refs_8_.1) | copy-start | bytes 786436
  45.7 11.9 %copy-start.10 = (f32[512]{0:T(512)S(1)}, f32[512]{0:T(512)}, u32[]{:S(2)}) copy-start(f32[512]{0:T(512)} %param.16) | copy-start | bytes 6148
  46.0 8.3 %collective-permute-start.11 = (bf16[4,2,16,384]{3,2,1,0:T(8,128)(2,1)S(1)}, bf16[4,2,16,384]{3,2,1,0:T(8,128)(2,1)S(1)}, u32[]{:S(2)}, u32[]{:S(2)}) collective-permute-start(bf16[4,2,16,384]{3,2,1,0:T(8,128)(2,1)S(1)} %get-tuple-element.48), channel_id=1, source_target_pairs={{0,16},{8,24},{16,32},{24,40},{32,48},{40,56},{48,0},{56,8},{64,80... | collective-permute-start | bytes 294920 | tf_op jit(solution)/shard_map/ppermute | solution.py:42
  47.0 10.5 %collective-permute-start.12 = (bf16[4,2,16,384]{3,2,1,0:T(8,128)(2,1)S(1)}, bf16[4,2,16,384]{3,2,1,0:T(8,128)(2,1)S(1)}, u32[]{:S(2)}, u32[]{:S(2)}) collective-permute-start(bf16[4,2,16,384]{3,2,1,0:T(8,128)(2,1)S(1)} %get-tuple-element.49), channel_id=1, source_target_pairs={{0,32},{8,40},{16,48},{24,56},{32,0},{40,8},{48,16},{56,24},{64,96... | collective-permute-start | bytes 294920 | tf_op jit(solution)/shard_map/ppermute | solution.py:42
  49.5 8.1 %collective-permute-start.13 = (bf16[4,2,16,384]{3,2,1,0:T(8,128)(2,1)S(1)}, bf16[4,2,16,384]{3,2,1,0:T(8,128)(2,1)S(1)}, u32[]{:S(2)}, u32[]{:S(2)}) collective-permute-start(bf16[4,2,16,384]{3,2,1,0:T(8,128)(2,1)S(1)} %get-tuple-element.50), channel_id=1, source_target_pairs={{0,48},{8,56},{16,0},{24,8},{32,16},{40,24},{48,32},{56,40},{64,11... | collective-permute-start | bytes 294920 | tf_op jit(solution)/shard_map/ppermute | solution.py:42
  (3 other events, 13.8 us)

commit v6 on v5

--- a/solution.py
+++ b/solution.py
@@ -62,8 +62,7 @@
     return (
         first.astype(narrow),
         np.ascontiguousarray(first.T).astype(narrow),
-        second.astype(narrow),
-        np.ascontiguousarray(second.transpose(0, 2, 1)).astype(narrow),
+        np.stack([second, second.transpose(0, 2, 1)]).astype(narrow),
         np.cos(psi).astype(np.float32),
         (-np.sin(psi)).astype(np.float32),
     )
@@ -155,7 +154,7 @@
         t_ref[0, lines, h:] = (ti[:, :h] + ti[:, h:]).astype(BF16)
         t_ref[1, lines, :h] = (tr[:, :h] - tr[:, h:]).astype(BF16)
         t_ref[1, lines, h:] = (ti[:, :h] - ti[:, h:]).astype(BF16)
-    return [dot(t_ref[parity], second_ref[parity]) for parity in (0, 1)]
+    return [dot(t_ref[parity], second_ref[0, parity]) for parity in (0, 1)]
 
 
 def filter_kernel(*refs):
@@ -199,7 +198,6 @@
     first_ref,
     first_t_ref,
     second_ref,
-    second_t_ref,
     twr_ref,
     twi_ref,
     own_ref,
@@ -223,9 +221,9 @@
     for parity in (0, 1):
         spec_ref[0, parity] = gated[parity]
         spec_ref[1, parity] = delta[parity]
-    even, odd = (dot(products(gated[parity], taps[parity], h, False), second_t_ref[parity]) for parity in (0, 1))
+    even, odd = (dot(products(gated[parity], taps[parity], h, False), second_ref[1, parity]) for parity in (0, 1))
     y_ref[:, :, :rows] = signal(scale, even, odd, first_t_ref, twr, twi, v_ref.at[0])
-    even, odd = (dot(products(taps[parity], delta[parity], h, True), second_t_ref[parity]) for parity in (0, 1))
+    even, odd = (dot(products(taps[parity], delta[parity], h, True), second_ref[1, parity]) for parity in (0, 1))
     back = signal(scale, even, odd, first_t_ref, twr, twi, v_ref.at[1])
     y_ref[:, :, rows:] = back[:, :, :h]
     rest_ref[...] = back[:, :, h:]
@@ -233,7 +231,7 @@
 
 
 def backward_kernel(
-    scale, spec_ref, rest_ref, first_t_ref, second_t_ref, twr_ref, twi_ref, y_hbm, v_ref, y_ref, sems
+    scale, spec_ref, rest_ref, first_t_ref, second_ref, twr_ref, twi_ref, y_hbm, v_ref, y_ref, sems
 ):
     groups, chans, rows = y_ref.shape
     h = rows // 2
@@ -243,7 +241,7 @@
         pltpu.make_async_copy(y_ref, y_hbm.at[:, :, pl.ds(0, rows)], sems.at[1]),
     ]
     copies[0].start()
-    even, odd = (dot(products(spec_ref[0, parity], spec_ref[1, parity], h, True), second_t_ref[parity]) for parity in (0, 1))
+    even, odd = (dot(products(spec_ref[0, parity], spec_ref[1, parity], h, True), second_ref[1, parity]) for parity in (0, 1))
     y_ref[...] = signal(scale, even, odd, first_t_ref, twr, twi, v_ref)
     copies[1].start()
     for copy in copies:
@@ -342,7 +340,7 @@
         )
         return [kept] + [send(part, 0, dx, 0) for dx, part in enumerate(leaving, start=1)]
 
-    first, first_t, second, second_t, twr, twi = make_tables(order, rows)
+    first, first_t, second, twr, twi = make_tables(order, rows)
     def keep(*arrays):
         return [pltpu.with_memory_space_constraint(x, pltpu.HBM) for x in arrays]
 
@@ -381,7 +379,7 @@
             pltpu.VMEM((2, chans, 2 * groups, rows), BF16),
             pltpu.VMEM((groups, *block), BF16),
         ],
-    )(items, taps, part, first, first_t, second, second_t, twr, twi)
+    )(items, taps, part, first, first_t, second, twr, twi)
     terms = call(
         functools.partial(backward_kernel, scale),
         "backward",
@@ -393,7 +391,7 @@
         ],
         in_specs=[near] * 6,
         out_specs=far,
-    )(spec, rest, first_t, second_t, twr, twi)
+    )(spec, rest, first_t, second, twr, twi)
     arrived = travel(own, other, terms, WEIGHT)
     parts = 2
     return call(

time: 59.2 us -> 59 us (level)
  no operation moved by 1% of the time
where the time goes in v6:
time: 59 us; the launch traced here: 58.6 us
  starting transfers between devices  34.8 us (59%)
  waiting for transfers between devices  14.2 us (24%)
  Pallas kernels  8.57 us (15%)
  between operations  0.92 us (2%)
    ppermute x14, starting transfers between devices, send(): return lax.ppermute(block, 'context', moves)  20.9 us
    ppermute x14, waiting for transfers between devices, send(): return lax.ppermute(block, 'context', moves)  14.2 us
    all_to_all x2, starting transfers between devices, swap(): lax.all_to_all(block, 'context', split_axis=0, concat_axis=0, tiled=True,...  13.9 us
    pallas_call x1, Pallas kernels, local(): call(functools.partial(forward_kernel, scale), 'forward', [shape(4, 4, *b...  2.02 us
    pallas_call x1, Pallas kernels, local(): call(pack_late_kernel, 'pack_late', shape(groups, *block), [pltpu.VMEM((2...  1.94 us
    pallas_call x1, Pallas kernels, local(): call(functools.partial(backward_kernel, scale), 'backward', shape(groups,...  1.32 us
    pallas_call x1, Pallas kernels, local(): call(gate_kernel, 'gate', [whole] * 5, [pltpu.VMEM((groups, *block), BF16...  1.28 us
    pallas_call x1, Pallas kernels, local(): call(pack_early_kernel, 'pack_early', [pltpu.VMEM((4, 4, *block), BF16)]...  1.28 us
  transfers between devices with their start and end apart: 16, of which 5 were waited for; matrix products, arithmetic and copies ran while one was open for 0% of the time, Pallas kernels for 7%

profile of v6, /device:TPU:1, one launch (start us, length us, event | category | flops | bytes accessed | tf_op | source)
XLA Modules:
  0.0 58.6 jit_solution(4665276364811377964)
XLA Ops:
  0.6 1.3 %pack_early.1 = (bf16[4,4,16,384]{3,2,1,0:T(8,128)(2,1)S(1)}, bf16[4,4,16,384]{3,2,1,0:T(8,128)(2,1)S(1)}, bf16[32,16,128]{2,1,0:T(8,128)(2,1)S(1)}) custom-call(bf16[256,512]{1,0:T(8,128)(2,1)} %f_hbm.1, bf16[256,512]{1,0:T(8,128)(2,1)} %refs_6_.2, bf16[256,512]{1,0:T(8,128)(2,1)} %refs_7_.2), custom_call_target="tpu_custom_call" | custom-call | tf_op jit(solution)/shard_map/pack_early/pallas_call | solution.py:348
  1.9 3.3 %collective-permute-start = (bf16[4,4,16,384]{3,2,1,0:T(8,128)(2,1)S(1)}, bf16[4,4,16,384]{3,2,1,0:T(8,128)(2,1)S(1)}, u32[]{:S(2)}, u32[]{:S(2)}) collective-permute-start(bf16[4,4,16,384]{3,2,1,0:T(8,128)(2,1)S(1)} %get-tuple-element.30), channel_id=1, source_target_pairs={{0,8},{8,0},{16,24},{24,16},{32,40},{40,32},{48,56},{56,48},{64,72... | collective-permute-start | bytes 589832 | tf_op jit(solution)/shard_map/ppermute | solution.py:42
  5.2 1.9 %pack_late.1.after_ref = bf16[32,16,384]{2,1,0:T(8,128)(2,1)} custom-call(bf16[256,512]{1,0:T(8,128)(2,1)} %refs_5_.2, bf16[256,512]{1,0:T(8,128)(2,1)} %refs_8_.1, bf16[32,16,128]{2,1,0:T(8,128)(2,1)S(1)} %get-tuple-element.28.rest_ref), custom_call_target="tpu_custom_call" | custom-call | tf_op jit(solution)/shard_map/pack_late/pallas_call | solution.py:356
  7.3 2.9 %collective-permute-start.2 = (bf16[2,4,16,384]{3,2,1,0:T(8,128)(2,1)S(1)}, bf16[2,4,16,384]{3,2,1,0:T(8,128)(2,1)S(1)}, u32[]{:S(2)}, u32[]{:S(2)}) collective-permute-start(bf16[2,4,16,384]{3,2,1,0:T(8,128)(2,1)S(1)} %get-tuple-element.32), channel_id=1, source_target_pairs={{0,128},{8,136},{16,144},{24,152},{32,160},{40,168},{48,176},{56,1... | collective-permute-start | bytes 294920 | tf_op jit(solution)/shard_map/ppermute | solution.py:42
  10.2 0.7 %collective-permute-start.3 = (bf16[2,4,16,384]{3,2,1,0:T(8,128)(2,1)S(1)}, bf16[2,4,16,384]{3,2,1,0:T(8,128)(2,1)S(1)}, u32[]{:S(2)}, u32[]{:S(2)}) collective-permute-start(bf16[2,4,16,384]{3,2,1,0:T(8,128)(2,1)S(1)} %get-tuple-element.33), channel_id=1, source_target_pairs={{0,192},{8,200},{16,208},{24,216},{32,224},{40,232},{48,240},{56,2... | collective-permute-start | bytes 294920 | tf_op jit(solution)/shard_map/ppermute | solution.py:42
  10.9 7.8 %all-to-all-start = ((bf16[32,16,384]{2,1,0:T(8,128)(2,1)}), bf16[32,16,384]{2,1,0:T(8,128)(2,1)S(1)}, u32[]{:S(2)}, u32[]{:S(2)}) async-start(bf16[32,16,384]{2,1,0:T(8,128)(2,1)} %pack_late.1.after_ref), calls=%async_computation | async-start | bytes 786432 | tf_op jit(solution)/shard_map/all_to_all | solution.py:308
  18.9 1.3 %collective-permute-start.4 = (bf16[4,2,16,384]{3,2,1,0:T(8,128)(2,1)S(1)}, bf16[4,2,16,384]{3,2,1,0:T(8,128)(2,1)S(1)}, u32[]{:S(2)}, u32[]{:S(2)}) collective-permute-start(bf16[4,2,16,384]{3,2,1,0:T(8,128)(2,1)S(1)} %get-tuple-element.35), channel_id=1, source_target_pairs={{0,16},{8,24},{16,32},{24,40},{32,48},{40,56},{48,0},{56,8},{64,80... | collective-permute-start | bytes 294920 | tf_op jit(solution)/shard_map/ppermute | solution.py:42
  20.1 2.4 %collective-permute-start.5 = (bf16[4,2,16,384]{3,2,1,0:T(8,128)(2,1)S(1)}, bf16[4,2,16,384]{3,2,1,0:T(8,128)(2,1)S(1)}, u32[]{:S(2)}, u32[]{:S(2)}) collective-permute-start(bf16[4,2,16,384]{3,2,1,0:T(8,128)(2,1)S(1)} %get-tuple-element.36), channel_id=1, source_target_pairs={{0,32},{8,40},{16,48},{24,56},{32,0},{40,8},{48,16},{56,24},{64,96... | collective-permute-start | bytes 294920 | tf_op jit(solution)/shard_map/ppermute | solution.py:42
  22.6 1.1 %collective-permute-start.6 = (bf16[4,2,16,384]{3,2,1,0:T(8,128)(2,1)S(1)}, bf16[4,2,16,384]{3,2,1,0:T(8,128)(2,1)S(1)}, u32[]{:S(2)}, u32[]{:S(2)}) collective-permute-start(bf16[4,2,16,384]{3,2,1,0:T(8,128)(2,1)S(1)} %get-tuple-element.37), channel_id=1, source_target_pairs={{0,48},{8,56},{16,0},{24,8},{32,16},{40,24},{48,32},{56,40},{64,11... | collective-permute-start | bytes 294920 | tf_op jit(solution)/shard_map/ppermute | solution.py:42
  23.7 3.9 %collective-permute-done.4.refs_1_ = bf16[4,2,16,384]{3,2,1,0:T(8,128)(2,1)S(1)} collective-permute-done((bf16[4,2,16,384]{3,2,1,0:T(8,128)(2,1)S(1)}, bf16[4,2,16,384]{3,2,1,0:T(8,128)(2,1)S(1)}, u32[]{:S(2)}, u32[]{:S(2)}) %collective-permute-start.4) | collective-permute-done | bytes 98336 | tf_op jit(solution)/shard_map/ppermute | solution.py:42
  27.6 3.0 %collective-permute-done.5.refs_2_ = bf16[4,2,16,384]{3,2,1,0:T(8,128)(2,1)S(1)} collective-permute-done((bf16[4,2,16,384]{3,2,1,0:T(8,128)(2,1)S(1)}, bf16[4,2,16,384]{3,2,1,0:T(8,128)(2,1)S(1)}, u32[]{:S(2)}, u32[]{:S(2)}) %collective-permute-start.5) | collective-permute-done | bytes 98336 | tf_op jit(solution)/shard_map/ppermute | solution.py:42
  30.7 0.6 %filter_spectrum.1 = (f32[2,512,256]{2,1,0:T(8,128)S(1)}, bf16[32,16,128]{2,1,0:T(8,128)(2,1)S(1)}) custom-call(bf16[4,2,16,384]{3,2,1,0:T(8,128)(2,1)S(1)} %get-tuple-element.34.refs_0_, bf16[4,2,16,384]{3,2,1,0:T(8,128)(2,1)S(1)} %collective-permute-done.4.refs_1_, bf16[4,2,16,384]{3,2,1,0:T(8,128)(2,1)S(1)} %collective-permute-done.5.refs_2_, ...), custom_call_target="tpu_custom_call" | custom-call | flops 5000000000 | bytes 5000000000 | tf_op jit(solution)/shard_map/filter_spectrum/pallas_call | solution.py:364
  31.4 2.0 %forward.1 = (bf16[4,4,16,384]{3,2,1,0:T(8,128)(2,1)S(1)}, bf16[4,4,16,384]{3,2,1,0:T(8,128)(2,1)S(1)}, bf16[32,16,128]{2,1,0:T(8,128)(2,1)S(1)}, f32[2,2,512,256]{3,2,1,0:T(8,128)S(1)}) custom-call(bf16[32,16,384]{2,1,0:T(8,128)(2,1)S(1)} %all-to-all-done.x_ref, f32[2,512,256]{2,1,0:T(8,128)S(1)} %get-tuple-element.38.taps_ref, ...), custom_call_target="tpu_custom_call" | custom-call | tf_op jit(solution)/shard_map/forward/pallas_call | solution.py:372
  33.4 0.9 %collective-permute-start.7 = (bf16[4,4,16,384]{3,2,1,0:T(8,128)(2,1)S(1)}, bf16[4,4,16,384]{3,2,1,0:T(8,128)(2,1)S(1)}, u32[]{:S(2)}, u32[]{:S(2)}) collective-permute-start(bf16[4,4,16,384]{3,2,1,0:T(8,128)(2,1)S(1)} %get-tuple-element.41), channel_id=1, source_target_pairs={{0,8},{8,0},{16,24},{24,16},{32,40},{40,32},{48,56},{56,48},{64,72... | collective-permute-start | bytes 589832 | tf_op jit(solution)/shard_map/ppermute | solution.py:42
  34.3 1.3 %backward.1.after_ref = bf16[32,16,384]{2,1,0:T(8,128)(2,1)} custom-call(f32[2,2,512,256]{3,2,1,0:T(8,128)S(1)} %get-tuple-element.42.spec_ref, bf16[32,16,128]{2,1,0:T(8,128)(2,1)S(1)} %get-tuple-element.43.rest_ref, bf16[32,64]{1,0:T(8,128)(2,1)S(1)} %copy-done.7, bf16[2,2,256,256]{3,2,1,0:T(8,128)(2,1)S(1)} %copy-done, f32[32,256]{1,0:T(8,128)S(1)} %copy-done.6, ...), custom_call_target="tpu_custom_call" | custom-call | tf_op jit(solution)/shard_map/backward/pallas_call | solution.py:383
  36.2 2.0 %collective-permute-start.9 = (bf16[2,4,16,384]{3,2,1,0:T(8,128)(2,1)S(1)}, bf16[2,4,16,384]{3,2,1,0:T(8,128)(2,1)S(1)}, u32[]{:S(2)}, u32[]{:S(2)}) collective-permute-start(bf16[2,4,16,384]{3,2,1,0:T(8,128)(2,1)S(1)} %get-tuple-element.45), channel_id=1, source_target_pairs={{0,128},{8,136},{16,144},{24,152},{32,160},{40,168},{48,176},{56,1... | collective-permute-start | bytes 294920 | tf_op jit(solution)/shard_map/ppermute | solution.py:42
  38.3 1.1 %collective-permute-start.10 = (bf16[2,4,16,384]{3,2,1,0:T(8,128)(2,1)S(1)}, bf16[2,4,16,384]{3,2,1,0:T(8,128)(2,1)S(1)}, u32[]{:S(2)}, u32[]{:S(2)}) collective-permute-start(bf16[2,4,16,384]{3,2,1,0:T(8,128)(2,1)S(1)} %get-tuple-element.46), channel_id=1, source_target_pairs={{0,192},{8,200},{16,208},{24,216},{32,224},{40,232},{48,240},{56,2... | collective-permute-start | bytes 294920 | tf_op jit(solution)/shard_map/ppermute | solution.py:42
  39.3 6.0 %all-to-all-start.1 = ((bf16[32,16,384]{2,1,0:T(8,128)(2,1)}), bf16[32,16,384]{2,1,0:T(8,128)(2,1)S(1)}, u32[]{:S(2)}, u32[]{:S(2)}) async-start(bf16[32,16,384]{2,1,0:T(8,128)(2,1)} %backward.1.after_ref), calls=%async_computation.1 | async-start | bytes 786432 | tf_op jit(solution)/shard_map/all_to_all | solution.py:308
  45.7 1.0 %collective-permute-start.11 = (bf16[4,2,16,384]{3,2,1,0:T(8,128)(2,1)S(1)}, bf16[4,2,16,384]{3,2,1,0:T(8,128)(2,1)S(1)}, u32[]{:S(2)}, u32[]{:S(2)}) collective-permute-start(bf16[4,2,16,384]{3,2,1,0:T(8,128)(2,1)S(1)} %get-tuple-element.48), channel_id=1, source_target_pairs={{0,16},{8,24},{16,32},{24,40},{32,48},{40,56},{48,0},{56,8},{64,80... | collective-permute-start | bytes 294920 | tf_op jit(solution)/shard_map/ppermute | solution.py:42
  46.7 2.4 %collective-permute-start.12 = (bf16[4,2,16,384]{3,2,1,0:T(8,128)(2,1)S(1)}, bf16[4,2,16,384]{3,2,1,0:T(8,128)(2,1)S(1)}, u32[]{:S(2)}, u32[]{:S(2)}) collective-permute-start(bf16[4,2,16,384]{3,2,1,0:T(8,128)(2,1)S(1)} %get-tuple-element.49), channel_id=1, source_target_pairs={{0,32},{8,40},{16,48},{24,56},{32,0},{40,8},{48,16},{56,24},{64,96... | collective-permute-start | bytes 294920 | tf_op jit(solution)/shard_map/ppermute | solution.py:42
  49.2 1.1 %collective-permute-start.13 = (bf16[4,2,16,384]{3,2,1,0:T(8,128)(2,1)S(1)}, bf16[4,2,16,384]{3,2,1,0:T(8,128)(2,1)S(1)}, u32[]{:S(2)}, u32[]{:S(2)}) collective-permute-start(bf16[4,2,16,384]{3,2,1,0:T(8,128)(2,1)S(1)} %get-tuple-element.50), channel_id=1, source_target_pairs={{0,48},{8,56},{16,0},{24,8},{32,16},{40,24},{48,32},{56,40},{64,11... | collective-permute-start | bytes 294920 | tf_op jit(solution)/shard_map/ppermute | solution.py:42
  50.3 3.7 %collective-permute-done.11.refs_1_ = bf16[4,2,16,384]{3,2,1,0:T(8,128)(2,1)S(1)} collective-permute-done((bf16[4,2,16,384]{3,2,1,0:T(8,128)(2,1)S(1)}, bf16[4,2,16,384]{3,2,1,0:T(8,128)(2,1)S(1)}, u32[]{:S(2)}, u32[]{:S(2)}) %collective-permute-start.11) | collective-permute-done | bytes 98336 | tf_op jit(solution)/shard_map/ppermute | solution.py:42
  54.0 3.3 %collective-permute-done.12.refs_2_ = bf16[4,2,16,384]{3,2,1,0:T(8,128)(2,1)S(1)} collective-permute-done((bf16[4,2,16,384]{3,2,1,0:T(8,128)(2,1)S(1)}, bf16[4,2,16,384]{3,2,1,0:T(8,128)(2,1)S(1)}, u32[]{:S(2)}, u32[]{:S(2)}) %collective-permute-start.12) | collective-permute-done | bytes 98336 | tf_op jit(solution)/shard_map/ppermute | solution.py:42
  57.3 1.3 %gate.1 = (bf16[256,512]{1,0:T(8,128)(2,1)}, bf16[256,512]{1,0:T(8,128)(2,1)}, bf16[256,512]{1,0:T(8,128)(2,1)}, bf16[256,512]{1,0:T(8,128)(2,1)}, bf16[256,512]{1,0:T(8,128)(2,1)}) custom-call(bf16[4,2,16,384]{3,2,1,0:T(8,128)(2,1)S(1)} %get-tuple-element.47.refs_0_, bf16[4,2,16,384]{3,2,1,0:T(8,128)(2,1)S(1)} %collective-permute-done.11.refs_1_, ...), custom_call_target="tpu_custom_call" | custom-call | tf_op jit(solution)/shard_map/gate/pallas_call | solution.py:397
  (38 shorter events, 1.2 us)
Async XLA Ops:
  1.9 5.3 %collective-permute-start = (bf16[4,4,16,384]{3,2,1,0:T(8,128)(2,1)S(1)}, bf16[4,4,16,384]{3,2,1,0:T(8,128)(2,1)S(1)}, u32[]{:S(2)}, u32[]{:S(2)}) collective-permute-start(bf16[4,4,16,384]{3,2,1,0:T(8,128)(2,1)S(1)} %get-tuple-element.30), channel_id=1, source_target_pairs={{0,8},{8,0},{16,24},{24,16},{32,40},{40,32},{48,56},{56,48},{64,72... | collective-permute-start | bytes 589832 | tf_op jit(solution)/shard_map/ppermute | solution.py:42
  7.2 11.5 %collective-permute-start.1 = (bf16[2,4,16,384]{3,2,1,0:T(8,128)(2,1)S(1)}, bf16[2,4,16,384]{3,2,1,0:T(8,128)(2,1)S(1)}, u32[]{:S(2)}, u32[]{:S(2)}) collective-permute-start(bf16[2,4,16,384]{3,2,1,0:T(8,128)(2,1)S(1)} %get-tuple-element.31), channel_id=1, source_target_pairs={{0,64},{8,72},{16,80},{24,88},{32,96},{40,104},{48,112},{56,120},{... | collective-permute-start | bytes 294920 | tf_op jit(solution)/shard_map/ppermute | solution.py:42
  7.3 11.4 %collective-permute-start.2 = (bf16[2,4,16,384]{3,2,1,0:T(8,128)(2,1)S(1)}, bf16[2,4,16,384]{3,2,1,0:T(8,128)(2,1)S(1)}, u32[]{:S(2)}, u32[]{:S(2)}) collective-permute-start(bf16[2,4,16,384]{3,2,1,0:T(8,128)(2,1)S(1)} %get-tuple-element.32), channel_id=1, source_target_pairs={{0,128},{8,136},{16,144},{24,152},{32,160},{40,168},{48,176},{56,1... | collective-permute-start | bytes 294920 | tf_op jit(solution)/shard_map/ppermute | solution.py:42
  10.2 8.6 %collective-permute-start.3 = (bf16[2,4,16,384]{3,2,1,0:T(8,128)(2,1)S(1)}, bf16[2,4,16,384]{3,2,1,0:T(8,128)(2,1)S(1)}, u32[]{:S(2)}, u32[]{:S(2)}) collective-permute-start(bf16[2,4,16,384]{3,2,1,0:T(8,128)(2,1)S(1)} %get-tuple-element.33), channel_id=1, source_target_pairs={{0,192},{8,200},{16,208},{24,216},{32,224},{40,232},{48,240},{56,2... | collective-permute-start | bytes 294920 | tf_op jit(solution)/shard_map/ppermute | solution.py:42
  10.9 20.4 %all-to-all-start = ((bf16[32,16,384]{2,1,0:T(8,128)(2,1)}), bf16[32,16,384]{2,1,0:T(8,128)(2,1)S(1)}, u32[]{:S(2)}, u32[]{:S(2)}) async-start(bf16[32,16,384]{2,1,0:T(8,128)(2,1)} %pack_late.1.after_ref), calls=%async_computation | async-start | bytes 786432 | tf_op jit(solution)/shard_map/all_to_all | solution.py:308
  18.7 11.9 %copy-start = (bf16[2,2,256,256]{3,2,1,0:T(8,128)(2,1)S(1)}, bf16[2,2,256,256]{3,2,1,0:T(8,128)(2,1)}, u32[]{:S(2)}) copy-start(bf16[2,2,256,256]{3,2,1,0:T(8,128)(2,1)} %constant.11.clone.refs_5_.second_ref) | copy-start | bytes 1572868
  18.7 11.9 %copy-start.5 = (f32[32,256]{1,0:T(8,128)S(1)}, f32[32,256]{1,0:T(8,128)}, u32[]{:S(2)}) copy-start(f32[32,256]{1,0:T(8,128)} %constant.13.clone.refs_7_.twi_ref) | copy-start | bytes 98308
  18.8 11.9 %copy-start.6 = (f32[32,256]{1,0:T(8,128)S(1)}, f32[32,256]{1,0:T(8,128)}, u32[]{:S(2)}) copy-start(f32[32,256]{1,0:T(8,128)} %constant.12.clone.refs_6_.twr_ref) | copy-start | bytes 98308
  18.9 8.8 %collective-permute-start.4 = (bf16[4,2,16,384]{3,2,1,0:T(8,128)(2,1)S(1)}, bf16[4,2,16,384]{3,2,1,0:T(8,128)(2,1)S(1)}, u32[]{:S(2)}, u32[]{:S(2)}) collective-permute-start(bf16[4,2,16,384]{3,2,1,0:T(8,128)(2,1)S(1)} %get-tuple-element.35), channel_id=1, source_target_pairs={{0,16},{8,24},{16,32},{24,40},{32,48},{40,56},{48,0},{56,8},{64,80... | collective-permute-start | bytes 294920 | tf_op jit(solution)/shard_map/ppermute | solution.py:42
  20.1 10.5 %collective-permute-start.5 = (bf16[4,2,16,384]{3,2,1,0:T(8,128)(2,1)S(1)}, bf16[4,2,16,384]{3,2,1,0:T(8,128)(2,1)S(1)}, u32[]{:S(2)}, u32[]{:S(2)}) collective-permute-start(bf16[4,2,16,384]{3,2,1,0:T(8,128)(2,1)S(1)} %get-tuple-element.36), channel_id=1, source_target_pairs={{0,32},{8,40},{16,48},{24,56},{32,0},{40,8},{48,16},{56,24},{64,96... | collective-permute-start | bytes 294920 | tf_op jit(solution)/shard_map/ppermute | solution.py:42
  22.6 8.1 %collective-permute-start.6 = (bf16[4,2,16,384]{3,2,1,0:T(8,128)(2,1)S(1)}, bf16[4,2,16,384]{3,2,1,0:T(8,128)(2,1)S(1)}, u32[]{:S(2)}, u32[]{:S(2)}) collective-permute-start(bf16[4,2,16,384]{3,2,1,0:T(8,128)(2,1)S(1)} %get-tuple-element.37), channel_id=1, source_target_pairs={{0,48},{8,56},{16,0},{24,8},{32,16},{40,24},{48,32},{56,40},{64,11... | collective-permute-start | bytes 294920 | tf_op jit(solution)/shard_map/ppermute | solution.py:42
  33.4 2.2 %collective-permute-start.7 = (bf16[4,4,16,384]{3,2,1,0:T(8,128)(2,1)S(1)}, bf16[4,4,16,384]{3,2,1,0:T(8,128)(2,1)S(1)}, u32[]{:S(2)}, u32[]{:S(2)}) collective-permute-start(bf16[4,4,16,384]{3,2,1,0:T(8,128)(2,1)S(1)} %get-tuple-element.41), channel_id=1, source_target_pairs={{0,8},{8,0},{16,24},{24,16},{32,40},{40,32},{48,56},{56,48},{64,72... | collective-permute-start | bytes 589832 | tf_op jit(solution)/shard_map/ppermute | solution.py:42
  35.7 9.7 %collective-permute-start.8 = (bf16[2,4,16,384]{3,2,1,0:T(8,128)(2,1)S(1)}, bf16[2,4,16,384]{3,2,1,0:T(8,128)(2,1)S(1)}, u32[]{:S(2)}, u32[]{:S(2)}) collective-permute-start(bf16[2,4,16,384]{3,2,1,0:T(8,128)(2,1)S(1)} %get-tuple-element.44), channel_id=1, source_target_pairs={{0,64},{8,72},{16,80},{24,88},{32,96},{40,104},{48,112},{56,120},{... | collective-permute-start | bytes 294920 | tf_op jit(solution)/shard_map/ppermute | solution.py:42
  36.2 9.2 %collective-permute-start.9 = (bf16[2,4,16,384]{3,2,1,0:T(8,128)(2,1)S(1)}, bf16[2,4,16,384]{3,2,1,0:T(8,128)(2,1)S(1)}, u32[]{:S(2)}, u32[]{:S(2)}) collective-permute-start(bf16[2,4,16,384]{3,2,1,0:T(8,128)(2,1)S(1)} %get-tuple-element.45), channel_id=1, source_target_pairs={{0,128},{8,136},{16,144},{24,152},{32,160},{40,168},{48,176},{56,1... | collective-permute-start | bytes 294920 | tf_op jit(solution)/shard_map/ppermute | solution.py:42
  38.3 7.4 %collective-permute-start.10 = (bf16[2,4,16,384]{3,2,1,0:T(8,128)(2,1)S(1)}, bf16[2,4,16,384]{3,2,1,0:T(8,128)(2,1)S(1)}, u32[]{:S(2)}, u32[]{:S(2)}) collective-permute-start(bf16[2,4,16,384]{3,2,1,0:T(8,128)(2,1)S(1)} %get-tuple-element.46), channel_id=1, source_target_pairs={{0,192},{8,200},{16,208},{24,216},{32,224},{40,232},{48,240},{56,2... | collective-permute-start | bytes 294920 | tf_op jit(solution)/shard_map/ppermute | solution.py:42
  39.3 18.0 %all-to-all-start.1 = ((bf16[32,16,384]{2,1,0:T(8,128)(2,1)}), bf16[32,16,384]{2,1,0:T(8,128)(2,1)S(1)}, u32[]{:S(2)}, u32[]{:S(2)}) async-start(bf16[32,16,384]{2,1,0:T(8,128)(2,1)} %backward.1.after_ref), calls=%async_computation.1 | async-start | bytes 786432 | tf_op jit(solution)/shard_map/all_to_all | solution.py:308
  45.3 11.9 %copy-start.1 = (bf16[256,512]{1,0:T(8,128)(2,1)S(1)}, bf16[256,512]{1,0:T(8,128)(2,1)}, u32[]{:S(2)}) copy-start(bf16[256,512]{1,0:T(8,128)(2,1)} %refs_6_.2) | copy-start | bytes 786436
  45.4 11.9 %copy-start.2 = (bf16[256,512]{1,0:T(8,128)(2,1)S(1)}, bf16[256,512]{1,0:T(8,128)(2,1)}, u32[]{:S(2)}) copy-start(bf16[256,512]{1,0:T(8,128)(2,1)} %refs_7_.2) | copy-start | bytes 786436
  45.4 11.9 %copy-start.3 = (bf16[256,512]{1,0:T(8,128)(2,1)S(1)}, bf16[256,512]{1,0:T(8,128)(2,1)}, u32[]{:S(2)}) copy-start(bf16[256,512]{1,0:T(8,128)(2,1)} %refs_5_.2) | copy-start | bytes 786436
  45.4 11.9 %copy-start.4 = (bf16[256,512]{1,0:T(8,128)(2,1)S(1)}, bf16[256,512]{1,0:T(8,128)(2,1)}, u32[]{:S(2)}) copy-start(bf16[256,512]{1,0:T(8,128)(2,1)} %refs_8_.1) | copy-start | bytes 786436
  45.4 11.9 %copy-start.9 = (f32[512]{0:T(512)S(1)}, f32[512]{0:T(512)}, u32[]{:S(2)}) copy-start(f32[512]{0:T(512)} %param.15) | copy-start | bytes 6148
  45.7 8.2 %collective-permute-start.11 = (bf16[4,2,16,384]{3,2,1,0:T(8,128)(2,1)S(1)}, bf16[4,2,16,384]{3,2,1,0:T(8,128)(2,1)S(1)}, u32[]{:S(2)}, u32[]{:S(2)}) collective-permute-start(bf16[4,2,16,384]{3,2,1,0:T(8,128)(2,1)S(1)} %get-tuple-element.48), channel_id=1, source_target_pairs={{0,16},{8,24},{16,32},{24,40},{32,48},{40,56},{48,0},{56,8},{64,80... | collective-permute-start | bytes 294920 | tf_op jit(solution)/shard_map/ppermute | solution.py:42
  46.7 10.5 %collective-permute-start.12 = (bf16[4,2,16,384]{3,2,1,0:T(8,128)(2,1)S(1)}, bf16[4,2,16,384]{3,2,1,0:T(8,128)(2,1)S(1)}, u32[]{:S(2)}, u32[]{:S(2)}) collective-permute-start(bf16[4,2,16,384]{3,2,1,0:T(8,128)(2,1)S(1)} %get-tuple-element.49), channel_id=1, source_target_pairs={{0,32},{8,40},{16,48},{24,56},{32,0},{40,8},{48,16},{56,24},{64,96... | collective-permute-start | bytes 294920 | tf_op jit(solution)/shard_map/ppermute | solution.py:42
  49.2 8.1 %collective-permute-start.13 = (bf16[4,2,16,384]{3,2,1,0:T(8,128)(2,1)S(1)}, bf16[4,2,16,384]{3,2,1,0:T(8,128)(2,1)S(1)}, u32[]{:S(2)}, u32[]{:S(2)}) collective-permute-start(bf16[4,2,16,384]{3,2,1,0:T(8,128)(2,1)S(1)} %get-tuple-element.50), channel_id=1, source_target_pairs={{0,48},{8,56},{16,0},{24,8},{32,16},{40,24},{48,32},{56,40},{64,11... | collective-permute-start | bytes 294920 | tf_op jit(solution)/shard_map/ppermute | solution.py:42
  (2 other events, 12.6 us)

commit v7 on v6

--- a/solution.py
+++ b/solution.py
@@ -13,7 +13,7 @@
 BF16 = jnp.bfloat16
 ZORDER = (1, 2, 3)
 F32 = jnp.float32
-WEIGHT1 = 5 * 10**9
+WEIGHT1 = 8 * 10**9
 WEIGHT = 8 * 10**9
 
 
@@ -157,17 +157,6 @@
     return [dot(t_ref[parity], second_ref[0, parity]) for parity in (0, 1)]
 
 
-def filter_kernel(*refs):
-    arrived = refs[:4]
-    first_ref, second_ref, twr_ref, twi_ref, spec_ref, rest_ref, x_ref, t_ref = refs[4:]
-    gather(lax.axis_index("context"), arrived, x_ref)
-    rows = twr_ref.shape[1]
-    items = jnp.swapaxes(x_ref[:, :, :rows], 0, 1)
-    for parity, bins in enumerate(spectrum(items, first_ref, second_ref, twr_ref[...], twi_ref[...], t_ref)):
-        spec_ref[parity] = bins
-    rest_ref[...] = x_ref[:, :, rows:]
-
-
 def products(left, right, h, conjugate):
     lr, li, rr, ri = left[:, :h], left[:, h:], right[:, :h], right[:, h:]
     if conjugate:
@@ -190,34 +179,19 @@
     return jnp.swapaxes(out.astype(BF16), 0, 1)
 
 
-def forward_kernel(
-    scale,
-    x_ref,
-    taps_ref,
-    part_ref,
-    first_ref,
-    first_t_ref,
-    second_ref,
-    twr_ref,
-    twi_ref,
-    own_ref,
-    other_ref,
-    rest_ref,
-    spec_ref,
-    t_ref,
-    v_ref,
-    y_ref,
-):
+def forward_kernel(scale, *refs):
+    arrived = refs[:4]
+    x_ref, first_ref, first_t_ref, second_ref, twr_ref, twi_ref = refs[4:10]
+    own_ref, other_ref, rest_ref, spec_ref, t_ref, v_ref, y_ref = refs[10:]
     rows = twr_ref.shape[1]
     h = rows // 2
     twr, twi = twr_ref[...], twi_ref[...]
-    gated = jnp.concatenate([part_ref[...], x_ref[:, :, rows:]], axis=2)
-    spectra = [
+    gather(lax.axis_index("context"), arrived, y_ref)
+    gated = jnp.concatenate([y_ref[:, :, rows:], x_ref[:, :, rows:]], axis=2)
+    taps, gated, delta = (
         spectrum(jnp.swapaxes(block, 0, 1), first_ref, second_ref, twr, twi, t_ref.at[s])
-        for s, block in enumerate((gated, x_ref[:, :, :rows]))
-    ]
-    gated, delta = spectra
-    taps = taps_ref
+        for s, block in enumerate((y_ref[:, :, :rows], gated, x_ref[:, :, :rows]))
+    )
     for parity in (0, 1):
         spec_ref[0, parity] = gated[parity]
         spec_ref[1, parity] = delta[parity]
@@ -361,13 +335,7 @@
         in_specs=[far] * 2 + [near],
         out_specs=far,
     )(*keep(q_gate, out_grad), rest)
-    taps, part = call(
-        filter_kernel,
-        "filter_spectrum",
-        [jax.ShapeDtypeStruct((2, *bins), F32), shape(groups, *half)],
-        [pltpu.VMEM((groups, *block), BF16), pltpu.VMEM((2, *bins), BF16)],
-        weight=WEIGHT1,
-    )(*travel(own, other, sent, WEIGHT1), first, second, twr, twi)
+    early = travel(own, other, sent, WEIGHT1)
     items = swap(sent)
     own, other, rest, spec = call(
         functools.partial(forward_kernel, scale),
@@ -375,11 +343,11 @@
         [shape(4, 4, *block)] * 2
         + [shape(groups, *half), jax.ShapeDtypeStruct((2, 2, *bins), F32)],
         [
-            pltpu.VMEM((2, 2, *bins), BF16),
+            pltpu.VMEM((3, 2, *bins), BF16),
             pltpu.VMEM((2, chans, 2 * groups, rows), BF16),
             pltpu.VMEM((groups, *block), BF16),
         ],
-    )(items, taps, part, first, first_t, second, twr, twi)
+    )(*early, items, first, first_t, second, twr, twi)
     terms = call(
         functools.partial(backward_kernel, scale),
         "backward",

time: 59 us -> 58.7 us (level)
    pallas_call x1 -> x0, Pallas kernels: 0.6 us -> none  [local(): call(filter_kernel, 'filter_spectrum', [jax.ShapeDtypeStruct((2, *bins),...]
  transfers between devices with their start and end apart: 16 -> 16, of which waited for: 5 -> 5; matrix products, arithmetic and copies ran while one was open for 0% -> 0% of each run, Pallas kernels for 7% -> 6%
where the time goes in v7:
time: 58.7 us; the launch traced here: 58.4 us
  starting transfers between devices  34.8 us (59%)
  waiting for transfers between devices  14.2 us (24%)
  Pallas kernels  8.44 us (14%)
  between operations  0.92 us (2%)
    ppermute x14, starting transfers between devices, send(): return lax.ppermute(block, 'context', moves)  21.2 us
    ppermute x14, waiting for transfers between devices, send(): return lax.ppermute(block, 'context', moves)  14.2 us
    all_to_all x2, starting transfers between devices, swap(): lax.all_to_all(block, 'context', split_axis=0, concat_axis=0, tiled=True,...  13.6 us
    pallas_call x1, Pallas kernels, local(): call(functools.partial(forward_kernel, scale), 'forward', [shape(4, 4, *b...  2.49 us
    pallas_call x1, Pallas kernels, local(): call(pack_late_kernel, 'pack_late', shape(groups, *block), [pltpu.VMEM((2...  1.93 us
    pallas_call x1, Pallas kernels, local(): call(functools.partial(backward_kernel, scale), 'backward', shape(groups,...  1.31 us
    pallas_call x1, Pallas kernels, local(): call(gate_kernel, 'gate', [whole] * 5, [pltpu.VMEM((groups, *block), BF16...  1.28 us
    pallas_call x1, Pallas kernels, local(): call(pack_early_kernel, 'pack_early', [pltpu.VMEM((4, 4, *block), BF16)]...  1.28 us
  transfers between devices with their start and end apart: 16, of which 5 were waited for; matrix products, arithmetic and copies ran while one was open for 0% of the time, Pallas kernels for 6%

profile of v7, /device:TPU:1, one launch (start us, length us, event | category | flops | bytes accessed | tf_op | source)
XLA Modules:
  0.0 58.4 jit_solution(17849215542875896686)
XLA Ops:
  0.6 1.3 %pack_early.1 = (bf16[4,4,16,384]{3,2,1,0:T(8,128)(2,1)S(1)}, bf16[4,4,16,384]{3,2,1,0:T(8,128)(2,1)S(1)}, bf16[32,16,128]{2,1,0:T(8,128)(2,1)S(1)}) custom-call(bf16[256,512]{1,0:T(8,128)(2,1)} %f_hbm.1, bf16[256,512]{1,0:T(8,128)(2,1)} %refs_6_.2, bf16[256,512]{1,0:T(8,128)(2,1)} %refs_7_.2), custom_call_target="tpu_custom_call" | custom-call | tf_op jit(solution)/shard_map/pack_early/pallas_call | solution.py:322
  1.9 3.3 %collective-permute-start = (bf16[4,4,16,384]{3,2,1,0:T(8,128)(2,1)S(1)}, bf16[4,4,16,384]{3,2,1,0:T(8,128)(2,1)S(1)}, u32[]{:S(2)}, u32[]{:S(2)}) collective-permute-start(bf16[4,4,16,384]{3,2,1,0:T(8,128)(2,1)S(1)} %get-tuple-element.27), channel_id=1, source_target_pairs={{0,8},{8,0},{16,24},{24,16},{32,40},{40,32},{48,56},{56,48},{64,72... | collective-permute-start | bytes 589832 | tf_op jit(solution)/shard_map/ppermute | solution.py:42
  5.2 1.9 %pack_late.1.after_ref = bf16[32,16,384]{2,1,0:T(8,128)(2,1)} custom-call(bf16[256,512]{1,0:T(8,128)(2,1)} %refs_5_.2, bf16[256,512]{1,0:T(8,128)(2,1)} %refs_8_.2, bf16[32,16,128]{2,1,0:T(8,128)(2,1)S(1)} %get-tuple-element.28.rest_ref), custom_call_target="tpu_custom_call" | custom-call | tf_op jit(solution)/shard_map/pack_late/pallas_call | solution.py:330
  7.3 2.9 %collective-permute-start.2 = (bf16[2,4,16,384]{3,2,1,0:T(8,128)(2,1)S(1)}, bf16[2,4,16,384]{3,2,1,0:T(8,128)(2,1)S(1)}, u32[]{:S(2)}, u32[]{:S(2)}) collective-permute-start(bf16[2,4,16,384]{3,2,1,0:T(8,128)(2,1)S(1)} %get-tuple-element.30), channel_id=1, source_target_pairs={{0,128},{8,136},{16,144},{24,152},{32,160},{40,168},{48,176},{56,1... | collective-permute-start | bytes 294920 | tf_op jit(solution)/shard_map/ppermute | solution.py:42
  10.2 0.7 %collective-permute-start.3 = (bf16[2,4,16,384]{3,2,1,0:T(8,128)(2,1)S(1)}, bf16[2,4,16,384]{3,2,1,0:T(8,128)(2,1)S(1)}, u32[]{:S(2)}, u32[]{:S(2)}) collective-permute-start(bf16[2,4,16,384]{3,2,1,0:T(8,128)(2,1)S(1)} %get-tuple-element.31), channel_id=1, source_target_pairs={{0,192},{8,200},{16,208},{24,216},{32,224},{40,232},{48,240},{56,2... | collective-permute-start | bytes 294920 | tf_op jit(solution)/shard_map/ppermute | solution.py:42
  10.9 7.8 %all-to-all-start = ((bf16[32,16,384]{2,1,0:T(8,128)(2,1)}), bf16[32,16,384]{2,1,0:T(8,128)(2,1)S(1)}, u32[]{:S(2)}, u32[]{:S(2)}) async-start(bf16[32,16,384]{2,1,0:T(8,128)(2,1)} %pack_late.1.after_ref), calls=%async_computation | async-start | bytes 786432 | tf_op jit(solution)/shard_map/all_to_all | solution.py:282
  18.9 1.3 %collective-permute-start.4 = (bf16[4,2,16,384]{3,2,1,0:T(8,128)(2,1)S(1)}, bf16[4,2,16,384]{3,2,1,0:T(8,128)(2,1)S(1)}, u32[]{:S(2)}, u32[]{:S(2)}) collective-permute-start(bf16[4,2,16,384]{3,2,1,0:T(8,128)(2,1)S(1)} %get-tuple-element.33), channel_id=1, source_target_pairs={{0,16},{8,24},{16,32},{24,40},{32,48},{40,56},{48,0},{56,8},{64,80... | collective-permute-start | bytes 294920 | tf_op jit(solution)/shard_map/ppermute | solution.py:42
  20.1 2.4 %collective-permute-start.5 = (bf16[4,2,16,384]{3,2,1,0:T(8,128)(2,1)S(1)}, bf16[4,2,16,384]{3,2,1,0:T(8,128)(2,1)S(1)}, u32[]{:S(2)}, u32[]{:S(2)}) collective-permute-start(bf16[4,2,16,384]{3,2,1,0:T(8,128)(2,1)S(1)} %get-tuple-element.34), channel_id=1, source_target_pairs={{0,32},{8,40},{16,48},{24,56},{32,0},{40,8},{48,16},{56,24},{64,96... | collective-permute-start | bytes 294920 | tf_op jit(solution)/shard_map/ppermute | solution.py:42
  22.6 1.1 %collective-permute-start.6 = (bf16[4,2,16,384]{3,2,1,0:T(8,128)(2,1)S(1)}, bf16[4,2,16,384]{3,2,1,0:T(8,128)(2,1)S(1)}, u32[]{:S(2)}, u32[]{:S(2)}) collective-permute-start(bf16[4,2,16,384]{3,2,1,0:T(8,128)(2,1)S(1)} %get-tuple-element.35), channel_id=1, source_target_pairs={{0,48},{8,56},{16,0},{24,8},{32,16},{40,24},{48,32},{56,40},{64,11... | collective-permute-start | bytes 294920 | tf_op jit(solution)/shard_map/ppermute | solution.py:42
  23.7 3.9 %collective-permute-done.4.refs_1_ = bf16[4,2,16,384]{3,2,1,0:T(8,128)(2,1)S(1)} collective-permute-done((bf16[4,2,16,384]{3,2,1,0:T(8,128)(2,1)S(1)}, bf16[4,2,16,384]{3,2,1,0:T(8,128)(2,1)S(1)}, u32[]{:S(2)}, u32[]{:S(2)}) %collective-permute-start.4) | collective-permute-done | bytes 98336 | tf_op jit(solution)/shard_map/ppermute | solution.py:42
  27.6 3.0 %collective-permute-done.5.refs_2_ = bf16[4,2,16,384]{3,2,1,0:T(8,128)(2,1)S(1)} collective-permute-done((bf16[4,2,16,384]{3,2,1,0:T(8,128)(2,1)S(1)}, bf16[4,2,16,384]{3,2,1,0:T(8,128)(2,1)S(1)}, u32[]{:S(2)}, u32[]{:S(2)}) %collective-permute-start.5) | collective-permute-done | bytes 98336 | tf_op jit(solution)/shard_map/ppermute | solution.py:42
  30.7 2.5 %forward.1 = (bf16[4,4,16,384]{3,2,1,0:T(8,128)(2,1)S(1)}, bf16[4,4,16,384]{3,2,1,0:T(8,128)(2,1)S(1)}, bf16[32,16,128]{2,1,0:T(8,128)(2,1)S(1)}, f32[2,2,512,256]{3,2,1,0:T(8,128)S(1)}) custom-call(bf16[4,2,16,384]{3,2,1,0:T(8,128)(2,1)S(1)} %get-tuple-element.32.refs_0_, bf16[4,2,16,384]{3,2,1,0:T(8,128)(2,1)S(1)} %collective-permute-done.4.refs_1_, ...), custom_call_target="tpu_custom_call" | custom-call | tf_op jit(solution)/shard_map/forward/pallas_call | solution.py:340
  33.2 1.2 %collective-permute-start.7 = (bf16[4,4,16,384]{3,2,1,0:T(8,128)(2,1)S(1)}, bf16[4,4,16,384]{3,2,1,0:T(8,128)(2,1)S(1)}, u32[]{:S(2)}, u32[]{:S(2)}) collective-permute-start(bf16[4,4,16,384]{3,2,1,0:T(8,128)(2,1)S(1)} %get-tuple-element.37), channel_id=1, source_target_pairs={{0,8},{8,0},{16,24},{24,16},{32,40},{40,32},{48,56},{56,48},{64,72... | collective-permute-start | bytes 589832 | tf_op jit(solution)/shard_map/ppermute | solution.py:42
  34.4 1.3 %backward.1.after_ref = bf16[32,16,384]{2,1,0:T(8,128)(2,1)} custom-call(f32[2,2,512,256]{3,2,1,0:T(8,128)S(1)} %get-tuple-element.38.spec_ref, bf16[32,16,128]{2,1,0:T(8,128)(2,1)S(1)} %get-tuple-element.39.rest_ref, bf16[32,64]{1,0:T(8,128)(2,1)S(1)} %copy-done.7, bf16[2,2,256,256]{3,2,1,0:T(8,128)(2,1)S(1)} %copy-done, f32[32,256]{1,0:T(8,128)S(1)} %copy-done.6, ...), custom_call_target="tpu_custom_call" | custom-call | tf_op jit(solution)/shard_map/backward/pallas_call | solution.py:351
  36.0 2.1 %collective-permute-start.9 = (bf16[2,4,16,384]{3,2,1,0:T(8,128)(2,1)S(1)}, bf16[2,4,16,384]{3,2,1,0:T(8,128)(2,1)S(1)}, u32[]{:S(2)}, u32[]{:S(2)}) collective-permute-start(bf16[2,4,16,384]{3,2,1,0:T(8,128)(2,1)S(1)} %get-tuple-element.41), channel_id=1, source_target_pairs={{0,128},{8,136},{16,144},{24,152},{32,160},{40,168},{48,176},{56,1... | collective-permute-start | bytes 294920 | tf_op jit(solution)/shard_map/ppermute | solution.py:42
  38.1 1.4 %collective-permute-start.10 = (bf16[2,4,16,384]{3,2,1,0:T(8,128)(2,1)S(1)}, bf16[2,4,16,384]{3,2,1,0:T(8,128)(2,1)S(1)}, u32[]{:S(2)}, u32[]{:S(2)}) collective-permute-start(bf16[2,4,16,384]{3,2,1,0:T(8,128)(2,1)S(1)} %get-tuple-element.42), channel_id=1, source_target_pairs={{0,192},{8,200},{16,208},{24,216},{32,224},{40,232},{48,240},{56,2... | collective-permute-start | bytes 294920 | tf_op jit(solution)/shard_map/ppermute | solution.py:42
  39.4 5.7 %all-to-all-start.1 = ((bf16[32,16,384]{2,1,0:T(8,128)(2,1)}), bf16[32,16,384]{2,1,0:T(8,128)(2,1)S(1)}, u32[]{:S(2)}, u32[]{:S(2)}) async-start(bf16[32,16,384]{2,1,0:T(8,128)(2,1)} %backward.1.after_ref), calls=%async_computation.1 | async-start | bytes 786432 | tf_op jit(solution)/shard_map/all_to_all | solution.py:282
  45.2 0.3 collective-permute-done.10.refs_2_
  45.5 1.0 %collective-permute-start.11 = (bf16[4,2,16,384]{3,2,1,0:T(8,128)(2,1)S(1)}, bf16[4,2,16,384]{3,2,1,0:T(8,128)(2,1)S(1)}, u32[]{:S(2)}, u32[]{:S(2)}) collective-permute-start(bf16[4,2,16,384]{3,2,1,0:T(8,128)(2,1)S(1)} %get-tuple-element.44), channel_id=1, source_target_pairs={{0,16},{8,24},{16,32},{24,40},{32,48},{40,56},{48,0},{56,8},{64,80... | collective-permute-start | bytes 294920 | tf_op jit(solution)/shard_map/ppermute | solution.py:42
  46.5 2.4 %collective-permute-start.12 = (bf16[4,2,16,384]{3,2,1,0:T(8,128)(2,1)S(1)}, bf16[4,2,16,384]{3,2,1,0:T(8,128)(2,1)S(1)}, u32[]{:S(2)}, u32[]{:S(2)}) collective-permute-start(bf16[4,2,16,384]{3,2,1,0:T(8,128)(2,1)S(1)} %get-tuple-element.45), channel_id=1, source_target_pairs={{0,32},{8,40},{16,48},{24,56},{32,0},{40,8},{48,16},{56,24},{64,96... | collective-permute-start | bytes 294920 | tf_op jit(solution)/shard_map/ppermute | solution.py:42
  49.0 1.1 %collective-permute-start.13 = (bf16[4,2,16,384]{3,2,1,0:T(8,128)(2,1)S(1)}, bf16[4,2,16,384]{3,2,1,0:T(8,128)(2,1)S(1)}, u32[]{:S(2)}, u32[]{:S(2)}) collective-permute-start(bf16[4,2,16,384]{3,2,1,0:T(8,128)(2,1)S(1)} %get-tuple-element.46), channel_id=1, source_target_pairs={{0,48},{8,56},{16,0},{24,8},{32,16},{40,24},{48,32},{56,40},{64,11... | collective-permute-start | bytes 294920 | tf_op jit(solution)/shard_map/ppermute | solution.py:42
  50.1 3.7 %collective-permute-done.11.refs_1_ = bf16[4,2,16,384]{3,2,1,0:T(8,128)(2,1)S(1)} collective-permute-done((bf16[4,2,16,384]{3,2,1,0:T(8,128)(2,1)S(1)}, bf16[4,2,16,384]{3,2,1,0:T(8,128)(2,1)S(1)}, u32[]{:S(2)}, u32[]{:S(2)}) %collective-permute-start.11) | collective-permute-done | bytes 98336 | tf_op jit(solution)/shard_map/ppermute | solution.py:42
  53.8 3.3 %collective-permute-done.12.refs_2_ = bf16[4,2,16,384]{3,2,1,0:T(8,128)(2,1)S(1)} collective-permute-done((bf16[4,2,16,384]{3,2,1,0:T(8,128)(2,1)S(1)}, bf16[4,2,16,384]{3,2,1,0:T(8,128)(2,1)S(1)}, u32[]{:S(2)}, u32[]{:S(2)}) %collective-permute-start.12) | collective-permute-done | bytes 98336 | tf_op jit(solution)/shard_map/ppermute | solution.py:42
  57.1 1.3 %gate.1 = (bf16[256,512]{1,0:T(8,128)(2,1)}, bf16[256,512]{1,0:T(8,128)(2,1)}, bf16[256,512]{1,0:T(8,128)(2,1)}, bf16[256,512]{1,0:T(8,128)(2,1)}, bf16[256,512]{1,0:T(8,128)(2,1)}) custom-call(bf16[4,2,16,384]{3,2,1,0:T(8,128)(2,1)S(1)} %get-tuple-element.43.refs_0_, bf16[4,2,16,384]{3,2,1,0:T(8,128)(2,1)S(1)} %collective-permute-done.11.refs_1_, ...), custom_call_target="tpu_custom_call" | custom-call | tf_op jit(solution)/shard_map/gate/pallas_call | solution.py:365
  (37 shorter events, 0.6 us)
Async XLA Ops:
  1.9 5.3 %collective-permute-start = (bf16[4,4,16,384]{3,2,1,0:T(8,128)(2,1)S(1)}, bf16[4,4,16,384]{3,2,1,0:T(8,128)(2,1)S(1)}, u32[]{:S(2)}, u32[]{:S(2)}) collective-permute-start(bf16[4,4,16,384]{3,2,1,0:T(8,128)(2,1)S(1)} %get-tuple-element.27), channel_id=1, source_target_pairs={{0,8},{8,0},{16,24},{24,16},{32,40},{40,32},{48,56},{56,48},{64,72... | collective-permute-start | bytes 589832 | tf_op jit(solution)/shard_map/ppermute | solution.py:42
  7.2 11.5 %collective-permute-start.1 = (bf16[2,4,16,384]{3,2,1,0:T(8,128)(2,1)S(1)}, bf16[2,4,16,384]{3,2,1,0:T(8,128)(2,1)S(1)}, u32[]{:S(2)}, u32[]{:S(2)}) collective-permute-start(bf16[2,4,16,384]{3,2,1,0:T(8,128)(2,1)S(1)} %get-tuple-element.29), channel_id=1, source_target_pairs={{0,64},{8,72},{16,80},{24,88},{32,96},{40,104},{48,112},{56,120},{... | collective-permute-start | bytes 294920 | tf_op jit(solution)/shard_map/ppermute | solution.py:42
  7.3 11.5 %collective-permute-start.2 = (bf16[2,4,16,384]{3,2,1,0:T(8,128)(2,1)S(1)}, bf16[2,4,16,384]{3,2,1,0:T(8,128)(2,1)S(1)}, u32[]{:S(2)}, u32[]{:S(2)}) collective-permute-start(bf16[2,4,16,384]{3,2,1,0:T(8,128)(2,1)S(1)} %get-tuple-element.30), channel_id=1, source_target_pairs={{0,128},{8,136},{16,144},{24,152},{32,160},{40,168},{48,176},{56,1... | collective-permute-start | bytes 294920 | tf_op jit(solution)/shard_map/ppermute | solution.py:42
  10.2 8.6 %collective-permute-start.3 = (bf16[2,4,16,384]{3,2,1,0:T(8,128)(2,1)S(1)}, bf16[2,4,16,384]{3,2,1,0:T(8,128)(2,1)S(1)}, u32[]{:S(2)}, u32[]{:S(2)}) collective-permute-start(bf16[2,4,16,384]{3,2,1,0:T(8,128)(2,1)S(1)} %get-tuple-element.31), channel_id=1, source_target_pairs={{0,192},{8,200},{16,208},{24,216},{32,224},{40,232},{48,240},{56,2... | collective-permute-start | bytes 294920 | tf_op jit(solution)/shard_map/ppermute | solution.py:42
  10.9 19.8 %all-to-all-start = ((bf16[32,16,384]{2,1,0:T(8,128)(2,1)}), bf16[32,16,384]{2,1,0:T(8,128)(2,1)S(1)}, u32[]{:S(2)}, u32[]{:S(2)}) async-start(bf16[32,16,384]{2,1,0:T(8,128)(2,1)} %pack_late.1.after_ref), calls=%async_computation | async-start | bytes 786432 | tf_op jit(solution)/shard_map/all_to_all | solution.py:282
  18.7 11.9 %copy-start = (bf16[2,2,256,256]{3,2,1,0:T(8,128)(2,1)S(1)}, bf16[2,2,256,256]{3,2,1,0:T(8,128)(2,1)}, u32[]{:S(2)}) copy-start(bf16[2,2,256,256]{3,2,1,0:T(8,128)(2,1)} %constant.12.clone.refs_7_.second_ref) | copy-start | bytes 1572868
  18.7 11.9 %copy-start.5 = (f32[32,256]{1,0:T(8,128)S(1)}, f32[32,256]{1,0:T(8,128)}, u32[]{:S(2)}) copy-start(f32[32,256]{1,0:T(8,128)} %constant.14.clone.refs_9_.twi_ref) | copy-start | bytes 98308
  18.7 11.9 %copy-start.6 = (f32[32,256]{1,0:T(8,128)S(1)}, f32[32,256]{1,0:T(8,128)}, u32[]{:S(2)}) copy-start(f32[32,256]{1,0:T(8,128)} %constant.13.clone.refs_8_.twr_ref) | copy-start | bytes 98308
  18.8 11.9 %copy-start.7 = (bf16[32,64]{1,0:T(8,128)(2,1)S(1)}, bf16[32,64]{1,0:T(8,128)(2,1)}, u32[]{:S(2)}) copy-start(bf16[32,64]{1,0:T(8,128)(2,1)} %constant.11.clone.refs_6_.first_t_ref) | copy-start | bytes 12292
  18.9 8.8 %collective-permute-start.4 = (bf16[4,2,16,384]{3,2,1,0:T(8,128)(2,1)S(1)}, bf16[4,2,16,384]{3,2,1,0:T(8,128)(2,1)S(1)}, u32[]{:S(2)}, u32[]{:S(2)}) collective-permute-start(bf16[4,2,16,384]{3,2,1,0:T(8,128)(2,1)S(1)} %get-tuple-element.33), channel_id=1, source_target_pairs={{0,16},{8,24},{16,32},{24,40},{32,48},{40,56},{48,0},{56,8},{64,80... | collective-permute-start | bytes 294920 | tf_op jit(solution)/shard_map/ppermute | solution.py:42
  20.1 10.5 %collective-permute-start.5 = (bf16[4,2,16,384]{3,2,1,0:T(8,128)(2,1)S(1)}, bf16[4,2,16,384]{3,2,1,0:T(8,128)(2,1)S(1)}, u32[]{:S(2)}, u32[]{:S(2)}) collective-permute-start(bf16[4,2,16,384]{3,2,1,0:T(8,128)(2,1)S(1)} %get-tuple-element.34), channel_id=1, source_target_pairs={{0,32},{8,40},{16,48},{24,56},{32,0},{40,8},{48,16},{56,24},{64,96... | collective-permute-start | bytes 294920 | tf_op jit(solution)/shard_map/ppermute | solution.py:42
  22.6 8.1 %collective-permute-start.6 = (bf16[4,2,16,384]{3,2,1,0:T(8,128)(2,1)S(1)}, bf16[4,2,16,384]{3,2,1,0:T(8,128)(2,1)S(1)}, u32[]{:S(2)}, u32[]{:S(2)}) collective-permute-start(bf16[4,2,16,384]{3,2,1,0:T(8,128)(2,1)S(1)} %get-tuple-element.35), channel_id=1, source_target_pairs={{0,48},{8,56},{16,0},{24,8},{32,16},{40,24},{48,32},{56,40},{64,11... | collective-permute-start | bytes 294920 | tf_op jit(solution)/shard_map/ppermute | solution.py:42
  33.2 2.5 %collective-permute-start.7 = (bf16[4,4,16,384]{3,2,1,0:T(8,128)(2,1)S(1)}, bf16[4,4,16,384]{3,2,1,0:T(8,128)(2,1)S(1)}, u32[]{:S(2)}, u32[]{:S(2)}) collective-permute-start(bf16[4,4,16,384]{3,2,1,0:T(8,128)(2,1)S(1)} %get-tuple-element.37), channel_id=1, source_target_pairs={{0,8},{8,0},{16,24},{24,16},{32,40},{40,32},{48,56},{56,48},{64,72... | collective-permute-start | bytes 589832 | tf_op jit(solution)/shard_map/ppermute | solution.py:42
  35.8 9.5 %collective-permute-start.8 = (bf16[2,4,16,384]{3,2,1,0:T(8,128)(2,1)S(1)}, bf16[2,4,16,384]{3,2,1,0:T(8,128)(2,1)S(1)}, u32[]{:S(2)}, u32[]{:S(2)}) collective-permute-start(bf16[2,4,16,384]{3,2,1,0:T(8,128)(2,1)S(1)} %get-tuple-element.40), channel_id=1, source_target_pairs={{0,64},{8,72},{16,80},{24,88},{32,96},{40,104},{48,112},{56,120},{... | collective-permute-start | bytes 294920 | tf_op jit(solution)/shard_map/ppermute | solution.py:42
  36.0 9.2 %collective-permute-start.9 = (bf16[2,4,16,384]{3,2,1,0:T(8,128)(2,1)S(1)}, bf16[2,4,16,384]{3,2,1,0:T(8,128)(2,1)S(1)}, u32[]{:S(2)}, u32[]{:S(2)}) collective-permute-start(bf16[2,4,16,384]{3,2,1,0:T(8,128)(2,1)S(1)} %get-tuple-element.41), channel_id=1, source_target_pairs={{0,128},{8,136},{16,144},{24,152},{32,160},{40,168},{48,176},{56,1... | collective-permute-start | bytes 294920 | tf_op jit(solution)/shard_map/ppermute | solution.py:42
  38.1 7.4 %collective-permute-start.10 = (bf16[2,4,16,384]{3,2,1,0:T(8,128)(2,1)S(1)}, bf16[2,4,16,384]{3,2,1,0:T(8,128)(2,1)S(1)}, u32[]{:S(2)}, u32[]{:S(2)}) collective-permute-start(bf16[2,4,16,384]{3,2,1,0:T(8,128)(2,1)S(1)} %get-tuple-element.42), channel_id=1, source_target_pairs={{0,192},{8,200},{16,208},{24,216},{32,224},{40,232},{48,240},{56,2... | collective-permute-start | bytes 294920 | tf_op jit(solution)/shard_map/ppermute | solution.py:42
  39.4 17.7 %all-to-all-start.1 = ((bf16[32,16,384]{2,1,0:T(8,128)(2,1)}), bf16[32,16,384]{2,1,0:T(8,128)(2,1)S(1)}, u32[]{:S(2)}, u32[]{:S(2)}) async-start(bf16[32,16,384]{2,1,0:T(8,128)(2,1)} %backward.1.after_ref), calls=%async_computation.1 | async-start | bytes 786432 | tf_op jit(solution)/shard_map/all_to_all | solution.py:282
  45.1 11.9 %copy-start.1 = (bf16[256,512]{1,0:T(8,128)(2,1)S(1)}, bf16[256,512]{1,0:T(8,128)(2,1)}, u32[]{:S(2)}) copy-start(bf16[256,512]{1,0:T(8,128)(2,1)} %refs_6_.2) | copy-start | bytes 786436
  45.2 11.9 %copy-start.2 = (bf16[256,512]{1,0:T(8,128)(2,1)S(1)}, bf16[256,512]{1,0:T(8,128)(2,1)}, u32[]{:S(2)}) copy-start(bf16[256,512]{1,0:T(8,128)(2,1)} %refs_7_.2) | copy-start | bytes 786436
  45.2 11.9 %copy-start.3 = (bf16[256,512]{1,0:T(8,128)(2,1)S(1)}, bf16[256,512]{1,0:T(8,128)(2,1)}, u32[]{:S(2)}) copy-start(bf16[256,512]{1,0:T(8,128)(2,1)} %refs_5_.2) | copy-start | bytes 786436
  45.2 11.9 %copy-start.4 = (bf16[256,512]{1,0:T(8,128)(2,1)S(1)}, bf16[256,512]{1,0:T(8,128)(2,1)}, u32[]{:S(2)}) copy-start(bf16[256,512]{1,0:T(8,128)(2,1)} %refs_8_.2) | copy-start | bytes 786436
  45.5 8.3 %collective-permute-start.11 = (bf16[4,2,16,384]{3,2,1,0:T(8,128)(2,1)S(1)}, bf16[4,2,16,384]{3,2,1,0:T(8,128)(2,1)S(1)}, u32[]{:S(2)}, u32[]{:S(2)}) collective-permute-start(bf16[4,2,16,384]{3,2,1,0:T(8,128)(2,1)S(1)} %get-tuple-element.44), channel_id=1, source_target_pairs={{0,16},{8,24},{16,32},{24,40},{32,48},{40,56},{48,0},{56,8},{64,80... | collective-permute-start | bytes 294920 | tf_op jit(solution)/shard_map/ppermute | solution.py:42
  46.5 10.5 %collective-permute-start.12 = (bf16[4,2,16,384]{3,2,1,0:T(8,128)(2,1)S(1)}, bf16[4,2,16,384]{3,2,1,0:T(8,128)(2,1)S(1)}, u32[]{:S(2)}, u32[]{:S(2)}) collective-permute-start(bf16[4,2,16,384]{3,2,1,0:T(8,128)(2,1)S(1)} %get-tuple-element.45), channel_id=1, source_target_pairs={{0,32},{8,40},{16,48},{24,56},{32,0},{40,8},{48,16},{56,24},{64,96... | collective-permute-start | bytes 294920 | tf_op jit(solution)/shard_map/ppermute | solution.py:42
  49.0 8.1 %collective-permute-start.13 = (bf16[4,2,16,384]{3,2,1,0:T(8,128)(2,1)S(1)}, bf16[4,2,16,384]{3,2,1,0:T(8,128)(2,1)S(1)}, u32[]{:S(2)}, u32[]{:S(2)}) collective-permute-start(bf16[4,2,16,384]{3,2,1,0:T(8,128)(2,1)S(1)} %get-tuple-element.46), channel_id=1, source_target_pairs={{0,48},{8,56},{16,0},{24,8},{32,16},{40,24},{48,32},{56,40},{64,11... | collective-permute-start | bytes 294920 | tf_op jit(solution)/shard_map/ppermute | solution.py:42
  (2 other events, 23.9 us)

commit v8 on v7

--- a/solution.py
+++ b/solution.py
@@ -182,7 +182,7 @@
 def forward_kernel(scale, *refs):
     arrived = refs[:4]
     x_ref, first_ref, first_t_ref, second_ref, twr_ref, twi_ref = refs[4:10]
-    own_ref, other_ref, rest_ref, spec_ref, t_ref, v_ref, y_ref = refs[10:]
+    own_ref, other_ref, rest_ref, prod_ref, t_ref, v_ref, y_ref = refs[10:]
     rows = twr_ref.shape[1]
     h = rows // 2
     twr, twi = twr_ref[...], twi_ref[...]
@@ -193,8 +193,7 @@
         for s, block in enumerate((y_ref[:, :, :rows], gated, x_ref[:, :, :rows]))
     )
     for parity in (0, 1):
-        spec_ref[0, parity] = gated[parity]
-        spec_ref[1, parity] = delta[parity]
+        prod_ref[parity] = products(gated[parity], delta[parity], h, True)
     even, odd = (dot(products(gated[parity], taps[parity], h, False), second_ref[1, parity]) for parity in (0, 1))
     y_ref[:, :, :rows] = signal(scale, even, odd, first_t_ref, twr, twi, v_ref.at[0])
     even, odd = (dot(products(taps[parity], delta[parity], h, True), second_ref[1, parity]) for parity in (0, 1))
@@ -205,7 +204,7 @@
 
 
 def backward_kernel(
-    scale, spec_ref, rest_ref, first_t_ref, second_ref, twr_ref, twi_ref, y_hbm, v_ref, y_ref, sems
+    scale, prod_ref, rest_ref, first_t_ref, second_ref, twr_ref, twi_ref, y_hbm, v_ref, y_ref, sems
 ):
     groups, chans, rows = y_ref.shape
     h = rows // 2
@@ -215,7 +214,7 @@
         pltpu.make_async_copy(y_ref, y_hbm.at[:, :, pl.ds(0, rows)], sems.at[1]),
     ]
     copies[0].start()
-    even, odd = (dot(products(spec_ref[0, parity], spec_ref[1, parity], h, True), second_ref[1, parity]) for parity in (0, 1))
+    even, odd = (dot(prod_ref[parity], second_ref[1, parity]) for parity in (0, 1))
     y_ref[...] = signal(scale, even, odd, first_t_ref, twr, twi, v_ref)
     copies[1].start()
     for copy in copies:
@@ -337,11 +336,11 @@
     )(*keep(q_gate, out_grad), rest)
     early = travel(own, other, sent, WEIGHT1)
     items = swap(sent)
-    own, other, rest, spec = call(
+    own, other, rest, crossed = call(
         functools.partial(forward_kernel, scale),
         "forward",
         [shape(4, 4, *block)] * 2
-        + [shape(groups, *half), jax.ShapeDtypeStruct((2, 2, *bins), F32)],
+        + [shape(groups, *half), shape(2, *bins)],
         [
             pltpu.VMEM((3, 2, *bins), BF16),
             pltpu.VMEM((2, chans, 2 * groups, rows), BF16),
@@ -359,7 +358,7 @@
         ],
         in_specs=[near] * 6,
         out_specs=far,
-    )(spec, rest, first_t, second, twr, twi)
+    )(crossed, rest, first_t, second, twr, twi)
     arrived = travel(own, other, terms, WEIGHT)
     parts = 2
     return call(

time: 58.7 us -> 58.7 us (level)
  no operation moved by 1% of the time
where the time goes in v8:
time: 58.7 us; the launch traced here: 58.4 us
  starting transfers between devices  35 us (60%)
  waiting for transfers between devices  14.1 us (24%)
  Pallas kernels  8.41 us (14%)
  between operations  0.92 us (2%)
    ppermute x14, starting transfers between devices, send(): return lax.ppermute(block, 'context', moves)  21.3 us
    ppermute x14, waiting for transfers between devices, send(): return lax.ppermute(block, 'context', moves)  14.1 us
    all_to_all x2, starting transfers between devices, swap(): lax.all_to_all(block, 'context', split_axis=0, concat_axis=0, tiled=True,...  13.6 us
    pallas_call x1, Pallas kernels, local(): call(functools.partial(forward_kernel, scale), 'forward', [shape(4, 4, *b...  2.48 us
    pallas_call x1, Pallas kernels, local(): call(pack_late_kernel, 'pack_late', shape(groups, *block), [pltpu.VMEM((2...  1.93 us
    pallas_call x1, Pallas kernels, local(): call(functools.partial(backward_kernel, scale), 'backward', shape(groups,...  1.3 us
    pallas_call x1, Pallas kernels, local(): call(gate_kernel, 'gate', [whole] * 5, [pltpu.VMEM((groups, *block), BF16...  1.28 us
    pallas_call x1, Pallas kernels, local(): call(pack_early_kernel, 'pack_early', [pltpu.VMEM((4, 4, *block), BF16)]...  1.28 us
  transfers between devices with their start and end apart: 16, of which 5 were waited for; matrix products, arithmetic and copies ran while one was open for 0% of the time, Pallas kernels for 6%

profile of v8, /device:TPU:1, one launch (start us, length us, event | category | flops | bytes accessed | tf_op | source)
XLA Modules:
  0.0 58.4 jit_solution(11678761280671251265)
XLA Ops:
  0.6 1.3 %pack_early.1 = (bf16[4,4,16,384]{3,2,1,0:T(8,128)(2,1)S(1)}, bf16[4,4,16,384]{3,2,1,0:T(8,128)(2,1)S(1)}, bf16[32,16,128]{2,1,0:T(8,128)(2,1)S(1)}) custom-call(bf16[256,512]{1,0:T(8,128)(2,1)} %f_hbm.1, bf16[256,512]{1,0:T(8,128)(2,1)} %refs_6_.2, bf16[256,512]{1,0:T(8,128)(2,1)} %refs_7_.2), custom_call_target="tpu_custom_call" | custom-call | tf_op jit(solution)/shard_map/pack_early/pallas_call | solution.py:321
  1.9 3.3 %collective-permute-start = (bf16[4,4,16,384]{3,2,1,0:T(8,128)(2,1)S(1)}, bf16[4,4,16,384]{3,2,1,0:T(8,128)(2,1)S(1)}, u32[]{:S(2)}, u32[]{:S(2)}) collective-permute-start(bf16[4,4,16,384]{3,2,1,0:T(8,128)(2,1)S(1)} %get-tuple-element.27), channel_id=1, source_target_pairs={{0,8},{8,0},{16,24},{24,16},{32,40},{40,32},{48,56},{56,48},{64,72... | collective-permute-start | bytes 589832 | tf_op jit(solution)/shard_map/ppermute | solution.py:42
  5.2 1.9 %pack_late.1.after_ref = bf16[32,16,384]{2,1,0:T(8,128)(2,1)} custom-call(bf16[256,512]{1,0:T(8,128)(2,1)} %refs_5_.2, bf16[256,512]{1,0:T(8,128)(2,1)} %refs_8_.2, bf16[32,16,128]{2,1,0:T(8,128)(2,1)S(1)} %get-tuple-element.28.rest_ref), custom_call_target="tpu_custom_call" | custom-call | tf_op jit(solution)/shard_map/pack_late/pallas_call | solution.py:329
  7.3 2.9 %collective-permute-start.2 = (bf16[2,4,16,384]{3,2,1,0:T(8,128)(2,1)S(1)}, bf16[2,4,16,384]{3,2,1,0:T(8,128)(2,1)S(1)}, u32[]{:S(2)}, u32[]{:S(2)}) collective-permute-start(bf16[2,4,16,384]{3,2,1,0:T(8,128)(2,1)S(1)} %get-tuple-element.30), channel_id=1, source_target_pairs={{0,128},{8,136},{16,144},{24,152},{32,160},{40,168},{48,176},{56,1... | collective-permute-start | bytes 294920 | tf_op jit(solution)/shard_map/ppermute | solution.py:42
  10.2 0.7 %collective-permute-start.3 = (bf16[2,4,16,384]{3,2,1,0:T(8,128)(2,1)S(1)}, bf16[2,4,16,384]{3,2,1,0:T(8,128)(2,1)S(1)}, u32[]{:S(2)}, u32[]{:S(2)}) collective-permute-start(bf16[2,4,16,384]{3,2,1,0:T(8,128)(2,1)S(1)} %get-tuple-element.31), channel_id=1, source_target_pairs={{0,192},{8,200},{16,208},{24,216},{32,224},{40,232},{48,240},{56,2... | collective-permute-start | bytes 294920 | tf_op jit(solution)/shard_map/ppermute | solution.py:42
  10.9 7.8 %all-to-all-start = ((bf16[32,16,384]{2,1,0:T(8,128)(2,1)}), bf16[32,16,384]{2,1,0:T(8,128)(2,1)S(1)}, u32[]{:S(2)}, u32[]{:S(2)}) async-start(bf16[32,16,384]{2,1,0:T(8,128)(2,1)} %pack_late.1.after_ref), calls=%async_computation | async-start | bytes 786432 | tf_op jit(solution)/shard_map/all_to_all | solution.py:281
  18.9 1.3 %collective-permute-start.4 = (bf16[4,2,16,384]{3,2,1,0:T(8,128)(2,1)S(1)}, bf16[4,2,16,384]{3,2,1,0:T(8,128)(2,1)S(1)}, u32[]{:S(2)}, u32[]{:S(2)}) collective-permute-start(bf16[4,2,16,384]{3,2,1,0:T(8,128)(2,1)S(1)} %get-tuple-element.33), channel_id=1, source_target_pairs={{0,16},{8,24},{16,32},{24,40},{32,48},{40,56},{48,0},{56,8},{64,80... | collective-permute-start | bytes 294920 | tf_op jit(solution)/shard_map/ppermute | solution.py:42
  20.1 2.4 %collective-permute-start.5 = (bf16[4,2,16,384]{3,2,1,0:T(8,128)(2,1)S(1)}, bf16[4,2,16,384]{3,2,1,0:T(8,128)(2,1)S(1)}, u32[]{:S(2)}, u32[]{:S(2)}) collective-permute-start(bf16[4,2,16,384]{3,2,1,0:T(8,128)(2,1)S(1)} %get-tuple-element.34), channel_id=1, source_target_pairs={{0,32},{8,40},{16,48},{24,56},{32,0},{40,8},{48,16},{56,24},{64,96... | collective-permute-start | bytes 294920 | tf_op jit(solution)/shard_map/ppermute | solution.py:42
  22.6 1.1 %collective-permute-start.6 = (bf16[4,2,16,384]{3,2,1,0:T(8,128)(2,1)S(1)}, bf16[4,2,16,384]{3,2,1,0:T(8,128)(2,1)S(1)}, u32[]{:S(2)}, u32[]{:S(2)}) collective-permute-start(bf16[4,2,16,384]{3,2,1,0:T(8,128)(2,1)S(1)} %get-tuple-element.35), channel_id=1, source_target_pairs={{0,48},{8,56},{16,0},{24,8},{32,16},{40,24},{48,32},{56,40},{64,11... | collective-permute-start | bytes 294920 | tf_op jit(solution)/shard_map/ppermute | solution.py:42
  23.7 3.9 %collective-permute-done.4.refs_1_ = bf16[4,2,16,384]{3,2,1,0:T(8,128)(2,1)S(1)} collective-permute-done((bf16[4,2,16,384]{3,2,1,0:T(8,128)(2,1)S(1)}, bf16[4,2,16,384]{3,2,1,0:T(8,128)(2,1)S(1)}, u32[]{:S(2)}, u32[]{:S(2)}) %collective-permute-start.4) | collective-permute-done | bytes 98336 | tf_op jit(solution)/shard_map/ppermute | solution.py:42
  27.6 3.0 %collective-permute-done.5.refs_2_ = bf16[4,2,16,384]{3,2,1,0:T(8,128)(2,1)S(1)} collective-permute-done((bf16[4,2,16,384]{3,2,1,0:T(8,128)(2,1)S(1)}, bf16[4,2,16,384]{3,2,1,0:T(8,128)(2,1)S(1)}, u32[]{:S(2)}, u32[]{:S(2)}) %collective-permute-start.5) | collective-permute-done | bytes 98336 | tf_op jit(solution)/shard_map/ppermute | solution.py:42
  30.7 2.5 %forward.1 = (bf16[4,4,16,384]{3,2,1,0:T(8,128)(2,1)S(1)}, bf16[4,4,16,384]{3,2,1,0:T(8,128)(2,1)S(1)}, bf16[32,16,128]{2,1,0:T(8,128)(2,1)S(1)}, bf16[2,512,256]{2,1,0:T(8,128)(2,1)S(1)}) custom-call(bf16[4,2,16,384]{3,2,1,0:T(8,128)(2,1)S(1)} %get-tuple-element.32.refs_0_, bf16[4,2,16,384]{3,2,1,0:T(8,128)(2,1)S(1)} %collective-permute-done.4.refs_1_, ...), custom_call_target="tpu_custom_call" | custom-call | tf_op jit(solution)/shard_map/forward/pallas_call | solution.py:339
  33.2 1.2 %collective-permute-start.7 = (bf16[4,4,16,384]{3,2,1,0:T(8,128)(2,1)S(1)}, bf16[4,4,16,384]{3,2,1,0:T(8,128)(2,1)S(1)}, u32[]{:S(2)}, u32[]{:S(2)}) collective-permute-start(bf16[4,4,16,384]{3,2,1,0:T(8,128)(2,1)S(1)} %get-tuple-element.37), channel_id=1, source_target_pairs={{0,8},{8,0},{16,24},{24,16},{32,40},{40,32},{48,56},{56,48},{64,72... | collective-permute-start | bytes 589832 | tf_op jit(solution)/shard_map/ppermute | solution.py:42
  34.4 1.3 %backward.1.after_ref = bf16[32,16,384]{2,1,0:T(8,128)(2,1)} custom-call(bf16[2,512,256]{2,1,0:T(8,128)(2,1)S(1)} %get-tuple-element.38.prod_ref, bf16[32,16,128]{2,1,0:T(8,128)(2,1)S(1)} %get-tuple-element.39.rest_ref, bf16[32,64]{1,0:T(8,128)(2,1)S(1)} %copy-done.7, bf16[2,2,256,256]{3,2,1,0:T(8,128)(2,1)S(1)} %copy-done, f32[32,256]{1,0:T(8,128)S(1)} %copy-done.6, ...), custom_call_target="tpu_custom_call" | custom-call | tf_op jit(solution)/shard_map/backward/pallas_call | solution.py:350
  35.7 0.3 collective-permute-start.8
  36.0 2.0 %collective-permute-start.9 = (bf16[2,4,16,384]{3,2,1,0:T(8,128)(2,1)S(1)}, bf16[2,4,16,384]{3,2,1,0:T(8,128)(2,1)S(1)}, u32[]{:S(2)}, u32[]{:S(2)}) collective-permute-start(bf16[2,4,16,384]{3,2,1,0:T(8,128)(2,1)S(1)} %get-tuple-element.41), channel_id=1, source_target_pairs={{0,128},{8,136},{16,144},{24,152},{32,160},{40,168},{48,176},{56,1... | collective-permute-start | bytes 294920 | tf_op jit(solution)/shard_map/ppermute | solution.py:42
  38.0 1.4 %collective-permute-start.10 = (bf16[2,4,16,384]{3,2,1,0:T(8,128)(2,1)S(1)}, bf16[2,4,16,384]{3,2,1,0:T(8,128)(2,1)S(1)}, u32[]{:S(2)}, u32[]{:S(2)}) collective-permute-start(bf16[2,4,16,384]{3,2,1,0:T(8,128)(2,1)S(1)} %get-tuple-element.42), channel_id=1, source_target_pairs={{0,192},{8,200},{16,208},{24,216},{32,224},{40,232},{48,240},{56,2... | collective-permute-start | bytes 294920 | tf_op jit(solution)/shard_map/ppermute | solution.py:42
  39.4 5.8 %all-to-all-start.1 = ((bf16[32,16,384]{2,1,0:T(8,128)(2,1)}), bf16[32,16,384]{2,1,0:T(8,128)(2,1)S(1)}, u32[]{:S(2)}, u32[]{:S(2)}) async-start(bf16[32,16,384]{2,1,0:T(8,128)(2,1)} %backward.1.after_ref), calls=%async_computation.1 | async-start | bytes 786432 | tf_op jit(solution)/shard_map/all_to_all | solution.py:281
  45.4 1.1 %collective-permute-start.11 = (bf16[4,2,16,384]{3,2,1,0:T(8,128)(2,1)S(1)}, bf16[4,2,16,384]{3,2,1,0:T(8,128)(2,1)S(1)}, u32[]{:S(2)}, u32[]{:S(2)}) collective-permute-start(bf16[4,2,16,384]{3,2,1,0:T(8,128)(2,1)S(1)} %get-tuple-element.44), channel_id=1, source_target_pairs={{0,16},{8,24},{16,32},{24,40},{32,48},{40,56},{48,0},{56,8},{64,80... | collective-permute-start | bytes 294920 | tf_op jit(solution)/shard_map/ppermute | solution.py:42
  46.5 2.4 %collective-permute-start.12 = (bf16[4,2,16,384]{3,2,1,0:T(8,128)(2,1)S(1)}, bf16[4,2,16,384]{3,2,1,0:T(8,128)(2,1)S(1)}, u32[]{:S(2)}, u32[]{:S(2)}) collective-permute-start(bf16[4,2,16,384]{3,2,1,0:T(8,128)(2,1)S(1)} %get-tuple-element.45), channel_id=1, source_target_pairs={{0,32},{8,40},{16,48},{24,56},{32,0},{40,8},{48,16},{56,24},{64,96... | collective-permute-start | bytes 294920 | tf_op jit(solution)/shard_map/ppermute | solution.py:42
  49.0 1.1 %collective-permute-start.13 = (bf16[4,2,16,384]{3,2,1,0:T(8,128)(2,1)S(1)}, bf16[4,2,16,384]{3,2,1,0:T(8,128)(2,1)S(1)}, u32[]{:S(2)}, u32[]{:S(2)}) collective-permute-start(bf16[4,2,16,384]{3,2,1,0:T(8,128)(2,1)S(1)} %get-tuple-element.46), channel_id=1, source_target_pairs={{0,48},{8,56},{16,0},{24,8},{32,16},{40,24},{48,32},{56,40},{64,11... | collective-permute-start | bytes 294920 | tf_op jit(solution)/shard_map/ppermute | solution.py:42
  50.1 3.7 %collective-permute-done.11.refs_1_ = bf16[4,2,16,384]{3,2,1,0:T(8,128)(2,1)S(1)} collective-permute-done((bf16[4,2,16,384]{3,2,1,0:T(8,128)(2,1)S(1)}, bf16[4,2,16,384]{3,2,1,0:T(8,128)(2,1)S(1)}, u32[]{:S(2)}, u32[]{:S(2)}) %collective-permute-start.11) | collective-permute-done | bytes 98336 | tf_op jit(solution)/shard_map/ppermute | solution.py:42
  53.8 3.3 %collective-permute-done.12.refs_2_ = bf16[4,2,16,384]{3,2,1,0:T(8,128)(2,1)S(1)} collective-permute-done((bf16[4,2,16,384]{3,2,1,0:T(8,128)(2,1)S(1)}, bf16[4,2,16,384]{3,2,1,0:T(8,128)(2,1)S(1)}, u32[]{:S(2)}, u32[]{:S(2)}) %collective-permute-start.12) | collective-permute-done | bytes 98336 | tf_op jit(solution)/shard_map/ppermute | solution.py:42
  57.1 1.3 %gate.1 = (bf16[256,512]{1,0:T(8,128)(2,1)}, bf16[256,512]{1,0:T(8,128)(2,1)}, bf16[256,512]{1,0:T(8,128)(2,1)}, bf16[256,512]{1,0:T(8,128)(2,1)}, bf16[256,512]{1,0:T(8,128)(2,1)}) custom-call(bf16[4,2,16,384]{3,2,1,0:T(8,128)(2,1)S(1)} %get-tuple-element.43.refs_0_, bf16[4,2,16,384]{3,2,1,0:T(8,128)(2,1)S(1)} %collective-permute-done.11.refs_1_, ...), custom_call_target="tpu_custom_call" | custom-call | tf_op jit(solution)/shard_map/gate/pallas_call | solution.py:364
  (37 shorter events, 0.5 us)
Async XLA Ops:
  1.9 5.3 %collective-permute-start = (bf16[4,4,16,384]{3,2,1,0:T(8,128)(2,1)S(1)}, bf16[4,4,16,384]{3,2,1,0:T(8,128)(2,1)S(1)}, u32[]{:S(2)}, u32[]{:S(2)}) collective-permute-start(bf16[4,4,16,384]{3,2,1,0:T(8,128)(2,1)S(1)} %get-tuple-element.27), channel_id=1, source_target_pairs={{0,8},{8,0},{16,24},{24,16},{32,40},{40,32},{48,56},{56,48},{64,72... | collective-permute-start | bytes 589832 | tf_op jit(solution)/shard_map/ppermute | solution.py:42
  7.2 11.5 %collective-permute-start.1 = (bf16[2,4,16,384]{3,2,1,0:T(8,128)(2,1)S(1)}, bf16[2,4,16,384]{3,2,1,0:T(8,128)(2,1)S(1)}, u32[]{:S(2)}, u32[]{:S(2)}) collective-permute-start(bf16[2,4,16,384]{3,2,1,0:T(8,128)(2,1)S(1)} %get-tuple-element.29), channel_id=1, source_target_pairs={{0,64},{8,72},{16,80},{24,88},{32,96},{40,104},{48,112},{56,120},{... | collective-permute-start | bytes 294920 | tf_op jit(solution)/shard_map/ppermute | solution.py:42
  7.3 11.4 %collective-permute-start.2 = (bf16[2,4,16,384]{3,2,1,0:T(8,128)(2,1)S(1)}, bf16[2,4,16,384]{3,2,1,0:T(8,128)(2,1)S(1)}, u32[]{:S(2)}, u32[]{:S(2)}) collective-permute-start(bf16[2,4,16,384]{3,2,1,0:T(8,128)(2,1)S(1)} %get-tuple-element.30), channel_id=1, source_target_pairs={{0,128},{8,136},{16,144},{24,152},{32,160},{40,168},{48,176},{56,1... | collective-permute-start | bytes 294920 | tf_op jit(solution)/shard_map/ppermute | solution.py:42
  10.2 8.6 %collective-permute-start.3 = (bf16[2,4,16,384]{3,2,1,0:T(8,128)(2,1)S(1)}, bf16[2,4,16,384]{3,2,1,0:T(8,128)(2,1)S(1)}, u32[]{:S(2)}, u32[]{:S(2)}) collective-permute-start(bf16[2,4,16,384]{3,2,1,0:T(8,128)(2,1)S(1)} %get-tuple-element.31), channel_id=1, source_target_pairs={{0,192},{8,200},{16,208},{24,216},{32,224},{40,232},{48,240},{56,2... | collective-permute-start | bytes 294920 | tf_op jit(solution)/shard_map/ppermute | solution.py:42
  10.9 19.8 %all-to-all-start = ((bf16[32,16,384]{2,1,0:T(8,128)(2,1)}), bf16[32,16,384]{2,1,0:T(8,128)(2,1)S(1)}, u32[]{:S(2)}, u32[]{:S(2)}) async-start(bf16[32,16,384]{2,1,0:T(8,128)(2,1)} %pack_late.1.after_ref), calls=%async_computation | async-start | bytes 786432 | tf_op jit(solution)/shard_map/all_to_all | solution.py:281
  18.7 11.9 %copy-start = (bf16[2,2,256,256]{3,2,1,0:T(8,128)(2,1)S(1)}, bf16[2,2,256,256]{3,2,1,0:T(8,128)(2,1)}, u32[]{:S(2)}) copy-start(bf16[2,2,256,256]{3,2,1,0:T(8,128)(2,1)} %constant.12.clone.refs_7_.second_ref) | copy-start | bytes 1572868
  18.7 11.9 %copy-start.5 = (f32[32,256]{1,0:T(8,128)S(1)}, f32[32,256]{1,0:T(8,128)}, u32[]{:S(2)}) copy-start(f32[32,256]{1,0:T(8,128)} %constant.14.clone.refs_9_.twi_ref) | copy-start | bytes 98308
  18.7 11.9 %copy-start.6 = (f32[32,256]{1,0:T(8,128)S(1)}, f32[32,256]{1,0:T(8,128)}, u32[]{:S(2)}) copy-start(f32[32,256]{1,0:T(8,128)} %constant.13.clone.refs_8_.twr_ref) | copy-start | bytes 98308
  18.8 11.9 %copy-start.7 = (bf16[32,64]{1,0:T(8,128)(2,1)S(1)}, bf16[32,64]{1,0:T(8,128)(2,1)}, u32[]{:S(2)}) copy-start(bf16[32,64]{1,0:T(8,128)(2,1)} %constant.11.clone.refs_6_.first_t_ref) | copy-start | bytes 12292
  18.9 8.8 %collective-permute-start.4 = (bf16[4,2,16,384]{3,2,1,0:T(8,128)(2,1)S(1)}, bf16[4,2,16,384]{3,2,1,0:T(8,128)(2,1)S(1)}, u32[]{:S(2)}, u32[]{:S(2)}) collective-permute-start(bf16[4,2,16,384]{3,2,1,0:T(8,128)(2,1)S(1)} %get-tuple-element.33), channel_id=1, source_target_pairs={{0,16},{8,24},{16,32},{24,40},{32,48},{40,56},{48,0},{56,8},{64,80... | collective-permute-start | bytes 294920 | tf_op jit(solution)/shard_map/ppermute | solution.py:42
  20.1 10.5 %collective-permute-start.5 = (bf16[4,2,16,384]{3,2,1,0:T(8,128)(2,1)S(1)}, bf16[4,2,16,384]{3,2,1,0:T(8,128)(2,1)S(1)}, u32[]{:S(2)}, u32[]{:S(2)}) collective-permute-start(bf16[4,2,16,384]{3,2,1,0:T(8,128)(2,1)S(1)} %get-tuple-element.34), channel_id=1, source_target_pairs={{0,32},{8,40},{16,48},{24,56},{32,0},{40,8},{48,16},{56,24},{64,96... | collective-permute-start | bytes 294920 | tf_op jit(solution)/shard_map/ppermute | solution.py:42
  22.6 8.1 %collective-permute-start.6 = (bf16[4,2,16,384]{3,2,1,0:T(8,128)(2,1)S(1)}, bf16[4,2,16,384]{3,2,1,0:T(8,128)(2,1)S(1)}, u32[]{:S(2)}, u32[]{:S(2)}) collective-permute-start(bf16[4,2,16,384]{3,2,1,0:T(8,128)(2,1)S(1)} %get-tuple-element.35), channel_id=1, source_target_pairs={{0,48},{8,56},{16,0},{24,8},{32,16},{40,24},{48,32},{56,40},{64,11... | collective-permute-start | bytes 294920 | tf_op jit(solution)/shard_map/ppermute | solution.py:42
  33.2 2.5 %collective-permute-start.7 = (bf16[4,4,16,384]{3,2,1,0:T(8,128)(2,1)S(1)}, bf16[4,4,16,384]{3,2,1,0:T(8,128)(2,1)S(1)}, u32[]{:S(2)}, u32[]{:S(2)}) collective-permute-start(bf16[4,4,16,384]{3,2,1,0:T(8,128)(2,1)S(1)} %get-tuple-element.37), channel_id=1, source_target_pairs={{0,8},{8,0},{16,24},{24,16},{32,40},{40,32},{48,56},{56,48},{64,72... | collective-permute-start | bytes 589832 | tf_op jit(solution)/shard_map/ppermute | solution.py:42
  35.7 9.5 %collective-permute-start.8 = (bf16[2,4,16,384]{3,2,1,0:T(8,128)(2,1)S(1)}, bf16[2,4,16,384]{3,2,1,0:T(8,128)(2,1)S(1)}, u32[]{:S(2)}, u32[]{:S(2)}) collective-permute-start(bf16[2,4,16,384]{3,2,1,0:T(8,128)(2,1)S(1)} %get-tuple-element.40), channel_id=1, source_target_pairs={{0,64},{8,72},{16,80},{24,88},{32,96},{40,104},{48,112},{56,120},{... | collective-permute-start | bytes 294920 | tf_op jit(solution)/shard_map/ppermute | solution.py:42
  36.0 9.2 %collective-permute-start.9 = (bf16[2,4,16,384]{3,2,1,0:T(8,128)(2,1)S(1)}, bf16[2,4,16,384]{3,2,1,0:T(8,128)(2,1)S(1)}, u32[]{:S(2)}, u32[]{:S(2)}) collective-permute-start(bf16[2,4,16,384]{3,2,1,0:T(8,128)(2,1)S(1)} %get-tuple-element.41), channel_id=1, source_target_pairs={{0,128},{8,136},{16,144},{24,152},{32,160},{40,168},{48,176},{56,1... | collective-permute-start | bytes 294920 | tf_op jit(solution)/shard_map/ppermute | solution.py:42
  38.0 7.4 %collective-permute-start.10 = (bf16[2,4,16,384]{3,2,1,0:T(8,128)(2,1)S(1)}, bf16[2,4,16,384]{3,2,1,0:T(8,128)(2,1)S(1)}, u32[]{:S(2)}, u32[]{:S(2)}) collective-permute-start(bf16[2,4,16,384]{3,2,1,0:T(8,128)(2,1)S(1)} %get-tuple-element.42), channel_id=1, source_target_pairs={{0,192},{8,200},{16,208},{24,216},{32,224},{40,232},{48,240},{56,2... | collective-permute-start | bytes 294920 | tf_op jit(solution)/shard_map/ppermute | solution.py:42
  39.4 17.7 %all-to-all-start.1 = ((bf16[32,16,384]{2,1,0:T(8,128)(2,1)}), bf16[32,16,384]{2,1,0:T(8,128)(2,1)S(1)}, u32[]{:S(2)}, u32[]{:S(2)}) async-start(bf16[32,16,384]{2,1,0:T(8,128)(2,1)} %backward.1.after_ref), calls=%async_computation.1 | async-start | bytes 786432 | tf_op jit(solution)/shard_map/all_to_all | solution.py:281
  45.2 11.9 %copy-start.1 = (bf16[256,512]{1,0:T(8,128)(2,1)S(1)}, bf16[256,512]{1,0:T(8,128)(2,1)}, u32[]{:S(2)}) copy-start(bf16[256,512]{1,0:T(8,128)(2,1)} %refs_6_.2) | copy-start | bytes 786436
  45.2 11.9 %copy-start.2 = (bf16[256,512]{1,0:T(8,128)(2,1)S(1)}, bf16[256,512]{1,0:T(8,128)(2,1)}, u32[]{:S(2)}) copy-start(bf16[256,512]{1,0:T(8,128)(2,1)} %refs_7_.2) | copy-start | bytes 786436
  45.2 11.9 %copy-start.3 = (bf16[256,512]{1,0:T(8,128)(2,1)S(1)}, bf16[256,512]{1,0:T(8,128)(2,1)}, u32[]{:S(2)}) copy-start(bf16[256,512]{1,0:T(8,128)(2,1)} %refs_5_.2) | copy-start | bytes 786436
  45.2 11.9 %copy-start.4 = (bf16[256,512]{1,0:T(8,128)(2,1)S(1)}, bf16[256,512]{1,0:T(8,128)(2,1)}, u32[]{:S(2)}) copy-start(bf16[256,512]{1,0:T(8,128)(2,1)} %refs_8_.2) | copy-start | bytes 786436
  45.4 8.4 %collective-permute-start.11 = (bf16[4,2,16,384]{3,2,1,0:T(8,128)(2,1)S(1)}, bf16[4,2,16,384]{3,2,1,0:T(8,128)(2,1)S(1)}, u32[]{:S(2)}, u32[]{:S(2)}) collective-permute-start(bf16[4,2,16,384]{3,2,1,0:T(8,128)(2,1)S(1)} %get-tuple-element.44), channel_id=1, source_target_pairs={{0,16},{8,24},{16,32},{24,40},{32,48},{40,56},{48,0},{56,8},{64,80... | collective-permute-start | bytes 294920 | tf_op jit(solution)/shard_map/ppermute | solution.py:42
  46.5 10.5 %collective-permute-start.12 = (bf16[4,2,16,384]{3,2,1,0:T(8,128)(2,1)S(1)}, bf16[4,2,16,384]{3,2,1,0:T(8,128)(2,1)S(1)}, u32[]{:S(2)}, u32[]{:S(2)}) collective-permute-start(bf16[4,2,16,384]{3,2,1,0:T(8,128)(2,1)S(1)} %get-tuple-element.45), channel_id=1, source_target_pairs={{0,32},{8,40},{16,48},{24,56},{32,0},{40,8},{48,16},{56,24},{64,96... | collective-permute-start | bytes 294920 | tf_op jit(solution)/shard_map/ppermute | solution.py:42
  49.0 8.1 %collective-permute-start.13 = (bf16[4,2,16,384]{3,2,1,0:T(8,128)(2,1)S(1)}, bf16[4,2,16,384]{3,2,1,0:T(8,128)(2,1)S(1)}, u32[]{:S(2)}, u32[]{:S(2)}) collective-permute-start(bf16[4,2,16,384]{3,2,1,0:T(8,128)(2,1)S(1)} %get-tuple-element.46), channel_id=1, source_target_pairs={{0,48},{8,56},{16,0},{24,8},{32,16},{40,24},{48,32},{56,40},{64,11... | collective-permute-start | bytes 294920 | tf_op jit(solution)/shard_map/ppermute | solution.py:42
  (2 other events, 20.0 us)

commit v9 on v8

--- a/solution.py
+++ b/solution.py
@@ -171,11 +171,12 @@
     groups = twice // 2
     h = rows // 2
     even, odd = even.reshape(chans, groups, rows), odd.reshape(chans, groups, rows)
+    twr, twi = twr * scale, twi * scale
     for part, lanes in ((even + odd, slice(0, h)), (even - odd, slice(h, rows))):
         real, imag = part[:, :, :h], part[:, :, h:]
         v_ref[:, :groups, lanes] = (real * twr[:, lanes] + imag * twi[:, lanes]).astype(BF16)
         v_ref[:, groups:, lanes] = (imag * twr[:, lanes] - real * twi[:, lanes]).astype(BF16)
-    out = jnp.stack([dot(first_t_ref[...], v_ref[c]) * scale for c in range(chans)], axis=0)
+    out = jnp.stack([dot(first_t_ref[...], v_ref[c]) for c in range(chans)], axis=0)
     return jnp.swapaxes(out.astype(BF16), 0, 1)
 
 

time: 58.7 us -> 58.8 us (level)
  no operation moved by 1% of the time
where the time goes in v9:
time: 58.8 us; the launch traced here: 58.5 us
  starting transfers between devices  34.8 us (59%)
  waiting for transfers between devices  14.2 us (24%)
  Pallas kernels  8.49 us (14%)
  between operations  0.92 us (2%)
    ppermute x14, starting transfers between devices, send(): return lax.ppermute(block, 'context', moves)  21.2 us
    ppermute x14, waiting for transfers between devices, send(): return lax.ppermute(block, 'context', moves)  14.2 us
    all_to_all x2, starting transfers between devices, swap(): lax.all_to_all(block, 'context', split_axis=0, concat_axis=0, tiled=True,...  13.6 us
    pallas_call x1, Pallas kernels, local(): call(functools.partial(forward_kernel, scale), 'forward', [shape(4, 4, *b...  2.54 us
    pallas_call x1, Pallas kernels, local(): call(pack_late_kernel, 'pack_late', shape(groups, *block), [pltpu.VMEM((2...  1.93 us
    pallas_call x1, Pallas kernels, local(): call(functools.partial(backward_kernel, scale), 'backward', shape(groups,...  1.31 us
    pallas_call x1, Pallas kernels, local(): call(gate_kernel, 'gate', [whole] * 5, [pltpu.VMEM((groups, *block), BF16...  1.28 us
    pallas_call x1, Pallas kernels, local(): call(pack_early_kernel, 'pack_early', [pltpu.VMEM((4, 4, *block), BF16)]...  1.28 us
  transfers between devices with their start and end apart: 16, of which 5 were waited for; matrix products, arithmetic and copies ran while one was open for 0% of the time, Pallas kernels for 6%

profile of v9, /device:TPU:1, one launch (start us, length us, event | category | flops | bytes accessed | tf_op | source)
XLA Modules:
  0.0 58.5 jit_solution(13511436351166671694)
XLA Ops:
  0.6 1.3 %pack_early.1 = (bf16[4,4,16,384]{3,2,1,0:T(8,128)(2,1)S(1)}, bf16[4,4,16,384]{3,2,1,0:T(8,128)(2,1)S(1)}, bf16[32,16,128]{2,1,0:T(8,128)(2,1)S(1)}) custom-call(bf16[256,512]{1,0:T(8,128)(2,1)} %f_hbm.1, bf16[256,512]{1,0:T(8,128)(2,1)} %refs_6_.2, bf16[256,512]{1,0:T(8,128)(2,1)} %refs_7_.2), custom_call_target="tpu_custom_call" | custom-call | tf_op jit(solution)/shard_map/pack_early/pallas_call | solution.py:322
  1.9 3.3 %collective-permute-start = (bf16[4,4,16,384]{3,2,1,0:T(8,128)(2,1)S(1)}, bf16[4,4,16,384]{3,2,1,0:T(8,128)(2,1)S(1)}, u32[]{:S(2)}, u32[]{:S(2)}) collective-permute-start(bf16[4,4,16,384]{3,2,1,0:T(8,128)(2,1)S(1)} %get-tuple-element.27), channel_id=1, source_target_pairs={{0,8},{8,0},{16,24},{24,16},{32,40},{40,32},{48,56},{56,48},{64,72... | collective-permute-start | bytes 589832 | tf_op jit(solution)/shard_map/ppermute | solution.py:42
  5.2 1.9 %pack_late.1.after_ref = bf16[32,16,384]{2,1,0:T(8,128)(2,1)} custom-call(bf16[256,512]{1,0:T(8,128)(2,1)} %refs_5_.2, bf16[256,512]{1,0:T(8,128)(2,1)} %refs_8_.2, bf16[32,16,128]{2,1,0:T(8,128)(2,1)S(1)} %get-tuple-element.28.rest_ref), custom_call_target="tpu_custom_call" | custom-call | tf_op jit(solution)/shard_map/pack_late/pallas_call | solution.py:330
  7.3 2.9 %collective-permute-start.2 = (bf16[2,4,16,384]{3,2,1,0:T(8,128)(2,1)S(1)}, bf16[2,4,16,384]{3,2,1,0:T(8,128)(2,1)S(1)}, u32[]{:S(2)}, u32[]{:S(2)}) collective-permute-start(bf16[2,4,16,384]{3,2,1,0:T(8,128)(2,1)S(1)} %get-tuple-element.30), channel_id=1, source_target_pairs={{0,128},{8,136},{16,144},{24,152},{32,160},{40,168},{48,176},{56,1... | collective-permute-start | bytes 294920 | tf_op jit(solution)/shard_map/ppermute | solution.py:42
  10.2 0.7 %collective-permute-start.3 = (bf16[2,4,16,384]{3,2,1,0:T(8,128)(2,1)S(1)}, bf16[2,4,16,384]{3,2,1,0:T(8,128)(2,1)S(1)}, u32[]{:S(2)}, u32[]{:S(2)}) collective-permute-start(bf16[2,4,16,384]{3,2,1,0:T(8,128)(2,1)S(1)} %get-tuple-element.31), channel_id=1, source_target_pairs={{0,192},{8,200},{16,208},{24,216},{32,224},{40,232},{48,240},{56,2... | collective-permute-start | bytes 294920 | tf_op jit(solution)/shard_map/ppermute | solution.py:42
  10.9 7.8 %all-to-all-start = ((bf16[32,16,384]{2,1,0:T(8,128)(2,1)}), bf16[32,16,384]{2,1,0:T(8,128)(2,1)S(1)}, u32[]{:S(2)}, u32[]{:S(2)}) async-start(bf16[32,16,384]{2,1,0:T(8,128)(2,1)} %pack_late.1.after_ref), calls=%async_computation | async-start | bytes 786432 | tf_op jit(solution)/shard_map/all_to_all | solution.py:282
  18.9 1.3 %collective-permute-start.4 = (bf16[4,2,16,384]{3,2,1,0:T(8,128)(2,1)S(1)}, bf16[4,2,16,384]{3,2,1,0:T(8,128)(2,1)S(1)}, u32[]{:S(2)}, u32[]{:S(2)}) collective-permute-start(bf16[4,2,16,384]{3,2,1,0:T(8,128)(2,1)S(1)} %get-tuple-element.33), channel_id=1, source_target_pairs={{0,16},{8,24},{16,32},{24,40},{32,48},{40,56},{48,0},{56,8},{64,80... | collective-permute-start | bytes 294920 | tf_op jit(solution)/shard_map/ppermute | solution.py:42
  20.1 2.4 %collective-permute-start.5 = (bf16[4,2,16,384]{3,2,1,0:T(8,128)(2,1)S(1)}, bf16[4,2,16,384]{3,2,1,0:T(8,128)(2,1)S(1)}, u32[]{:S(2)}, u32[]{:S(2)}) collective-permute-start(bf16[4,2,16,384]{3,2,1,0:T(8,128)(2,1)S(1)} %get-tuple-element.34), channel_id=1, source_target_pairs={{0,32},{8,40},{16,48},{24,56},{32,0},{40,8},{48,16},{56,24},{64,96... | collective-permute-start | bytes 294920 | tf_op jit(solution)/shard_map/ppermute | solution.py:42
  22.6 1.1 %collective-permute-start.6 = (bf16[4,2,16,384]{3,2,1,0:T(8,128)(2,1)S(1)}, bf16[4,2,16,384]{3,2,1,0:T(8,128)(2,1)S(1)}, u32[]{:S(2)}, u32[]{:S(2)}) collective-permute-start(bf16[4,2,16,384]{3,2,1,0:T(8,128)(2,1)S(1)} %get-tuple-element.35), channel_id=1, source_target_pairs={{0,48},{8,56},{16,0},{24,8},{32,16},{40,24},{48,32},{56,40},{64,11... | collective-permute-start | bytes 294920 | tf_op jit(solution)/shard_map/ppermute | solution.py:42
  23.7 3.9 %collective-permute-done.4.refs_1_ = bf16[4,2,16,384]{3,2,1,0:T(8,128)(2,1)S(1)} collective-permute-done((bf16[4,2,16,384]{3,2,1,0:T(8,128)(2,1)S(1)}, bf16[4,2,16,384]{3,2,1,0:T(8,128)(2,1)S(1)}, u32[]{:S(2)}, u32[]{:S(2)}) %collective-permute-start.4) | collective-permute-done | bytes 98336 | tf_op jit(solution)/shard_map/ppermute | solution.py:42
  27.6 3.0 %collective-permute-done.5.refs_2_ = bf16[4,2,16,384]{3,2,1,0:T(8,128)(2,1)S(1)} collective-permute-done((bf16[4,2,16,384]{3,2,1,0:T(8,128)(2,1)S(1)}, bf16[4,2,16,384]{3,2,1,0:T(8,128)(2,1)S(1)}, u32[]{:S(2)}, u32[]{:S(2)}) %collective-permute-start.5) | collective-permute-done | bytes 98336 | tf_op jit(solution)/shard_map/ppermute | solution.py:42
  30.7 2.5 %forward.1 = (bf16[4,4,16,384]{3,2,1,0:T(8,128)(2,1)S(1)}, bf16[4,4,16,384]{3,2,1,0:T(8,128)(2,1)S(1)}, bf16[32,16,128]{2,1,0:T(8,128)(2,1)S(1)}, bf16[2,512,256]{2,1,0:T(8,128)(2,1)S(1)}) custom-call(bf16[4,2,16,384]{3,2,1,0:T(8,128)(2,1)S(1)} %get-tuple-element.32.refs_0_, bf16[4,2,16,384]{3,2,1,0:T(8,128)(2,1)S(1)} %collective-permute-done.4.refs_1_, ...), custom_call_target="tpu_custom_call" | custom-call | tf_op jit(solution)/shard_map/forward/pallas_call | solution.py:340
  33.3 1.2 %collective-permute-start.7 = (bf16[4,4,16,384]{3,2,1,0:T(8,128)(2,1)S(1)}, bf16[4,4,16,384]{3,2,1,0:T(8,128)(2,1)S(1)}, u32[]{:S(2)}, u32[]{:S(2)}) collective-permute-start(bf16[4,4,16,384]{3,2,1,0:T(8,128)(2,1)S(1)} %get-tuple-element.37), channel_id=1, source_target_pairs={{0,8},{8,0},{16,24},{24,16},{32,40},{40,32},{48,56},{56,48},{64,72... | collective-permute-start | bytes 589832 | tf_op jit(solution)/shard_map/ppermute | solution.py:42
  34.4 1.3 %backward.1.after_ref = bf16[32,16,384]{2,1,0:T(8,128)(2,1)} custom-call(bf16[2,512,256]{2,1,0:T(8,128)(2,1)S(1)} %get-tuple-element.38.prod_ref, bf16[32,16,128]{2,1,0:T(8,128)(2,1)S(1)} %get-tuple-element.39.rest_ref, bf16[32,64]{1,0:T(8,128)(2,1)S(1)} %copy-done.7, bf16[2,2,256,256]{3,2,1,0:T(8,128)(2,1)S(1)} %copy-done, f32[32,256]{1,0:T(8,128)S(1)} %copy-done.6, ...), custom_call_target="tpu_custom_call" | custom-call | tf_op jit(solution)/shard_map/backward/pallas_call | solution.py:351
  36.1 2.0 %collective-permute-start.9 = (bf16[2,4,16,384]{3,2,1,0:T(8,128)(2,1)S(1)}, bf16[2,4,16,384]{3,2,1,0:T(8,128)(2,1)S(1)}, u32[]{:S(2)}, u32[]{:S(2)}) collective-permute-start(bf16[2,4,16,384]{3,2,1,0:T(8,128)(2,1)S(1)} %get-tuple-element.41), channel_id=1, source_target_pairs={{0,128},{8,136},{16,144},{24,152},{32,160},{40,168},{48,176},{56,1... | collective-permute-start | bytes 294920 | tf_op jit(solution)/shard_map/ppermute | solution.py:42
  38.1 1.4 %collective-permute-start.10 = (bf16[2,4,16,384]{3,2,1,0:T(8,128)(2,1)S(1)}, bf16[2,4,16,384]{3,2,1,0:T(8,128)(2,1)S(1)}, u32[]{:S(2)}, u32[]{:S(2)}) collective-permute-start(bf16[2,4,16,384]{3,2,1,0:T(8,128)(2,1)S(1)} %get-tuple-element.42), channel_id=1, source_target_pairs={{0,192},{8,200},{16,208},{24,216},{32,224},{40,232},{48,240},{56,2... | collective-permute-start | bytes 294920 | tf_op jit(solution)/shard_map/ppermute | solution.py:42
  39.5 5.7 %all-to-all-start.1 = ((bf16[32,16,384]{2,1,0:T(8,128)(2,1)}), bf16[32,16,384]{2,1,0:T(8,128)(2,1)S(1)}, u32[]{:S(2)}, u32[]{:S(2)}) async-start(bf16[32,16,384]{2,1,0:T(8,128)(2,1)} %backward.1.after_ref), calls=%async_computation.1 | async-start | bytes 786432 | tf_op jit(solution)/shard_map/all_to_all | solution.py:282
  45.3 0.3 collective-permute-done.10.refs_2_
  45.6 1.0 %collective-permute-start.11 = (bf16[4,2,16,384]{3,2,1,0:T(8,128)(2,1)S(1)}, bf16[4,2,16,384]{3,2,1,0:T(8,128)(2,1)S(1)}, u32[]{:S(2)}, u32[]{:S(2)}) collective-permute-start(bf16[4,2,16,384]{3,2,1,0:T(8,128)(2,1)S(1)} %get-tuple-element.44), channel_id=1, source_target_pairs={{0,16},{8,24},{16,32},{24,40},{32,48},{40,56},{48,0},{56,8},{64,80... | collective-permute-start | bytes 294920 | tf_op jit(solution)/shard_map/ppermute | solution.py:42
  46.6 2.4 %collective-permute-start.12 = (bf16[4,2,16,384]{3,2,1,0:T(8,128)(2,1)S(1)}, bf16[4,2,16,384]{3,2,1,0:T(8,128)(2,1)S(1)}, u32[]{:S(2)}, u32[]{:S(2)}) collective-permute-start(bf16[4,2,16,384]{3,2,1,0:T(8,128)(2,1)S(1)} %get-tuple-element.45), channel_id=1, source_target_pairs={{0,32},{8,40},{16,48},{24,56},{32,0},{40,8},{48,16},{56,24},{64,96... | collective-permute-start | bytes 294920 | tf_op jit(solution)/shard_map/ppermute | solution.py:42
  49.0 1.1 %collective-permute-start.13 = (bf16[4,2,16,384]{3,2,1,0:T(8,128)(2,1)S(1)}, bf16[4,2,16,384]{3,2,1,0:T(8,128)(2,1)S(1)}, u32[]{:S(2)}, u32[]{:S(2)}) collective-permute-start(bf16[4,2,16,384]{3,2,1,0:T(8,128)(2,1)S(1)} %get-tuple-element.46), channel_id=1, source_target_pairs={{0,48},{8,56},{16,0},{24,8},{32,16},{40,24},{48,32},{56,40},{64,11... | collective-permute-start | bytes 294920 | tf_op jit(solution)/shard_map/ppermute | solution.py:42
  50.2 3.7 %collective-permute-done.11.refs_1_ = bf16[4,2,16,384]{3,2,1,0:T(8,128)(2,1)S(1)} collective-permute-done((bf16[4,2,16,384]{3,2,1,0:T(8,128)(2,1)S(1)}, bf16[4,2,16,384]{3,2,1,0:T(8,128)(2,1)S(1)}, u32[]{:S(2)}, u32[]{:S(2)}) %collective-permute-start.11) | collective-permute-done | bytes 98336 | tf_op jit(solution)/shard_map/ppermute | solution.py:42
  53.9 3.3 %collective-permute-done.12.refs_2_ = bf16[4,2,16,384]{3,2,1,0:T(8,128)(2,1)S(1)} collective-permute-done((bf16[4,2,16,384]{3,2,1,0:T(8,128)(2,1)S(1)}, bf16[4,2,16,384]{3,2,1,0:T(8,128)(2,1)S(1)}, u32[]{:S(2)}, u32[]{:S(2)}) %collective-permute-start.12) | collective-permute-done | bytes 98336 | tf_op jit(solution)/shard_map/ppermute | solution.py:42
  57.2 1.3 %gate.1 = (bf16[256,512]{1,0:T(8,128)(2,1)}, bf16[256,512]{1,0:T(8,128)(2,1)}, bf16[256,512]{1,0:T(8,128)(2,1)}, bf16[256,512]{1,0:T(8,128)(2,1)}, bf16[256,512]{1,0:T(8,128)(2,1)}) custom-call(bf16[4,2,16,384]{3,2,1,0:T(8,128)(2,1)S(1)} %get-tuple-element.43.refs_0_, bf16[4,2,16,384]{3,2,1,0:T(8,128)(2,1)S(1)} %collective-permute-done.11.refs_1_, ...), custom_call_target="tpu_custom_call" | custom-call | tf_op jit(solution)/shard_map/gate/pallas_call | solution.py:365
  (37 shorter events, 0.6 us)
Async XLA Ops:
  1.9 5.3 %collective-permute-start = (bf16[4,4,16,384]{3,2,1,0:T(8,128)(2,1)S(1)}, bf16[4,4,16,384]{3,2,1,0:T(8,128)(2,1)S(1)}, u32[]{:S(2)}, u32[]{:S(2)}) collective-permute-start(bf16[4,4,16,384]{3,2,1,0:T(8,128)(2,1)S(1)} %get-tuple-element.27), channel_id=1, source_target_pairs={{0,8},{8,0},{16,24},{24,16},{32,40},{40,32},{48,56},{56,48},{64,72... | collective-permute-start | bytes 589832 | tf_op jit(solution)/shard_map/ppermute | solution.py:42
  7.2 11.5 %collective-permute-start.1 = (bf16[2,4,16,384]{3,2,1,0:T(8,128)(2,1)S(1)}, bf16[2,4,16,384]{3,2,1,0:T(8,128)(2,1)S(1)}, u32[]{:S(2)}, u32[]{:S(2)}) collective-permute-start(bf16[2,4,16,384]{3,2,1,0:T(8,128)(2,1)S(1)} %get-tuple-element.29), channel_id=1, source_target_pairs={{0,64},{8,72},{16,80},{24,88},{32,96},{40,104},{48,112},{56,120},{... | collective-permute-start | bytes 294920 | tf_op jit(solution)/shard_map/ppermute | solution.py:42
  7.3 11.4 %collective-permute-start.2 = (bf16[2,4,16,384]{3,2,1,0:T(8,128)(2,1)S(1)}, bf16[2,4,16,384]{3,2,1,0:T(8,128)(2,1)S(1)}, u32[]{:S(2)}, u32[]{:S(2)}) collective-permute-start(bf16[2,4,16,384]{3,2,1,0:T(8,128)(2,1)S(1)} %get-tuple-element.30), channel_id=1, source_target_pairs={{0,128},{8,136},{16,144},{24,152},{32,160},{40,168},{48,176},{56,1... | collective-permute-start | bytes 294920 | tf_op jit(solution)/shard_map/ppermute | solution.py:42
  10.2 8.6 %collective-permute-start.3 = (bf16[2,4,16,384]{3,2,1,0:T(8,128)(2,1)S(1)}, bf16[2,4,16,384]{3,2,1,0:T(8,128)(2,1)S(1)}, u32[]{:S(2)}, u32[]{:S(2)}) collective-permute-start(bf16[2,4,16,384]{3,2,1,0:T(8,128)(2,1)S(1)} %get-tuple-element.31), channel_id=1, source_target_pairs={{0,192},{8,200},{16,208},{24,216},{32,224},{40,232},{48,240},{56,2... | collective-permute-start | bytes 294920 | tf_op jit(solution)/shard_map/ppermute | solution.py:42
  10.9 19.8 %all-to-all-start = ((bf16[32,16,384]{2,1,0:T(8,128)(2,1)}), bf16[32,16,384]{2,1,0:T(8,128)(2,1)S(1)}, u32[]{:S(2)}, u32[]{:S(2)}) async-start(bf16[32,16,384]{2,1,0:T(8,128)(2,1)} %pack_late.1.after_ref), calls=%async_computation | async-start | bytes 786432 | tf_op jit(solution)/shard_map/all_to_all | solution.py:282
  18.7 11.9 %copy-start = (bf16[2,2,256,256]{3,2,1,0:T(8,128)(2,1)S(1)}, bf16[2,2,256,256]{3,2,1,0:T(8,128)(2,1)}, u32[]{:S(2)}) copy-start(bf16[2,2,256,256]{3,2,1,0:T(8,128)(2,1)} %constant.12.clone.refs_7_.second_ref) | copy-start | bytes 1572868
  18.7 11.9 %copy-start.5 = (f32[32,256]{1,0:T(8,128)S(1)}, f32[32,256]{1,0:T(8,128)}, u32[]{:S(2)}) copy-start(f32[32,256]{1,0:T(8,128)} %constant.14.clone.refs_9_.twi_ref) | copy-start | bytes 98308
  18.7 11.9 %copy-start.6 = (f32[32,256]{1,0:T(8,128)S(1)}, f32[32,256]{1,0:T(8,128)}, u32[]{:S(2)}) copy-start(f32[32,256]{1,0:T(8,128)} %constant.13.clone.refs_8_.twr_ref) | copy-start | bytes 98308
  18.8 11.9 %copy-start.7 = (bf16[32,64]{1,0:T(8,128)(2,1)S(1)}, bf16[32,64]{1,0:T(8,128)(2,1)}, u32[]{:S(2)}) copy-start(bf16[32,64]{1,0:T(8,128)(2,1)} %constant.11.clone.refs_6_.first_t_ref) | copy-start | bytes 12292
  18.9 8.8 %collective-permute-start.4 = (bf16[4,2,16,384]{3,2,1,0:T(8,128)(2,1)S(1)}, bf16[4,2,16,384]{3,2,1,0:T(8,128)(2,1)S(1)}, u32[]{:S(2)}, u32[]{:S(2)}) collective-permute-start(bf16[4,2,16,384]{3,2,1,0:T(8,128)(2,1)S(1)} %get-tuple-element.33), channel_id=1, source_target_pairs={{0,16},{8,24},{16,32},{24,40},{32,48},{40,56},{48,0},{56,8},{64,80... | collective-permute-start | bytes 294920 | tf_op jit(solution)/shard_map/ppermute | solution.py:42
  20.1 10.5 %collective-permute-start.5 = (bf16[4,2,16,384]{3,2,1,0:T(8,128)(2,1)S(1)}, bf16[4,2,16,384]{3,2,1,0:T(8,128)(2,1)S(1)}, u32[]{:S(2)}, u32[]{:S(2)}) collective-permute-start(bf16[4,2,16,384]{3,2,1,0:T(8,128)(2,1)S(1)} %get-tuple-element.34), channel_id=1, source_target_pairs={{0,32},{8,40},{16,48},{24,56},{32,0},{40,8},{48,16},{56,24},{64,96... | collective-permute-start | bytes 294920 | tf_op jit(solution)/shard_map/ppermute | solution.py:42
  22.6 8.1 %collective-permute-start.6 = (bf16[4,2,16,384]{3,2,1,0:T(8,128)(2,1)S(1)}, bf16[4,2,16,384]{3,2,1,0:T(8,128)(2,1)S(1)}, u32[]{:S(2)}, u32[]{:S(2)}) collective-permute-start(bf16[4,2,16,384]{3,2,1,0:T(8,128)(2,1)S(1)} %get-tuple-element.35), channel_id=1, source_target_pairs={{0,48},{8,56},{16,0},{24,8},{32,16},{40,24},{48,32},{56,40},{64,11... | collective-permute-start | bytes 294920 | tf_op jit(solution)/shard_map/ppermute | solution.py:42
  33.3 2.5 %collective-permute-start.7 = (bf16[4,4,16,384]{3,2,1,0:T(8,128)(2,1)S(1)}, bf16[4,4,16,384]{3,2,1,0:T(8,128)(2,1)S(1)}, u32[]{:S(2)}, u32[]{:S(2)}) collective-permute-start(bf16[4,4,16,384]{3,2,1,0:T(8,128)(2,1)S(1)} %get-tuple-element.37), channel_id=1, source_target_pairs={{0,8},{8,0},{16,24},{24,16},{32,40},{40,32},{48,56},{56,48},{64,72... | collective-permute-start | bytes 589832 | tf_op jit(solution)/shard_map/ppermute | solution.py:42
  35.8 9.5 %collective-permute-start.8 = (bf16[2,4,16,384]{3,2,1,0:T(8,128)(2,1)S(1)}, bf16[2,4,16,384]{3,2,1,0:T(8,128)(2,1)S(1)}, u32[]{:S(2)}, u32[]{:S(2)}) collective-permute-start(bf16[2,4,16,384]{3,2,1,0:T(8,128)(2,1)S(1)} %get-tuple-element.40), channel_id=1, source_target_pairs={{0,64},{8,72},{16,80},{24,88},{32,96},{40,104},{48,112},{56,120},{... | collective-permute-start | bytes 294920 | tf_op jit(solution)/shard_map/ppermute | solution.py:42
  36.1 9.2 %collective-permute-start.9 = (bf16[2,4,16,384]{3,2,1,0:T(8,128)(2,1)S(1)}, bf16[2,4,16,384]{3,2,1,0:T(8,128)(2,1)S(1)}, u32[]{:S(2)}, u32[]{:S(2)}) collective-permute-start(bf16[2,4,16,384]{3,2,1,0:T(8,128)(2,1)S(1)} %get-tuple-element.41), channel_id=1, source_target_pairs={{0,128},{8,136},{16,144},{24,152},{32,160},{40,168},{48,176},{56,1... | collective-permute-start | bytes 294920 | tf_op jit(solution)/shard_map/ppermute | solution.py:42
  38.1 7.4 %collective-permute-start.10 = (bf16[2,4,16,384]{3,2,1,0:T(8,128)(2,1)S(1)}, bf16[2,4,16,384]{3,2,1,0:T(8,128)(2,1)S(1)}, u32[]{:S(2)}, u32[]{:S(2)}) collective-permute-start(bf16[2,4,16,384]{3,2,1,0:T(8,128)(2,1)S(1)} %get-tuple-element.42), channel_id=1, source_target_pairs={{0,192},{8,200},{16,208},{24,216},{32,224},{40,232},{48,240},{56,2... | collective-permute-start | bytes 294920 | tf_op jit(solution)/shard_map/ppermute | solution.py:42
  39.5 17.7 %all-to-all-start.1 = ((bf16[32,16,384]{2,1,0:T(8,128)(2,1)}), bf16[32,16,384]{2,1,0:T(8,128)(2,1)S(1)}, u32[]{:S(2)}, u32[]{:S(2)}) async-start(bf16[32,16,384]{2,1,0:T(8,128)(2,1)} %backward.1.after_ref), calls=%async_computation.1 | async-start | bytes 786432 | tf_op jit(solution)/shard_map/all_to_all | solution.py:282
  45.2 11.9 %copy-start.1 = (bf16[256,512]{1,0:T(8,128)(2,1)S(1)}, bf16[256,512]{1,0:T(8,128)(2,1)}, u32[]{:S(2)}) copy-start(bf16[256,512]{1,0:T(8,128)(2,1)} %refs_6_.2) | copy-start | bytes 786436
  45.2 11.9 %copy-start.2 = (bf16[256,512]{1,0:T(8,128)(2,1)S(1)}, bf16[256,512]{1,0:T(8,128)(2,1)}, u32[]{:S(2)}) copy-start(bf16[256,512]{1,0:T(8,128)(2,1)} %refs_7_.2) | copy-start | bytes 786436
  45.2 11.9 %copy-start.3 = (bf16[256,512]{1,0:T(8,128)(2,1)S(1)}, bf16[256,512]{1,0:T(8,128)(2,1)}, u32[]{:S(2)}) copy-start(bf16[256,512]{1,0:T(8,128)(2,1)} %refs_5_.2) | copy-start | bytes 786436
  45.2 11.9 %copy-start.4 = (bf16[256,512]{1,0:T(8,128)(2,1)S(1)}, bf16[256,512]{1,0:T(8,128)(2,1)}, u32[]{:S(2)}) copy-start(bf16[256,512]{1,0:T(8,128)(2,1)} %refs_8_.2) | copy-start | bytes 786436
  45.6 8.3 %collective-permute-start.11 = (bf16[4,2,16,384]{3,2,1,0:T(8,128)(2,1)S(1)}, bf16[4,2,16,384]{3,2,1,0:T(8,128)(2,1)S(1)}, u32[]{:S(2)}, u32[]{:S(2)}) collective-permute-start(bf16[4,2,16,384]{3,2,1,0:T(8,128)(2,1)S(1)} %get-tuple-element.44), channel_id=1, source_target_pairs={{0,16},{8,24},{16,32},{24,40},{32,48},{40,56},{48,0},{56,8},{64,80... | collective-permute-start | bytes 294920 | tf_op jit(solution)/shard_map/ppermute | solution.py:42
  46.6 10.5 %collective-permute-start.12 = (bf16[4,2,16,384]{3,2,1,0:T(8,128)(2,1)S(1)}, bf16[4,2,16,384]{3,2,1,0:T(8,128)(2,1)S(1)}, u32[]{:S(2)}, u32[]{:S(2)}) collective-permute-start(bf16[4,2,16,384]{3,2,1,0:T(8,128)(2,1)S(1)} %get-tuple-element.45), channel_id=1, source_target_pairs={{0,32},{8,40},{16,48},{24,56},{32,0},{40,8},{48,16},{56,24},{64,96... | collective-permute-start | bytes 294920 | tf_op jit(solution)/shard_map/ppermute | solution.py:42
  49.0 8.1 %collective-permute-start.13 = (bf16[4,2,16,384]{3,2,1,0:T(8,128)(2,1)S(1)}, bf16[4,2,16,384]{3,2,1,0:T(8,128)(2,1)S(1)}, u32[]{:S(2)}, u32[]{:S(2)}) collective-permute-start(bf16[4,2,16,384]{3,2,1,0:T(8,128)(2,1)S(1)} %get-tuple-element.46), channel_id=1, source_target_pairs={{0,48},{8,56},{16,0},{24,8},{32,16},{40,24},{48,32},{56,40},{64,11... | collective-permute-start | bytes 294920 | tf_op jit(solution)/shard_map/ppermute | solution.py:42
  (2 other events, 20.0 us)
